TPU v7x, 32 devices: a whole 2x2x4 slice. The times are simulated.
32 devices in a mesh: seq: 8 (over y, x, core), head: 4 (over z).
Axes of the slice: x: 2, y: 2, z: 4, core: 2. Of those that a mesh axis runs over, the one named last changes fastest.
Arguments:
- tokens: bfloat16 [4096, 1152], P(('seq', 'head')), may hold values from -6 to 6
- segment_ids: int32 [4096], replicated, may hold values from 0 to 5, as said below
- w_query: bfloat16 [1152, 1024], replicated, may hold values from -0.1875 to 0.1875
- w_key: bfloat16 [1152, 256], replicated, may hold values from -0.1875 to 0.1875
- w_value: bfloat16 [1152, 256], replicated, may hold values from -0.1875 to 0.1875
- w_out: bfloat16 [1024, 1152], replicated, may hold values from -0.1875 to 0.1875
- w_gate: bfloat16 [1152, 6912], P(None, 'head'), may hold values from -0.1875 to 0.1875
- w_up: bfloat16 [1152, 6912], P(None, 'head'), may hold values from -0.1875 to 0.1875
- w_down: bfloat16 [6912, 1152], P('head'), may hold values from -0.078125 to 0.078125
- gain_attn_in: float32 [1152], replicated, may hold values from 0.25 to 1.75
- gain_attn_out: float32 [1152], replicated, may hold values from 0.25 to 1.75
- gain_ffn_in: float32 [1152], replicated, may hold values from 0.25 to 1.75
- gain_ffn_out: float32 [1152], replicated, may hold values from 0.25 to 1.75
- gain_query: float32 [256], replicated, may hold values from 0.25 to 1.75
- gain_key: float32 [256], replicated, may hold values from 0.25 to 1.75
- cotangent: bfloat16 [4096, 1152], P(('seq', 'head'))
Outputs:
- output: bfloat16 [4096, 1152], P(('seq', 'head'))
- grad_tokens: bfloat16 [4096, 1152], P(('seq', 'head'))
- grad_w_query: float32 [1152, 1024], P(('seq', 'head'))
- grad_w_key: float32 [1152, 256], P(('seq', 'head'))
- grad_w_value: float32 [1152, 256], P(('seq', 'head'))
- grad_w_out: float32 [1024, 1152], P(('seq', 'head'))
- grad_w_gate: float32 [1152, 6912], P('seq', 'head')
- grad_w_up: float32 [1152, 6912], P('seq', 'head')
- grad_w_down: float32 [6912, 1152], P('head', 'seq')
- grad_gain_attn_in: float32 [1152], P(('seq', 'head'))
- grad_gain_attn_out: float32 [1152], P(('seq', 'head'))
- grad_gain_ffn_in: float32 [1152], P(('seq', 'head'))
- grad_gain_ffn_out: float32 [1152], P(('seq', 'head'))
- grad_gain_query: float32 [256], P(('seq', 'head'))
- grad_gain_key: float32 [256], P(('seq', 'head'))
Inputs may be any that keep to these rules, and one draw needn't show every extreme that they name: `segment_ids`: nonzero ids never decrease and each forms one run; id 0 marks padding, one run at the end of the row; id 2 runs from within the first 512 tokens into the last 512.
All inputs are finite; a program needn't handle non-finite values.
Results may differ from a plain program's by a relative error of at most 0.024.
Values may be sent and summed in bfloat16 or wider, within the bound.
A program may use at most 192 MiB of HBM per device.

v0:
```python
import math

import jax
import jax.numpy as jnp
from jax import lax
from jax.sharding import PartitionSpec as P

EPS = 1e-06
NEG = -1e30


def norm_rows(v, gain):
    return v * lax.rsqrt(jnp.mean(v * v, axis=-1, keepdims=True) + EPS) * gain


def rotate(v, cosines, sines):
    half = v.shape[-1] // 2
    first = v[..., :half]
    second = v[..., half:]
    return jnp.concatenate(
        [first * cosines - second * sines, second * cosines + first * sines], axis=-1
    )


def rope_tables(positions, width):
    half = width // 2
    freq = jnp.exp(jnp.arange(half, dtype=jnp.float32) * (-2.0 * math.log(1000000.0) / width))
    angle = positions.astype(jnp.float32)[:, None] * freq[None, :]
    return (jnp.cos(angle), jnp.sin(angle))


def row_positions(segment_ids):
    total = segment_ids.shape[0]
    index = jnp.arange(total, dtype=jnp.int32)
    change = jnp.concatenate([jnp.ones((1,), dtype=bool), segment_ids[1:] != segment_ids[:-1]])
    starts = lax.cummax(jnp.where(change, index, 0), axis=0)
    return index - starts


def contract_first(left, right):
    return lax.dot_general(
        left, right, (((0,), (0,)), ((), ())), preferred_element_type=jnp.float32
    )


def contract_last(left, right):
    return lax.dot_general(
        left, right, (((1,), (1,)), ((), ())), preferred_element_type=jnp.float32
    )


def local(
    tokens,
    segment_ids,
    w_query,
    w_key,
    w_value,
    w_out,
    w_gate,
    w_up,
    w_down,
    gain_attn_in,
    gain_attn_out,
    gain_ffn_in,
    gain_ffn_out,
    gain_query,
    gain_key,
    cotangent,
):
    heads = lax.axis_size("head")
    head_index = lax.axis_index("head")
    seq_index = lax.axis_index("seq")
    local_rows = tokens.shape[0]
    width = gain_query.shape[0]
    qcount = w_query.shape[1] // width
    group = local_rows * heads
    total = segment_ids.shape[0]
    scale = 1.0 / math.sqrt(width)
    first_row = (seq_index * heads + head_index) * local_rows
    positions = row_positions(segment_ids)
    my_positions = lax.dynamic_slice_in_dim(positions, first_row, local_rows)
    cosines, sines = rope_tables(my_positions, width)

    def query_path(linear, gain):
        shaped = linear.reshape(local_rows, qcount, width)
        turned = rotate(norm_rows(shaped, gain), cosines[:, None, :], sines[:, None, :])
        return turned.reshape(local_rows, qcount * width)

    def key_path(linear, gain):
        return rotate(norm_rows(linear, gain), cosines, sines)

    def gated(gate, up):
        return jax.nn.gelu(gate, approximate=True) * up

    inputs = tokens.astype(jnp.float32)
    attn_in = norm_rows(inputs, gain_attn_in).astype(jnp.bfloat16)
    q_linear = jnp.dot(attn_in, w_query, preferred_element_type=jnp.float32)
    queries_local = query_path(q_linear, gain_query).astype(jnp.bfloat16)
    k_linear = jnp.dot(attn_in, w_key, preferred_element_type=jnp.float32)
    keys_local = key_path(k_linear, gain_key).astype(jnp.bfloat16)
    values_local = jnp.dot(attn_in, w_value, preferred_element_type=jnp.float32).astype(
        jnp.bfloat16
    )
    queries = lax.all_to_all(queries_local, "head", split_axis=1, concat_axis=0, tiled=True)
    keys, values = (
        lax.all_gather(keys_local, ("seq", "head"), axis=0, tiled=True),
        lax.all_gather(values_local, ("seq", "head"), axis=0, tiled=True),
    )
    key_block = min(512, total)
    query_start = seq_index * group
    query_index = query_start + jnp.arange(group, dtype=jnp.int32)
    query_seg = lax.dynamic_slice_in_dim(segment_ids, query_start, group)
    needed = ((seq_index + 1) * group + key_block - 1) // key_block

    def block_scores(block):
        start = block * key_block
        key_rows = lax.dynamic_slice_in_dim(keys, start, key_block)
        value_rows = lax.dynamic_slice_in_dim(values, start, key_block)
        key_seg = lax.dynamic_slice_in_dim(segment_ids, start, key_block)
        key_index = start + jnp.arange(key_block, dtype=jnp.int32)
        allowed = (query_seg[:, None] == key_seg[None, :]) & (
            key_index[None, :] <= query_index[:, None]
        )
        raw = contract_last(queries, key_rows)
        return (jnp.where(allowed, raw * scale, NEG), allowed, key_rows, value_rows)

    def running_total(block, carry):
        top, mass = carry
        scores, allowed, key_rows, value_rows = block_scores(block)
        new_top = jnp.maximum(top, jnp.max(scores, axis=1))
        terms = jnp.where(allowed, jnp.exp(scores - new_top[:, None]), 0.0)
        return (new_top, mass * jnp.exp(top - new_top) + jnp.sum(terms, axis=1))

    top, mass = lax.fori_loop(
        0,
        needed,
        running_total,
        (jnp.full((group,), NEG, jnp.float32), jnp.zeros((group,), jnp.float32)),
    )
    log_total = top + jnp.log(mass)

    def add_values(block, accum):
        scores, allowed, key_rows, value_rows = block_scores(block)
        probs = jnp.where(allowed, jnp.exp(scores - log_total[:, None]), 0.0).astype(jnp.bfloat16)
        return accum + jnp.dot(probs, value_rows, preferred_element_type=jnp.float32)

    attended = lax.fori_loop(0, needed, add_values, jnp.zeros((group, width), jnp.float32))
    mixed_local = lax.all_to_all(
        attended.astype(jnp.bfloat16), "head", split_axis=0, concat_axis=1, tiled=True
    )
    projected = jnp.dot(mixed_local, w_out, preferred_element_type=jnp.float32)
    hidden = inputs + norm_rows(projected, gain_attn_out)
    ffn_in = norm_rows(hidden, gain_ffn_in).astype(jnp.bfloat16)
    ffn_rows = lax.all_gather(ffn_in, "head", axis=0, tiled=True)
    gate = jnp.dot(ffn_rows, w_gate, preferred_element_type=jnp.float32)
    up = jnp.dot(ffn_rows, w_up, preferred_element_type=jnp.float32)
    activated = gated(gate, up).astype(jnp.bfloat16)
    ffn_out = lax.psum_scatter(
        jnp.dot(activated, w_down, preferred_element_type=jnp.float32).astype(jnp.bfloat16),
        "head",
        scatter_dimension=0,
        tiled=True,
    ).astype(jnp.float32)
    output = hidden + norm_rows(ffn_out, gain_ffn_out)
    upstream = cotangent.astype(jnp.float32)
    unused, back_four = jax.vjp(norm_rows, ffn_out, gain_ffn_out)
    d_ffn_out, d_gain_four = back_four(upstream)
    d_ffn_rows = lax.all_gather(d_ffn_out.astype(jnp.bfloat16), "head", axis=0, tiled=True)
    d_activated = contract_last(d_ffn_rows, w_down)
    d_w_down = contract_first(activated, d_ffn_rows)
    unused, back_gate = jax.vjp(gated, gate, up)
    d_gate, d_up = back_gate(d_activated)
    d_gate = d_gate.astype(jnp.bfloat16)
    d_up = d_up.astype(jnp.bfloat16)
    d_w_gate = contract_first(ffn_rows, d_gate)
    d_w_up = contract_first(ffn_rows, d_up)
    d_ffn_in = lax.psum_scatter(
        (contract_last(d_gate, w_gate) + contract_last(d_up, w_up)).astype(jnp.bfloat16),
        "head",
        scatter_dimension=0,
        tiled=True,
    ).astype(jnp.float32)
    unused, back_three = jax.vjp(norm_rows, hidden, gain_ffn_in)
    d_hidden_part, d_gain_three = back_three(d_ffn_in)
    d_hidden = upstream + d_hidden_part
    unused, back_two = jax.vjp(norm_rows, projected, gain_attn_out)
    d_projected, d_gain_two = back_two(d_hidden)
    d_projected = d_projected.astype(jnp.bfloat16)
    d_w_out = contract_first(mixed_local, d_projected)
    d_mixed = contract_last(d_projected, w_out).astype(jnp.bfloat16)
    grad_attended = lax.all_to_all(d_mixed, "head", split_axis=1, concat_axis=0, tiled=True)
    row_dots = jnp.sum(grad_attended.astype(jnp.float32) * attended, axis=1)

    def back_block(block, carry):
        d_queries, key_terms = carry
        scores, allowed, key_rows, value_rows = block_scores(block)
        probs = jnp.where(allowed, jnp.exp(scores - log_total[:, None]), 0.0)
        d_values = contract_first(probs.astype(jnp.bfloat16), grad_attended)
        d_probs = contract_last(grad_attended, value_rows)
        d_scores = (probs * (d_probs - row_dots[:, None]) * scale).astype(jnp.bfloat16)
        d_queries = d_queries + jnp.dot(d_scores, key_rows, preferred_element_type=jnp.float32)
        d_keys = contract_first(d_scores, queries)
        key_terms = lax.dynamic_update_slice_in_dim(
            key_terms, jnp.concatenate([d_keys, d_values], axis=1), block * key_block, 0
        )
        return (d_queries, key_terms)

    d_queries, key_terms = lax.fori_loop(
        0,
        needed,
        back_block,
        (jnp.zeros((group, width), jnp.float32), jnp.zeros((total, 2 * width), jnp.float32)),
    )
    sectioned = lax.psum_scatter(
        key_terms.reshape(total // group, group, 2 * width).astype(jnp.bfloat16),
        "seq",
        scatter_dimension=0,
        tiled=True,
    ).astype(jnp.float32)
    key_grads = lax.psum_scatter(
        sectioned.reshape(group, 2 * width).astype(jnp.bfloat16),
        "head",
        scatter_dimension=0,
        tiled=True,
    ).astype(jnp.float32)
    d_query_rot = lax.all_to_all(
        d_queries.astype(jnp.bfloat16), "head", split_axis=0, concat_axis=1, tiled=True
    ).astype(d_queries.dtype)
    unused, back_query = jax.vjp(query_path, q_linear, gain_query)
    d_q_linear, d_gain_query = back_query(d_query_rot)
    unused, back_key = jax.vjp(key_path, k_linear, gain_key)
    d_k_linear, d_gain_key = back_key(key_grads[:, :width])
    d_q_linear = d_q_linear.astype(jnp.bfloat16)
    d_k_linear = d_k_linear.astype(jnp.bfloat16)
    d_v_linear = key_grads[:, width:].astype(jnp.bfloat16)
    d_w_query = contract_first(attn_in, d_q_linear)
    d_w_key = contract_first(attn_in, d_k_linear)
    d_w_value = contract_first(attn_in, d_v_linear)
    d_attn_in = (
        contract_last(d_q_linear, w_query)
        + contract_last(d_k_linear, w_key)
        + contract_last(d_v_linear, w_value)
    )
    unused, back_one = jax.vjp(norm_rows, inputs, gain_attn_in)
    d_inputs, d_gain_one = back_one(d_attn_in)
    grad_tokens = (d_hidden + d_inputs).astype(jnp.bfloat16)
    block_sums = (
        lax.psum_scatter(d_w_query, ("seq", "head"), scatter_dimension=0, tiled=True),
        lax.psum_scatter(d_w_key, ("seq", "head"), scatter_dimension=0, tiled=True),
        lax.psum_scatter(d_w_value, ("seq", "head"), scatter_dimension=0, tiled=True),
        lax.psum_scatter(d_w_out, ("seq", "head"), scatter_dimension=0, tiled=True),
        lax.psum_scatter(d_gain_one, ("seq", "head"), scatter_dimension=0, tiled=True),
        lax.psum_scatter(d_gain_two, ("seq", "head"), scatter_dimension=0, tiled=True),
        lax.psum_scatter(d_gain_three, ("seq", "head"), scatter_dimension=0, tiled=True),
        lax.psum_scatter(d_gain_four, ("seq", "head"), scatter_dimension=0, tiled=True),
        lax.psum_scatter(d_gain_query, ("seq", "head"), scatter_dimension=0, tiled=True),
        lax.psum_scatter(d_gain_key, ("seq", "head"), scatter_dimension=0, tiled=True),
    )
    ffn_sums = (
        lax.psum_scatter(
            d_w_gate.astype(jnp.bfloat16), "seq", scatter_dimension=0, tiled=True
        ).astype(jnp.float32),
        lax.psum_scatter(
            d_w_up.astype(jnp.bfloat16), "seq", scatter_dimension=0, tiled=True
        ).astype(jnp.float32),
        lax.psum_scatter(
            d_w_down.astype(jnp.bfloat16), "seq", scatter_dimension=1, tiled=True
        ).astype(jnp.float32),
    )
    return (
        output.astype(jnp.bfloat16),
        grad_tokens,
        block_sums[0],
        block_sums[1],
        block_sums[2],
        block_sums[3],
        ffn_sums[0],
        ffn_sums[1],
        ffn_sums[2],
        block_sums[4],
        block_sums[5],
        block_sums[6],
        block_sums[7],
        block_sums[8],
        block_sums[9],
    )


def solution(mesh):
    in_specs = (
        P(("seq", "head"), None),
        P(),
        P(),
        P(),
        P(),
        P(),
        P(None, "head"),
        P(None, "head"),
        P("head", None),
        P(),
        P(),
        P(),
        P(),
        P(),
        P(),
        P(("seq", "head"), None),
    )
    out_specs = (
        P(("seq", "head"), None),
        P(("seq", "head"), None),
        P(("seq", "head"), None),
        P(("seq", "head"), None),
        P(("seq", "head"), None),
        P(("seq", "head"), None),
        P("seq", "head"),
        P("seq", "head"),
        P("head", "seq"),
        P(("seq", "head")),
        P(("seq", "head")),
        P(("seq", "head")),
        P(("seq", "head")),
        P(("seq", "head")),
        P(("seq", "head")),
    )
    return jax.shard_map(local, mesh=mesh, in_specs=in_specs, out_specs=out_specs, check_vma=False)
```

profile of v0, /device:TPU:0, one launch (start us, length us, event | category | flops | bytes accessed | tf_op | source)
XLA Modules:
  0.0 933.1 jit_solution(11620761408420483461)
XLA Ops:
  10.1 1.5 multiply_reduce_fusion.10
  14.1 2.1 convolution_convert_fusion.5
  16.3 2.2 fusion.118
  24.1 6.3 all-to-all-start
  30.5 9.4 %all-to-all-done = bf16[128,4,256]{2,0,1:T(8,128)(2,1)S(1)} async-done(((bf16[128,4,256]{2,0,1:T(8,128)(2,1)}), bf16[128,4,256]{2,0,1:T(8,128)(2,1)S(1)}, u32[]{:S(2)}, u32[]{:S(2)}) %all-to-all-start) | async-done | bytes 262176 | tf_op jit(solution)/shard_map/all_to_all | solution.py:104
  39.9 35.2 %all-gather.5.cloned.1.call-done = bf16[4096,256]{1,0:T(8,128)(2,1)} async-done(((bf16[128,256]{1,0:T(8,128)(2,1)}), bf16[4096,256]{1,0:T(8,128)(2,1)}) %all-gather.5.cloned.1.call-update) | async-done | bytes 2097168 | tf_op jit(solution)/shard_map/all_gather | solution.py:106
  75.1 1.8 while.37
  77.0 57.0 %all-gather.7.cloned.1.call-done = bf16[4096,256]{1,0:T(8,128)(2,1)} async-done(((bf16[128,256]{1,0:T(8,128)(2,1)}), bf16[4096,256]{1,0:T(8,128)(2,1)}) %all-gather.7.cloned.1.call-update) | async-done | bytes 2097168 | tf_op jit(solution)/shard_map/all_gather | solution.py:107
  134.0 2.0 while.38
  134.1 1.9 fusion.196
  136.1 11.4 %all_to_all.67 = bf16[4,128,256]{2,1,0:T(8,128)(2,1)} all-to-all(bf16[4,128,256]{2,1,0:T(8,128)(2,1)S(1)} %bitcast.135), channel_id=1, replica_groups=mesh['seq'=8,'head'=4] {'head'}, dimensions={0} | all-to-all | bytes 524288 | tf_op jit(solution)/shard_map/all_to_all | solution.py:148
  147.5 1.8 copy.99
  149.3 1.6 multiply_reduce_fusion.3
  153.9 41.8 %all-gather.9.cloned.1.call-done = bf16[512,1152]{1,0:T(8,128)(2,1)} async-done(((bf16[128,1152]{1,0:T(8,128)(2,1)}), bf16[512,1152]{1,0:T(8,128)(2,1)}) %all-gather.9.cloned.1.call-update) | async-done | bytes 1179664 | tf_op jit(solution)/shard_map/all_gather | solution.py:154
  195.7 5.1 fusion.125
  200.9 5.0 multiply_convert_fusion.1
  207.1 3.6 convolution_convert_fusion.3
  210.8 28.4 %reduce-scatter.15.cloned.1.call-done = bf16[128,1152]{1,0:T(8,128)(2,1)} async-done(((bf16[512,1152]{1,0:T(8,128)(2,1)}), bf16[128,1152]{1,0:T(8,128)(2,1)}) %reduce-scatter.15.cloned.1.call-update) | async-done | bytes 294928 | tf_op jit(solution)/shard_map/reduce_scatter | solution.py:158
  240.3 1.9 fusion.77
  242.2 1.9 fusion.78
  244.4 29.1 %all-gather.11.cloned.1.call-done = bf16[512,1152]{1,0:T(8,128)(2,1)} async-done(((bf16[128,1152]{1,0:T(8,128)(2,1)}), bf16[512,1152]{1,0:T(8,128)(2,1)}) %all-gather.11.cloned.1.call-update) | async-done | bytes 1179664 | tf_op jit(solution)/shard_map/all_gather | solution.py:168
  273.5 9.7 %multiply_convert_fusion = (bf16[512,1728]{0,1:T(8,128)(2,1)S(1)}, bf16[512,1728]{0,1:T(8,128)(2,1)S(1)}) fusion(f32[512,1728]{0,1:T(8,128)} %copy-done.74, f32[512,1728]{0,1:T(8,128)} %get-tuple-element.386, bf16[512,1152]{1,0:T(8,128)(2,1)} %all-gather.11.cloned.1.call-done, bf16[1728,1152]{1,0:T(8,128)(2,1)} %param.30), kind=kOutput, calls=%fused_computation.76 | convolution fusion | flops 2059665408 | bytes 15777792 | tf_op jit(solution)/shard_map/dot_general | solution.py:47
  283.2 2.7 fusion.126
  286.6 3.7 fusion.64
  290.3 28.4 %reduce-scatter.17.cloned.1.call-done = bf16[128,1152]{1,0:T(8,128)(2,1)} async-done(((bf16[512,1152]{1,0:T(8,128)(2,1)}), bf16[128,1152]{1,0:T(8,128)(2,1)}) %reduce-scatter.17.cloned.1.call-update) | async-done | bytes 294928 | tf_op jit(solution)/shard_map/reduce_scatter | solution.py:177
  318.8 1.8 fusion.76
  321.2 3.1 multiply_reduce_fusion
  327.7 3.4 all-to-all-start.2
  331.2 9.0 all-to-all-done.2
  340.4 2.5 broadcast_in_dim.56
  342.8 5.9 while.39
  348.8 6.6 copy.104
  356.7 5.7 convolution_convert_fusion.2
  363.9 5.6 convolution_convert_fusion.1
  370.7 5.9 convolution_convert_fusion
  376.7 68.0 %reduce-scatter.19.cloned.1.call-done = bf16[1,512,512]{2,1,0:T(8,128)(2,1)} async-done(((bf16[8,512,512]{2,1,0:T(8,128)(2,1)}), bf16[1,512,512]{2,1,0:T(8,128)(2,1)}) %reduce-scatter.19.cloned.1.call-update) | async-done | bytes 524304 | tf_op jit(solution)/shard_map/reduce_scatter | solution.py:214
  445.4 4.6 all-to-all-start.3
  450.3 3.0 fusion.128
  453.3 5.7 all-to-all-done.3
  463.1 3.1 fusion.115
  466.2 33.4 %reduce-scatter.25.cloned.1.call-done = bf16[144,1728]{1,0:T(8,128)(2,1)} async-done(((bf16[1152,1728]{1,0:T(8,128)(2,1)}), bf16[144,1728]{1,0:T(8,128)(2,1)}) %reduce-scatter.25.cloned.1.call-update) | async-done | bytes 497680 | tf_op jit(solution)/shard_map/reduce_scatter | solution.py:260
  499.6 2.1 convert_element_type.155
  501.6 52.9 %reduce-scatter.27.cloned.1.call-done = bf16[144,1728]{1,0:T(8,128)(2,1)} async-done(((bf16[1152,1728]{1,0:T(8,128)(2,1)}), bf16[144,1728]{1,0:T(8,128)(2,1)}) %reduce-scatter.27.cloned.1.call-update) | async-done | bytes 497680 | tf_op jit(solution)/shard_map/reduce_scatter | solution.py:263
  554.5 2.1 convert_element_type.157
  556.6 52.7 %reduce-scatter.29.cloned.1.call-done = bf16[1728,144]{0,1:T(8,128)(2,1)} async-done(((bf16[1728,1152]{0,1:T(8,128)(2,1)}), bf16[1728,144]{0,1:T(8,128)(2,1)}) %reduce-scatter.29.cloned.1.call-update) | async-done | bytes 497680 | tf_op jit(solution)/shard_map/reduce_scatter | solution.py:266
  609.3 2.1 convert_element_type.159
  611.3 22.0 %reduce-scatter.21.cloned.1.call-done = bf16[128,512]{1,0:T(8,128)(2,1)} async-done(((bf16[512,512]{1,0:T(8,128)(2,1)}), bf16[128,512]{1,0:T(8,128)(2,1)}) %reduce-scatter.21.cloned.1.call-update) | async-done | bytes 131088 | tf_op jit(solution)/shard_map/reduce_scatter | solution.py:220
  637.1 194.6 %fusion.122 = (f32[40,1024]{1,0:T(8,128)S(1)}, f32[40,256]{1,0:T(8,128)}, f32[40,256]{1,0:T(8,128)S(1)}) fusion(f32[1152,1024]{1,0:T(8,128)} %fusion.115, f32[1152,256]{1,0:T(8,128)S(1)} %fusion.113, f32[1152,256]{1,0:T(8,128)S(1)} %fusion.102), kind=kCustom, calls=%all-reduce-scatter.3 | all-reduce-scatter fusion | flops 1966081 | bytes 7323648
  832.5 1.9 collective-permute-start.6
  834.4 2.2 collective-permute-start.5
  836.6 1.9 collective-permute-start.4
  838.5 1.9 collective-permute-start.7
  840.4 1.5 convolution_add_fusion.3
  842.0 1.5 fusion.72
  843.5 5.2 collective-permute-start.10
  848.8 3.3 collective-permute-start.11
  853.2 38.2 %all-reduce.16 = (f32[1152]{0:T(1024)S(1)}, f32[1152]{0:T(1024)S(1)}, f32[1152]{0:T(1024)S(1)}, f32[1152]{0:T(1024)S(1)}, f32[256]{0:T(256)S(1)}, /*index=5*/f32[256]{0:T(256)S(1)}) all-reduce(f32[1152]{0:T(1024)S(1)} %get-tuple-element.273, f32[1152]{0:T(1024)S(1)} %copy-done.38, ...), channel_id=13, replica_groups=mesh['seq'=8,'head'=4] {'seq','head'}, use_global_device_ids=true, to_apply=%region_35.36.clone | all-reduce | flops 5120 | bytes 40960
  894.9 4.2 collective-permute-start.2
  899.1 2.6 collective-permute-start.1
  901.8 3.2 collective-permute-start
  905.0 3.3 concatenate.22
  908.3 3.9 collective-permute-start.9
  912.2 5.4 collective-permute-start.8
  922.1 3.2 concatenate.21
  (281 shorter events, 52.2 us)
Async XLA Ops:
  7.2 142.1 %copy-start = (bf16[1024,1152]{1,0:T(8,128)(2,1)S(1)}, bf16[1024,1152]{1,0:T(8,128)(2,1)}, u32[]{:S(2)}) copy-start(bf16[1024,1152]{1,0:T(8,128)(2,1)} %param.27) | copy-start | bytes 7077892
  7.2 9.1 copy-start.2
  7.2 9.1 copy-start.24
  7.2 67.9 %all-gather.5.cloned.1.call-start = ((), (), s32[]{:S(2)}) async-start(), calls=%async_computation.12 | async-start | bytes 2162688 | tf_op jit(solution)/shard_map/all_gather | solution.py:106
  7.3 12.3 %copy-start.56 = (f32[128]{0:T(128)}, f32[128]{0:T(128)S(1)}, u32[]{:S(2)}) copy-start(f32[128]{0:T(128)S(1)} %multiply_exponential_fusion) | copy-start | bytes 1540
  10.1 9.5 %copy-start.41 = (f32[128]{0:T(128)}, f32[128]{0:T(128)S(1)}, u32[]{:S(2)}) copy-start(f32[128]{0:T(128)S(1)} %fusion.107) | copy-start | bytes 1540
  14.1 119.9 %all-gather.7.cloned.1.call-start = ((), (), s32[]{:S(2)}) async-start(), calls=%async_computation.13 | async-start | bytes 2162688 | tf_op jit(solution)/shard_map/all_gather | solution.py:107
  18.5 11.9 %copy-start.25 = (s32[4096]{0:T(1024)S(1)}, s32[4096]{0:T(1024)}, u32[]{:S(2)}) copy-start(s32[4096]{0:T(1024)} %param.23) | copy-start | bytes 49156
  20.8 54.3 %copy-start.8 = (f32[128,4,256]{0,2,1:T(8,128)}, f32[128,4,256]{0,2,1:T(8,128)S(1)}, u32[]{:S(2)}) copy-start(f32[128,4,256]{0,2,1:T(8,128)S(1)} %copy.95) | copy-start | bytes 1572868
  24.1 15.8 %all-to-all-start = ((bf16[128,4,256]{2,0,1:T(8,128)(2,1)}), bf16[128,4,256]{2,0,1:T(8,128)(2,1)S(1)}, u32[]{:S(2)}, u32[]{:S(2)}) async-start(bf16[128,4,256]{2,0,1:T(8,128)(2,1)} %copy.98), calls=%async_computation | async-start | bytes 524288 | tf_op jit(solution)/shard_map/all_to_all | solution.py:104
  30.4 165.3 %all-gather.9.cloned.1.call-start = ((), (), s32[]{:S(2)}) async-start(), calls=%async_computation.14 | async-start | bytes 1474560 | tf_op jit(solution)/shard_map/all_gather | solution.py:154
  136.0 14.9 %copy-start.14 = (f32[512,256]{1,0:T(8,128)}, f32[512,256]{1,0:T(8,128)S(1)}, u32[]{:S(2)}) copy-start(f32[512,256]{1,0:T(8,128)S(1)} %get-tuple-element.188) | copy-start | bytes 1572868
  136.0 14.9 %copy-start.32 = (s32[512]{0:T(512)}, s32[512]{0:T(512)S(1)}, u32[]{:S(2)}) copy-start(s32[512]{0:T(512)S(1)} %get-tuple-element.800) | copy-start | bytes 6148
  136.0 14.9 %copy-start.58 = (f32[512]{0:T(512)}, f32[512]{0:T(512)S(1)}, u32[]{:S(2)}) copy-start(f32[512]{0:T(512)S(1)} %get-tuple-element.812) | copy-start | bytes 6148
  136.1 15.6 %copy-start.31 = (f32[1152]{0:T(1024)S(1)}, f32[1152]{0:T(1024)}, u32[]{:S(2)}) copy-start(f32[1152]{0:T(1024)} %param.32) | copy-start | bytes 13828
  136.1 16.4 %copy-start.29 = (f32[1152]{0:T(1024)S(1)}, f32[1152]{0:T(1024)}, u32[]{:S(2)}) copy-start(f32[1152]{0:T(1024)} %param.33) | copy-start | bytes 13828
  150.9 49.9 %copy-start.49 = (f32[128]{0:T(128)}, f32[128]{0:T(128)S(1)}, u32[]{:S(2)}) copy-start(f32[128]{0:T(128)S(1)} %fusion.109) | copy-start | bytes 1540
  152.5 48.4 %copy-start.53 = (f32[128]{0:T(128)}, f32[128]{0:T(128)S(1)}, u32[]{:S(2)}) copy-start(f32[128]{0:T(128)S(1)} %fusion.110) | copy-start | bytes 1540
  153.3 85.9 %reduce-scatter.15.cloned.1.call-start = ((), (), s32[]{:S(2)}) async-start(), calls=%async_computation.15 | async-start | bytes 1474560 | tf_op jit(solution)/shard_map/reduce_scatter | solution.py:158
  207.1 33.2 %copy-start.30 = (f32[1152]{0:T(1024)S(1)}, f32[1152]{0:T(1024)}, u32[]{:S(2)}) copy-start(f32[1152]{0:T(1024)} %param.34) | copy-start | bytes 13828
  210.8 62.8 %all-gather.11.cloned.1.call-start = ((), (), s32[]{:S(2)}) async-start(), calls=%async_computation.16 | async-start | bytes 1474560 | tf_op jit(solution)/shard_map/all_gather | solution.py:168
  244.2 74.5 %reduce-scatter.17.cloned.1.call-start = ((), (), s32[]{:S(2)}) async-start(), calls=%async_computation.17 | async-start | bytes 1474560 | tf_op jit(solution)/shard_map/reduce_scatter | solution.py:177
  273.5 9.7 %copy-start.66 = (bf16[1152,1728]{0,1:T(8,128)(2,1)S(1)}, bf16[1152,1728]{0,1:T(8,128)(2,1)}, u32[]{:S(2)}) copy-start(bf16[1152,1728]{0,1:T(8,128)(2,1)} %param.28) | copy-start | bytes 11943940
  324.4 15.8 %copy-start.15 = (f32[512,256]{1,0:T(8,128)S(1)}, f32[512,256]{1,0:T(8,128)}, u32[]{:S(2)}) copy-start(f32[512,256]{1,0:T(8,128)} %copy-done.14) | copy-start | bytes 1572868
  327.0 15.8 %copy-start.33 = (s32[512]{0:T(512)S(1)}, s32[512]{0:T(512)}, u32[]{:S(2)}) copy-start(s32[512]{0:T(512)} %copy-done.32) | copy-start | bytes 6148
  327.0 15.8 %copy-start.59 = (f32[512]{0:T(512)S(1)}, f32[512]{0:T(512)}, u32[]{:S(2)}) copy-start(f32[512]{0:T(512)} %copy-done.58) | copy-start | bytes 6148
  327.7 12.4 %all-to-all-start.2 = ((bf16[128,4,256]{2,0,1:T(8,128)(2,1)}), bf16[128,4,256]{2,0,1:T(8,128)(2,1)S(1)}, u32[]{:S(2)}, u32[]{:S(2)}) async-start(bf16[128,4,256]{2,0,1:T(8,128)(2,1)} %bitcast.105), calls=%async_computation.4 | async-start | bytes 524288 | tf_op jit(solution)/shard_map/all_to_all | solution.py:191
  331.2 113.5 %reduce-scatter.19.cloned.1.call-start = ((), (), s32[]{:S(2)}) async-start(), calls=%async_computation.18 | async-start | bytes 4718592 | tf_op jit(solution)/shard_map/reduce_scatter | solution.py:214
  355.4 144.2 %reduce-scatter.25.cloned.1.call-start = ((), (), s32[]{:S(2)}) async-start(), calls=%async_computation.21 | async-start | bytes 4644864 | tf_op jit(solution)/shard_map/reduce_scatter | solution.py:260
  362.4 192.1 %reduce-scatter.27.cloned.1.call-start = ((), (), s32[]{:S(2)}) async-start(), calls=%async_computation.22 | async-start | bytes 4644864 | tf_op jit(solution)/shard_map/reduce_scatter | solution.py:263
  369.5 239.8 %reduce-scatter.29.cloned.1.call-start = ((), (), s32[]{:S(2)}) async-start(), calls=%async_computation.23 | async-start | bytes 4644864 | tf_op jit(solution)/shard_map/reduce_scatter | solution.py:266
  376.6 73.7 %copy-start.17 = (bf16[128,1152]{1,0:T(8,128)(2,1)S(1)}, bf16[128,1152]{1,0:T(8,128)(2,1)}, u32[]{:S(2)}) copy-start(bf16[128,1152]{1,0:T(8,128)(2,1)} %copy-done.16) | copy-start | bytes 884740
  376.6 73.7 %copy-start.18 = (bf16[128,4,256]{0,2,1:T(8,128)(2,1)S(1)}, bf16[128,4,256]{0,2,1:T(8,128)(2,1)}, u32[]{:S(2)}) copy-start(bf16[128,4,256]{0,2,1:T(8,128)(2,1)} %copy.99) | copy-start | bytes 786436
  376.6 256.7 %reduce-scatter.21.cloned.1.call-start = ((), (), s32[]{:S(2)}) async-start(), calls=%async_computation.19 | async-start | bytes 655360 | tf_op jit(solution)/shard_map/reduce_scatter | solution.py:220
  445.4 13.6 %all-to-all-start.3 = ((bf16[4,128,256]{2,1,0:T(8,128)(2,1)}), bf16[4,128,256]{2,1,0:T(8,128)(2,1)}, u32[]{:S(2)}, u32[]{:S(2)}) async-start(bf16[4,128,256]{2,1,0:T(8,128)(2,1)} %bitcast.11), calls=%async_computation.5 | async-start | bytes 524288 | tf_op jit(solution)/shard_map/all_to_all | solution.py:226
  450.0 476.0 %reduce-scatter.23.cloned.1.call-start = ((), (), s32[]{:S(2)}) async-start(), calls=%async_computation.20 | async-start | bytes 4866048 | tf_op jit(solution)/shard_map/reduce_scatter | solution.py:251
  453.3 8.7 copy-start.40
  453.3 8.8 copy-start.5
  466.1 168.1 %copy-start.52 = (f32[128]{0:T(128)S(1)}, f32[128]{0:T(128)}, u32[]{:S(2)}) copy-start(f32[128]{0:T(128)} %copy-done.51) | copy-start | bytes 1540
  466.1 168.1 %copy-start.57 = (f32[128]{0:T(128)S(1)}, f32[128]{0:T(128)}, u32[]{:S(2)}) copy-start(f32[128]{0:T(128)} %copy-done.56) | copy-start | bytes 1540
  466.1 168.4 %copy-start.20 = (f32[128,256]{1,0:T(8,128)S(1)}, f32[128,256]{1,0:T(8,128)}, u32[]{:S(2)}) copy-start(f32[128,256]{1,0:T(8,128)} %copy-done.19) | copy-start | bytes 393220
  466.1 168.5 %copy-start.44 = (f32[256]{0:T(256)S(1)}, f32[256]{0:T(256)}, u32[]{:S(2)}) copy-start(f32[256]{0:T(256)} %param.36) | copy-start | bytes 3076
  466.1 168.5 %copy-start.48 = (f32[128]{0:T(128)S(1)}, f32[128]{0:T(128)}, u32[]{:S(2)}) copy-start(f32[128]{0:T(128)} %copy-done.47) | copy-start | bytes 1540
  466.2 169.1 %copy-start.71 = (f32[128]{0:T(128)S(1)}, f32[128]{0:T(128)}, u32[]{:S(2)}) copy-start(f32[128]{0:T(128)} %copy-done.70) | copy-start | bytes 1540
  831.7 11.8 %copy-start.62 = (f32[128]{0:T(128)S(1)}, f32[128]{0:T(128)}, u32[]{:S(2)}) copy-start(f32[128]{0:T(128)} %copy-done.61) | copy-start | bytes 1540
  831.7 20.5 %copy-start.13 = (f32[128,1152]{1,0:T(8,128)S(1)}, f32[128,1152]{1,0:T(8,128)}, u32[]{:S(2)}) copy-start(f32[128,1152]{1,0:T(8,128)} %copy-done.12) | copy-start | bytes 1769476
  831.7 20.5 %copy-start.43 = (f32[128]{0:T(128)S(1)}, f32[128]{0:T(128)}, u32[]{:S(2)}) copy-start(f32[128]{0:T(128)} %copy-done.41) | copy-start | bytes 1540
  831.7 21.4 %copy-start.36 = (f32[1152]{0:T(1024)S(1)}, f32[1152]{0:T(1024)}, u32[]{:S(2)}) copy-start(f32[1152]{0:T(1024)} %get-tuple-element.275) | copy-start | bytes 13828
  831.7 21.4 %copy-start.37 = (f32[1152]{0:T(1024)S(1)}, f32[1152]{0:T(1024)}, u32[]{:S(2)}) copy-start(f32[1152]{0:T(1024)} %get-tuple-element.271) | copy-start | bytes 13828
  831.7 21.4 %copy-start.38 = (f32[1152]{0:T(1024)S(1)}, f32[1152]{0:T(1024)}, u32[]{:S(2)}) copy-start(f32[1152]{0:T(1024)} %get-tuple-element.267) | copy-start | bytes 13828
  832.5 62.4 %collective-permute-start.6 = (f32[40,256]{1,0:T(8,128)}, f32[40,256]{1,0:T(8,128)}, u32[]{:S(2)}, u32[]{:S(2)}) collective-permute-start(f32[40,256]{1,0:T(8,128)} %get-tuple-element.353), channel_id=1, source_target_pairs={{0,3},{1,4},{2,5},{3,6},{4,7},{5,8},{6,9},{7,10},{8,11},{9,12},{10... | collective-permute-start | bytes 122888
  834.4 64.7 %collective-permute-start.5 = (f32[40,256]{1,0:T(8,128)}, f32[40,256]{1,0:T(8,128)}, u32[]{:S(2)}, u32[]{:S(2)}) collective-permute-start(f32[40,256]{1,0:T(8,128)} %get-tuple-element.353), channel_id=1, source_target_pairs={{0,2},{1,3},{2,4},{3,5},{4,6},{5,7},{6,8},{7,9},{8,10},{9,11},{10,... | collective-permute-start | bytes 122888
  836.6 65.2 %collective-permute-start.4 = (f32[40,256]{1,0:T(8,128)}, f32[40,256]{1,0:T(8,128)}, u32[]{:S(2)}, u32[]{:S(2)}) collective-permute-start(f32[40,256]{1,0:T(8,128)} %get-tuple-element.353), channel_id=1, source_target_pairs={{0,1},{1,2},{2,3},{3,4},{4,5},{5,6},{6,7},{7,8},{8,9},{9,10},{10,1... | collective-permute-start | bytes 122888
  838.5 10.3 %collective-permute-start.7 = (f32[4,256]{1,0:T(4,128)S(1)}, f32[4,256]{1,0:T(4,128)S(1)}, u32[]{:S(2)}, u32[]{:S(2)}) collective-permute-start(f32[4,256]{1,0:T(4,128)S(1)} %slice.49), channel_id=1, source_target_pairs={{0,4},{1,5},{2,6},{3,7},{4,8},{5,9},{6,10},{7,11},{8,12},{9,13},{1... | collective-permute-start | bytes 12296
  840.4 85.6 %copy-start.1 = (bf16[1024,1152]{1,0:T(8,128)(2,1)S(1)}, bf16[1024,1152]{1,0:T(8,128)(2,1)}, u32[]{:S(2)}) copy-start(bf16[1024,1152]{1,0:T(8,128)(2,1)} %param.27) | copy-start | bytes 7077892
  842.0 63.0 %copy-start.26 = (f32[40,256]{1,0:T(8,128)S(1)}, f32[40,256]{1,0:T(8,128)}, u32[]{:S(2)}) copy-start(f32[40,256]{1,0:T(8,128)} %get-tuple-element.353) | copy-start | bytes 122884
  843.5 68.7 %collective-permute-start.10 = (f32[40,256]{1,0:T(8,128)S(1)}, f32[40,256]{1,0:T(8,128)S(1)}, u32[]{:S(2)}, u32[]{:S(2)}) collective-permute-start(f32[40,256]{1,0:T(8,128)S(1)} %get-tuple-element.354), channel_id=1, source_target_pairs={{0,3},{1,4},{2,5},{3,6},{4,7},{5,8},{6,9},{7,10},{8,11},{9,12},{10... | collective-permute-start | bytes 122888
  848.8 59.5 %collective-permute-start.11 = (f32[4,256]{1,0:T(4,128)S(1)}, f32[4,256]{1,0:T(4,128)S(1)}, u32[]{:S(2)}, u32[]{:S(2)}) collective-permute-start(f32[4,256]{1,0:T(4,128)S(1)} %slice.50), channel_id=1, source_target_pairs={{0,4},{1,5},{2,6},{3,7},{4,8},{5,9},{6,10},{7,11},{8,12},{9,13},{1... | collective-permute-start | bytes 12296
  894.9 25.8 %collective-permute-start.2 = (f32[40,1024]{1,0:T(8,128)S(1)}, f32[40,1024]{1,0:T(8,128)S(1)}, u32[]{:S(2)}, u32[]{:S(2)}) collective-permute-start(f32[40,1024]{1,0:T(8,128)S(1)} %get-tuple-element.352), channel_id=1, source_target_pairs={{0,3},{1,4},{2,5},{3,6},{4,7},{5,8},{6,9},{7,10},{8,11},{9,12},{10... | collective-permute-start | bytes 491528
  899.1 21.6 %collective-permute-start.1 = (f32[40,1024]{1,0:T(8,128)S(1)}, f32[40,1024]{1,0:T(8,128)S(1)}, u32[]{:S(2)}, u32[]{:S(2)}) collective-permute-start(f32[40,1024]{1,0:T(8,128)S(1)} %get-tuple-element.352), channel_id=1, source_target_pairs={{0,2},{1,3},{2,4},{3,5},{4,6},{5,7},{6,8},{7,9},{8,10},{9,11},{10,... | collective-permute-start | bytes 491528
  901.8 20.3 %collective-permute-start = (f32[40,1024]{1,0:T(8,128)S(1)}, f32[40,1024]{1,0:T(8,128)}, u32[]{:S(2)}, u32[]{:S(2)}) collective-permute-start(f32[40,1024]{1,0:T(8,128)S(1)} %get-tuple-element.352), channel_id=1, source_target_pairs={{0,1},{1,2},{2,3},{3,4},{4,5},{5,6},{6,7},{7,8},{8,9},{9,10},{10,1... | collective-permute-start | bytes 491528
  908.3 9.9 %collective-permute-start.9 = (f32[40,256]{1,0:T(8,128)S(1)}, f32[40,256]{1,0:T(8,128)S(1)}, u32[]{:S(2)}, u32[]{:S(2)}) collective-permute-start(f32[40,256]{1,0:T(8,128)S(1)} %get-tuple-element.354), channel_id=1, source_target_pairs={{0,2},{1,3},{2,4},{3,5},{4,6},{5,7},{6,8},{7,9},{8,10},{9,11},{10,... | collective-permute-start | bytes 122888
  912.2 7.3 collective-permute-start.8
  918.2 2.5 collective-permute-start.3
  (38 other events, 131.5 us)
Sparse Core Ops, SparseCore 0:
  14.2 60.8 all-gather.4
  78.6 55.3 all-gather.6
  153.5 42.2 all-gather.8
  210.9 28.2 reduce-scatter.14
  244.3 29.1 all-gather.10
  290.4 28.2 reduce-scatter.16
  355.5 89.0 reduce-scatter.18
  448.5 51.0 reduce-scatter.24
  503.4 51.0 reduce-scatter.26
  558.2 51.0 reduce-scatter.28
  611.6 21.6 reduce-scatter.20
  640.1 119.5 reduce-scatter.22
where the time goes:
time: 944 us; the launch traced here: 933 us
  waiting for transfers between devices  473 us (50%)
  blocking collectives  244 us (26%)
  matrix products  74.9 us (8%)
  starting transfers between devices  52.8 us (6%)
  local copies, waits for them, and re-layouts  41 us (4%)
  other arithmetic  31.1 us (3%)
  between operations  15.6 us (2%)
    unnamed x2, blocking collectives  233 us
    reduce_scatter x1, waiting for transfers between devices, local(): lax.psum_scatter(key_terms.reshape(total // group, group, 2 * width).asty...  68 us
    all_gather x1, waiting for transfers between devices, local(): lax.all_gather(values_local, ('seq', 'head'), axis=0, tiled=True)  57 us
    reduce_scatter x1, waiting for transfers between devices, local(): lax.psum_scatter(d_w_up.astype(jnp.bfloat16), 'seq', scatter_dimension=0,...  52.9 us
    reduce_scatter x1, waiting for transfers between devices, local(): lax.psum_scatter(d_w_down.astype(jnp.bfloat16), 'seq', scatter_dimension=...  52.7 us
    all_gather x1, waiting for transfers between devices, local(): ffn_rows = lax.all_gather(ffn_in, 'head', axis=0, tiled=True)  41.8 us
    unnamed x12, starting transfers between devices  37.1 us
    all_gather x1, waiting for transfers between devices, local(): lax.all_gather(keys_local, ('seq', 'head'), axis=0, tiled=True)  35.2 us
  transfers between devices with their start and end apart: 27, of which 14 were waited for; matrix products, arithmetic and copies ran while one was open for 28% of the time, Pallas kernels for 0%

commit v1 on v0

v1 whole, which is shorter than its diff:
```python
import functools
import math

import jax
import jax.numpy as jnp
from jax import lax
from jax.experimental import pallas as pl
from jax.experimental.pallas import tpu as pltpu
from jax.sharding import PartitionSpec as P

EPS = 1e-06
MESH = pl.DeviceIdType.MESH
VMEM = pltpu.VMEM
LIMIT = 56 * 2**20


def norm_rows(v, gain):
    return v * lax.rsqrt(jnp.mean(v * v, axis=-1, keepdims=True) + EPS) * gain


def rotate(v, cosines, sines):
    half = v.shape[-1] // 2
    first = v[..., :half]
    second = v[..., half:]
    return jnp.concatenate(
        [first * cosines - second * sines, second * cosines + first * sines], axis=-1
    )


def rope_tables(positions, width):
    half = width // 2
    freq = jnp.exp(jnp.arange(half, dtype=jnp.float32) * (-2.0 * math.log(1000000.0) / width))
    angle = positions.astype(jnp.float32)[:, None] * freq[None, :]
    return (jnp.cos(angle), jnp.sin(angle))


def contract_first(left, right):
    return lax.dot_general(
        left, right, (((0,), (0,)), ((), ())), preferred_element_type=jnp.float32
    )


def contract_last(left, right):
    return lax.dot_general(
        left, right, (((1,), (1,)), ((), ())), preferred_element_type=jnp.float32
    )


def place():
    return lax.axis_index("seq"), lax.axis_index("head")


def related(s, mask):
    out = s
    bit = 0
    while mask >> bit:
        if (mask >> bit) & 1:
            step = 1 << bit
            out = out + (1 - 2 * ((s // step) % 2)) * step
        bit += 1
    return out


def subsets(bits):
    out = [0]
    for bit in bits:
        out = out + [m | (1 << bit) for m in out]
    return out


def greet(targets):
    barrier = pltpu.get_barrier_semaphore()
    for target in targets:
        pl.semaphore_signal(barrier, inc=1, device_id=target, device_id_type=MESH)
    pl.semaphore_wait(barrier, len(targets))


def remote(src, dst, send, recv, target):
    return pltpu.make_async_remote_copy(
        src_ref=src,
        dst_ref=dst,
        send_sem=send,
        recv_sem=recv,
        device_id=target,
        device_id_type=MESH,
    )


def seq_orders(bits):
    upper = list(range(1, bits))
    return upper, upper[::-1]


def gather_kernel(nseq, heads, local_refs, out_refs, send, recv):
    bits = nseq.bit_length() - 1
    s, h = place()
    others = [lax.rem(h + d, heads) for d in range(1, heads)]
    greet([(related(s, 1 << b), h) for b in range(bits)] + [(s, o) for o in others])
    count = [0]
    started = []

    def go(src, dst, target):
        k = count[0]
        count[0] += 1
        copy = remote(src, dst, send.at[k], recv.at[k], target)
        copy.start()
        started.append(copy)
        return copy

    first = []
    for a in range(len(out_refs)):
        out_refs[a][s, h] = local_refs[a][...]
        first.append(
            [go(local_refs[a], out_refs[a].at[s, h], (s, o)) for o in others]
        )
    orders = [o + [0] for o in seq_orders(bits)]
    held = [{0: first[a]} for a in range(len(out_refs))]
    for stage in range(bits):
        for a in range(len(out_refs)):
            bit = orders[a % 2][stage]
            target = (related(s, 1 << bit), h)
            arrived = {}
            for mask in list(held[a]):
                for copy in held[a][mask]:
                    copy.wait_recv()
                held[a][mask] = []
                group = related(s, mask)
                copy = go(out_refs[a].at[group], out_refs[a].at[group], target)
                arrived[mask | (1 << bit)] = [copy]
            held[a].update(arrived)
    for a in range(len(out_refs)):
        for mask in held[a]:
            for copy in held[a][mask]:
                copy.wait_recv()
    for copy in started:
        copy.wait_send()


def gather_all(arrays, nseq, heads, cid):
    n = len(arrays)
    total = n * (heads - 1 + nseq - 1)

    def kernel(*refs):
        gather_kernel(nseq, heads, refs[:n], refs[n : 2 * n], refs[2 * n], refs[2 * n + 1])

    return pl.pallas_call(
        kernel,
        out_shape=[jax.ShapeDtypeStruct((nseq, heads) + a.shape, a.dtype) for a in arrays],
        in_specs=[pl.BlockSpec(memory_space=VMEM)] * n,
        out_specs=[pl.BlockSpec(memory_space=VMEM)] * n,
        scratch_shapes=[pltpu.SemaphoreType.DMA((total,)), pltpu.SemaphoreType.DMA((total,))],
        name="gather_all",
        compiler_params=pltpu.CompilerParams(
            collective_id=cid, has_side_effects=True, vmem_limit_bytes=LIMIT
        ),
    )(*arrays)


def line_gather_kernel(heads, x_ref, out_ref, send, recv):
    s, h = place()
    right = (s, lax.rem(h + 1, heads))
    left = (s, lax.rem(h + heads - 1, heads))
    greet([right, left])
    out_ref[h] = x_ref[...]
    for step in range(heads - 1):
        to_right = remote(
            out_ref.at[jnp.maximum(h - step, 0)],
            out_ref.at[jnp.maximum(h - step, 0)],
            send.at[0, step],
            recv.at[0, step],
            right,
        )
        to_left = remote(
            out_ref.at[jnp.minimum(h + step, heads - 1)],
            out_ref.at[jnp.minimum(h + step, heads - 1)],
            send.at[1, step],
            recv.at[1, step],
            left,
        )
        pl.when((h - step >= 0) & (h < heads - 1))(to_right.start)
        pl.when((h + step <= heads - 1) & (h > 0))(to_left.start)
        pl.when(h - 1 - step >= 0)(
            remote(
                out_ref.at[jnp.maximum(h - 1 - step, 0)],
                out_ref.at[jnp.maximum(h - 1 - step, 0)],
                send.at[0, step],
                recv.at[0, step],
                right,
            ).wait_recv
        )
        pl.when(h + 1 + step <= heads - 1)(
            remote(
                out_ref.at[jnp.minimum(h + 1 + step, heads - 1)],
                out_ref.at[jnp.minimum(h + 1 + step, heads - 1)],
                send.at[1, step],
                recv.at[1, step],
                left,
            ).wait_recv
        )
        pl.when((h - step >= 0) & (h < heads - 1))(to_right.wait_send)
        pl.when((h + step <= heads - 1) & (h > 0))(to_left.wait_send)


def line_gather(x, heads, cid):
    return pl.pallas_call(
        functools.partial(line_gather_kernel, heads),
        out_shape=jax.ShapeDtypeStruct((heads,) + x.shape, x.dtype),
        in_specs=[pl.BlockSpec(memory_space=VMEM)],
        out_specs=pl.BlockSpec(memory_space=VMEM),
        scratch_shapes=[
            pltpu.SemaphoreType.DMA((2, heads - 1)),
            pltpu.SemaphoreType.DMA((2, heads - 1)),
        ],
        name="line_gather",
        compiler_params=pltpu.CompilerParams(
            collective_id=cid, has_side_effects=True, vmem_limit_bytes=LIMIT
        ),
    )(x)


def line_scatter_kernel(heads, parts, out_ref, from_left, from_right, send, recv):
    s, h = place()
    last = heads - 1
    right = (s, lax.rem(h + 1, heads))
    left = (s, lax.rem(h + heads - 1, heads))
    greet([right, left])
    f32 = jnp.float32
    for step in range(heads - 1):
        r_dest = jnp.clip(last - (step - h), 0, last)
        l_dest = jnp.clip(step - (last - h), 0, last)
        r_on = (step >= h) & (h < last)
        l_on = (step >= last - h) & (h > 0)
        for on, dest, box, lane, target, first in (
            (r_on, r_dest, from_left, 0, right, step == h),
            (l_on, l_dest, from_right, 1, left, step == last - h),
        ):
            at_end = (h == 0) if lane == 0 else (h == last)
            if step > 0:

                def add(box=box, dest=dest):
                    box[step - 1] = (
                        box[step - 1].astype(f32) + parts[dest].astype(f32)
                    ).astype(box.dtype)

                pl.when(on & jnp.logical_not(at_end))(add)
                pl.when(on & jnp.logical_not(at_end))(
                    remote(
                        box.at[step - 1], box.at[step], send.at[lane, step], recv.at[lane, step], target
                    ).start
                )
            pl.when(on & at_end)(
                remote(
                    parts.at[dest], box.at[step], send.at[lane, step], recv.at[lane, step], target
                ).start
            )
        r_in = (step >= h - 1) & (h > 0)
        l_in = (step >= last - h - 1) & (h < last)
        pl.when(r_in)(
            remote(
                from_left.at[step], from_left.at[step], send.at[0, step], recv.at[0, step], right
            ).wait_recv
        )
        pl.when(l_in)(
            remote(
                from_right.at[step], from_right.at[step], send.at[1, step], recv.at[1, step], left
            ).wait_recv
        )
    for step in range(heads - 1):
        for on, box, lane, target in (
            ((step >= h) & (h < last), from_left, 0, right),
            ((step >= last - h) & (h > 0), from_right, 1, left),
        ):
            pl.when(on)(
                remote(
                    box.at[step], box.at[step], send.at[lane, step], recv.at[lane, step], target
                ).wait_send
            )
    out_ref[...] = parts[h].astype(f32)

    def add_left():
        out_ref[...] += from_left[heads - 2].astype(f32)

    def add_right():
        out_ref[...] += from_right[heads - 2].astype(f32)

    pl.when(h > 0)(add_left)
    pl.when(h < last)(add_right)


def line_scatter(parts, heads, cid):
    block = parts.shape[1:]
    return pl.pallas_call(
        functools.partial(line_scatter_kernel, heads),
        out_shape=jax.ShapeDtypeStruct(block, jnp.float32),
        in_specs=[pl.BlockSpec(memory_space=VMEM)],
        out_specs=pl.BlockSpec(memory_space=VMEM),
        scratch_shapes=[
            VMEM((heads - 1,) + block, parts.dtype),
            VMEM((heads - 1,) + block, parts.dtype),
            pltpu.SemaphoreType.DMA((2, heads - 1)),
            pltpu.SemaphoreType.DMA((2, heads - 1)),
        ],
        name="line_scatter",
        compiler_params=pltpu.CompilerParams(
            collective_id=cid, has_side_effects=True, vmem_limit_bytes=LIMIT
        ),
    )(parts)


def scatter_kernel(nseq, heads, zs, orders, parts, outs, boxes, zboxes, send, recv):
    bits = nseq.bit_length() - 1
    s, h = place()
    f32 = jnp.float32
    others = [lax.rem(h + d, heads) for d in range(1, heads)]
    greet(
        [(related(s, 1 << b), h) for b in range(bits)]
        + ([(s, o) for o in others] if any(zs) else [])
    )
    count = [0]
    started = []

    def go(src, dst, target):
        k = count[0]
        count[0] += 1
        copy = remote(src, dst, send.at[k], recv.at[k], target)
        copy.start()
        started.append(copy)
        return copy

    n = len(parts)
    offsets = [0] * n
    slot = [{} for _ in range(n)]
    waiting = [{} for _ in range(n)]

    def current(a, mask):
        if mask in slot[a]:
            return boxes[a].at[slot[a][mask]]
        return parts[a].at[related(s, mask)]

    def launch(a, stage):
        bit = orders[a][stage]
        rest = orders[a][stage + 1 :]
        target = (related(s, 1 << bit), h)
        after = 1 << rest[0] if rest else 0
        masks = sorted(subsets(rest), key=lambda m: 0 if m & after else 1)
        for mask in masks:
            where = offsets[a]
            offsets[a] += 1
            waiting[a][mask] = (
                go(current(a, mask | (1 << bit)), boxes[a].at[where], target),
                where,
            )

    def settle(a, mask):
        copy, where = waiting[a].pop(mask)
        mine = current(a, mask)
        copy.wait_recv()
        boxes[a][where] = (boxes[a][where].astype(f32) + mine[...].astype(f32)).astype(
            boxes[a].dtype
        )
        slot[a][mask] = where

    for a in range(n):
        launch(a, 0)
    for stage in range(bits):
        for a in range(n):
            for mask in list(waiting[a]):
                settle(a, mask)
            if stage + 1 < bits:
                launch(a, stage + 1)
    arriving = []
    for a in range(n):
        if not zs[a]:
            continue
        mine = current(a, 0)
        arriving.append(
            [
                go(mine.at[o], zboxes[a].at[d], (s, o))
                for d, o in enumerate(others)
            ]
        )
    z = 0
    for a in range(n):
        if zs[a]:
            total = current(a, 0)[h].astype(f32)
            for d, copy in enumerate(arriving[z]):
                copy.wait_recv()
                total = total + zboxes[a][d].astype(f32)
            outs[a][...] = total
            z += 1
        else:
            outs[a][...] = current(a, 0)[...].astype(f32)
    for copy in started:
        copy.wait_send()


def scatter_all(arrays, zs, orders, nseq, heads, cid, name):
    n = len(arrays)
    total = sum((nseq - 1) + (heads - 1 if z else 0) for z in zs)
    blocks = [a.shape[2:] if z else a.shape[1:] for a, z in zip(arrays, zs)]

    def kernel(*refs):
        scatter_kernel(
            nseq,
            heads,
            zs,
            orders,
            refs[:n],
            refs[n : 2 * n],
            refs[2 * n : 3 * n],
            refs[3 * n : 4 * n],
            refs[4 * n],
            refs[4 * n + 1],
        )

    return pl.pallas_call(
        kernel,
        out_shape=[jax.ShapeDtypeStruct(b, jnp.float32) for b in blocks],
        in_specs=[pl.BlockSpec(memory_space=VMEM)] * n,
        out_specs=[pl.BlockSpec(memory_space=VMEM)] * n,
        scratch_shapes=[VMEM((nseq - 1,) + a.shape[1:], a.dtype) for a in arrays]
        + [
            VMEM((heads - 1,) + b, a.dtype) if z else VMEM((8, 128), jnp.float32)
            for a, b, z in zip(arrays, blocks, zs)
        ]
        + [pltpu.SemaphoreType.DMA((total,)), pltpu.SemaphoreType.DMA((total,))],
        name=name,
        compiler_params=pltpu.CompilerParams(
            collective_id=cid, has_side_effects=True, vmem_limit_bytes=LIMIT
        ),
    )(*arrays)


def attend_kernel(q_ref, k_ref, v_ref, start_ref, index_ref, out_ref, log_ref):
    s = lax.axis_index("seq")
    span = k_ref.shape[1]
    start = start_ref[...]
    index = index_ref[...]
    queries = q_ref[...]
    rows = queries.shape[0]
    out_ref[...] = jnp.zeros_like(out_ref)

    def step(g, mass):
        scores = contract_last(k_ref[g], queries)
        key = g * span + lax.broadcasted_iota(jnp.int32, (span, rows), 0)
        terms = jnp.where((key >= start) & (key <= index), jnp.exp(scores), 0.0)
        out_ref[...] += contract_first(v_ref[g], terms.astype(jnp.bfloat16))
        return mass + jnp.sum(terms, axis=0, keepdims=True)

    mass = lax.fori_loop(0, s + 1, step, jnp.zeros((1, rows), jnp.float32))
    out_ref[...] = out_ref[...] / mass
    log_ref[...] = jnp.log(mass)


def attend(q, k, v, start, index):
    rows, width = q.shape
    return pl.pallas_call(
        attend_kernel,
        out_shape=[
            jax.ShapeDtypeStruct((width, rows), jnp.float32),
            jax.ShapeDtypeStruct((1, rows), jnp.float32),
        ],
        in_specs=[pl.BlockSpec(memory_space=VMEM)] * 5,
        out_specs=[pl.BlockSpec(memory_space=VMEM)] * 2,
        name="attend",
        compiler_params=pltpu.CompilerParams(vmem_limit_bytes=LIMIT),
    )(q, k, v, start, index)


def attend_back_kernel(
    q_ref, k_ref, v_ref, start_ref, index_ref, log_ref, dots_ref, d_ref, dq_ref, dk_ref, dv_ref
):
    s = lax.axis_index("seq")
    groups, span = k_ref.shape[:2]
    start = start_ref[...]
    index = index_ref[...]
    log_total = log_ref[...]
    dots = dots_ref[...]
    queries = q_ref[...]
    grads = d_ref[...]
    rows = queries.shape[0]
    dq_ref[...] = jnp.zeros_like(dq_ref)

    def step(g, carry):
        keys = k_ref[g]
        scores = contract_last(keys, queries)
        key = g * span + lax.broadcasted_iota(jnp.int32, (span, rows), 0)
        probs = jnp.where((key >= start) & (key <= index), jnp.exp(scores - log_total), 0.0)
        d_probs = contract_last(v_ref[g], grads)
        d_scores = (probs * (d_probs - dots)).astype(jnp.bfloat16)
        dv_ref[g] = jnp.dot(
            probs.astype(jnp.bfloat16), grads, preferred_element_type=jnp.float32
        ).astype(dv_ref.dtype)
        dk_ref[g] = jnp.dot(d_scores, queries, preferred_element_type=jnp.float32).astype(
            dk_ref.dtype
        )
        dq_ref[...] += contract_first(keys, d_scores)
        return carry

    lax.fori_loop(0, s + 1, step, 0)

    def blank(g, carry):
        dk_ref[g] = jnp.zeros(dk_ref.shape[1:], dk_ref.dtype)
        dv_ref[g] = jnp.zeros(dv_ref.shape[1:], dv_ref.dtype)
        return carry

    lax.fori_loop(s + 1, groups, blank, 0)


def attend_back(q, k, v, start, index, log_total, dots, grads):
    rows, width = q.shape
    return pl.pallas_call(
        attend_back_kernel,
        out_shape=[
            jax.ShapeDtypeStruct((width, rows), jnp.float32),
            jax.ShapeDtypeStruct(k.shape, jnp.bfloat16),
            jax.ShapeDtypeStruct(v.shape, jnp.bfloat16),
        ],
        in_specs=[pl.BlockSpec(memory_space=VMEM)] * 8,
        out_specs=[pl.BlockSpec(memory_space=VMEM)] * 3,
        name="attend_back",
        compiler_params=pltpu.CompilerParams(vmem_limit_bytes=LIMIT),
    )(q, k, v, start, index, log_total, dots, grads)


def local(
    tokens,
    segment_ids,
    w_query,
    w_key,
    w_value,
    w_out,
    w_gate,
    w_up,
    w_down,
    gain_attn_in,
    gain_attn_out,
    gain_ffn_in,
    gain_ffn_out,
    gain_query,
    gain_key,
    cotangent,
):
    heads = lax.axis_size("head")
    nseq = lax.axis_size("seq")
    head_index = lax.axis_index("head")
    seq_index = lax.axis_index("seq")
    bits = nseq.bit_length() - 1
    local_rows, model = tokens.shape
    width = gain_query.shape[0]
    qcount = w_query.shape[1] // width
    group = local_rows * heads
    total = segment_ids.shape[0]
    hidden_units = w_gate.shape[1]
    scale = 1.0 / math.sqrt(width)
    bf16 = jnp.bfloat16
    first_row = (seq_index * heads + head_index) * local_rows
    my_index = first_row + jnp.arange(local_rows, dtype=jnp.int32)
    my_ids = lax.dynamic_slice_in_dim(segment_ids, first_row, local_rows)
    my_starts = jnp.min(
        jnp.where(
            my_ids[:, None] == segment_ids[None, :],
            jnp.arange(total, dtype=jnp.int32)[None, :],
            total,
        ),
        axis=1,
    )
    cosines, sines = rope_tables(my_index - my_starts, width)

    def query_path(linear, gain):
        shaped = linear.reshape(local_rows, qcount, width)
        turned = rotate(norm_rows(shaped, gain), cosines[:, None, :], sines[:, None, :])
        return turned.reshape(local_rows, qcount * width)

    def key_path(linear, gain):
        return rotate(norm_rows(linear, gain), cosines, sines)

    def gated(gate, up):
        return jax.nn.gelu(gate, approximate=True) * up

    def stacked(v):
        return v.reshape(local_rows, qcount, width).transpose(1, 0, 2).reshape(-1, width)

    def unstacked(v):
        return v.reshape(qcount, local_rows, width).transpose(1, 0, 2).reshape(local_rows, -1)

    inputs = tokens.astype(jnp.float32)
    attn_in = norm_rows(inputs, gain_attn_in).astype(bf16)
    k_linear = jnp.dot(attn_in, w_key, preferred_element_type=jnp.float32)
    keys_local = key_path(k_linear, gain_key).astype(bf16)
    values_local = jnp.dot(attn_in, w_value, preferred_element_type=jnp.float32).astype(bf16)
    q_linear = jnp.dot(attn_in, w_query, preferred_element_type=jnp.float32)
    queries_local = query_path(q_linear, gain_query).astype(bf16)
    queries = stacked(queries_local) * jnp.asarray(scale, bf16)
    keys, values = gather_all([keys_local, values_local], nseq, heads, 1)
    keys = keys.reshape(nseq, group, width)
    values = values.reshape(nseq, group, width)
    starts = jnp.tile(my_starts, qcount)[None, :]
    index = jnp.tile(my_index, qcount)[None, :]
    attended_t, log_total = attend(queries, keys, values, starts, index)
    attended = attended_t.T
    mixed_local = unstacked(attended.astype(bf16))
    projected = jnp.dot(mixed_local, w_out, preferred_element_type=jnp.float32)
    hidden = inputs + norm_rows(projected, gain_attn_out)
    ffn_in = norm_rows(hidden, gain_ffn_in).astype(bf16)
    ffn_rows = line_gather(ffn_in, heads, 2).reshape(group, model)
    gate = jnp.dot(ffn_rows, w_gate, preferred_element_type=jnp.float32)
    up = jnp.dot(ffn_rows, w_up, preferred_element_type=jnp.float32)
    activated = gated(gate, up).astype(bf16)
    ffn_out = line_scatter(
        jnp.dot(activated, w_down, preferred_element_type=jnp.float32)
        .astype(bf16)
        .reshape(heads, local_rows, model),
        heads,
        3,
    )
    output = hidden + norm_rows(ffn_out, gain_ffn_out)
    upstream = cotangent.astype(jnp.float32)
    unused, back_four = jax.vjp(norm_rows, ffn_out, gain_ffn_out)
    d_ffn_out, d_gain_four = back_four(upstream)
    d_ffn_rows = line_gather(d_ffn_out.astype(bf16), heads, 4).reshape(group, model)
    d_activated = contract_last(d_ffn_rows, w_down)
    d_w_down = contract_first(d_ffn_rows, activated)
    unused, back_gate = jax.vjp(gated, gate, up)
    d_gate, d_up = back_gate(d_activated)
    d_gate = d_gate.astype(bf16)
    d_up = d_up.astype(bf16)
    d_ffn_in = line_scatter(
        (contract_last(d_gate, w_gate) + contract_last(d_up, w_up))
        .astype(bf16)
        .reshape(heads, local_rows, model),
        heads,
        5,
    )
    d_w_gate = contract_first(ffn_rows, d_gate)
    d_w_up = contract_first(ffn_rows, d_up)
    unused, back_three = jax.vjp(norm_rows, hidden, gain_ffn_in)
    d_hidden_part, d_gain_three = back_three(d_ffn_in)
    d_hidden = upstream + d_hidden_part
    unused, back_two = jax.vjp(norm_rows, projected, gain_attn_out)
    d_projected, d_gain_two = back_two(d_hidden)
    d_projected = d_projected.astype(bf16)
    d_w_out = contract_first(mixed_local, d_projected)
    d_mixed = contract_last(d_projected, w_out).astype(bf16)
    grad_attended = stacked(d_mixed)
    row_dots = jnp.sum(grad_attended.astype(jnp.float32) * attended, axis=1)[None, :]
    d_queries_t, d_keys, d_values = attend_back(
        queries, keys, values, starts, index, log_total, row_dots, grad_attended
    )
    shape = (nseq, heads, local_rows, width)
    ups, downs = seq_orders(bits)
    d_keys, d_values = scatter_all(
        [d_keys.reshape(shape), d_values.reshape(shape)],
        [True, True],
        [[0] + ups, [0] + downs],
        nseq,
        heads,
        6,
        "scatter_keys",
    )
    d_query_rot = unstacked((d_queries_t.T * scale).astype(bf16)).astype(jnp.float32)
    unused, back_query = jax.vjp(query_path, q_linear, gain_query)
    d_q_linear, d_gain_query = back_query(d_query_rot)
    unused, back_key = jax.vjp(key_path, k_linear, gain_key)
    d_k_linear, d_gain_key = back_key(d_keys)
    d_qkv = jnp.concatenate([d_q_linear, d_k_linear, d_values], axis=1).astype(bf16)
    qw = qcount * width
    d_w_qkv = contract_first(attn_in, d_qkv)
    d_attn_in = (
        contract_last(d_qkv[:, :qw], w_query)
        + contract_last(d_qkv[:, qw : qw + width], w_key)
        + contract_last(d_qkv[:, qw + width :], w_value)
    )
    unused, back_one = jax.vjp(norm_rows, inputs, gain_attn_in)
    d_inputs, d_gain_one = back_one(d_attn_in)
    grad_tokens = (d_hidden + d_inputs).astype(bf16)

    def cut(v):
        return v.reshape(nseq, heads, -1)

    wide = jnp.stack([cut(d_gain_one), cut(d_gain_two), cut(d_gain_three), cut(d_gain_four)], 2)
    narrow = jnp.stack([cut(d_gain_query), cut(d_gain_key)], 2)
    each, few = wide.shape[-1], narrow.shape[-1]
    gains = jnp.concatenate(
        [
            jnp.pad(wide, ((0, 0), (0, 0), (0, 0), (0, 128 - each))),
            jnp.pad(narrow, ((0, 0), (0, 0), (0, 2), (0, 128 - few))),
        ],
        axis=2,
    )
    sum_qkv, sum_out, sum_gains = scatter_all(
        [
            d_w_qkv.astype(bf16).reshape(nseq, heads, -1, d_qkv.shape[1]),
            d_w_out.astype(bf16).reshape(nseq, heads, -1, model),
            gains,
        ],
        [True, True, True],
        [[0] + ups, [0] + downs, [0] + downs],
        nseq,
        heads,
        7,
        "scatter_attn",
    )
    sum_gate, sum_up, sum_down = scatter_all(
        [
            d.astype(bf16).reshape(nseq, model // nseq, hidden_units)
            for d in (d_w_gate, d_w_up, d_w_down)
        ],
        [False, False, False],
        [[0] + ups, [0] + downs, [0] + ups],
        nseq,
        heads,
        8,
        "scatter_ffn",
    )
    return (
        output.astype(bf16),
        grad_tokens,
        sum_qkv[:, :qw],
        sum_qkv[:, qw : qw + width],
        sum_qkv[:, qw + width :],
        sum_out,
        sum_gate,
        sum_up,
        sum_down.T,
        sum_gains[0, :each],
        sum_gains[1, :each],
        sum_gains[2, :each],
        sum_gains[3, :each],
        sum_gains[4, :few],
        sum_gains[5, :few],
    )


def solution(mesh):
    rows = P(("seq", "head"), None)
    in_specs = (
        rows,
        P(),
        P(),
        P(),
        P(),
        P(),
        P(None, "head"),
        P(None, "head"),
        P("head", None),
        P(),
        P(),
        P(),
        P(),
        P(),
        P(),
        rows,
    )
    out_specs = (
        rows,
        rows,
        rows,
        rows,
        rows,
        rows,
        P("seq", "head"),
        P("seq", "head"),
        P("head", "seq"),
    ) + (P(("seq", "head")),) * 6
    return jax.shard_map(local, mesh=mesh, in_specs=in_specs, out_specs=out_specs, check_vma=False)
```

time: 944 us -> 476 us (0.50)
  waiting for transfers between devices: 473 us -> 0 us
  Pallas kernels: 0 us -> 340 us
  blocking collectives: 244 us -> 0 us
  starting transfers between devices: 52.8 us -> 0 us
  matrix products: 74.9 us -> 58 us
  between operations: 15.6 us -> 1.98 us
    pallas_call x0 -> x10, Pallas kernels: none -> 340 us  [the longest x3 184 us: scatter_all(): pl.pallas_call(kernel, out_shape=[jax.ShapeDtypeStruct(b, jnp.float32) fo...]
    reduce_scatter x8 -> x0, waiting for transfers between devices: 286 us -> none  [the longest x1 68 us: local(): lax.psum_scatter(key_terms.reshape(total // group, group, 2 * width).asty...]
    unnamed x2 -> x0, blocking collectives: 233 us -> none
    all_gather x4 -> x0, waiting for transfers between devices: 163 us -> none  [the longest x1 57 us: local(): lax.all_gather(values_local, ('seq', 'head'), axis=0, tiled=True)]
    unnamed x12 -> x0, starting transfers between devices: 37.1 us -> none
    all_to_all x3 -> x0, waiting for transfers between devices: 24.1 us -> none  [the longest x1 9.39 us: local(): lax.all_to_all(queries_local, 'head', split_axis=1, concat_axis=0, tiled=...]
    unnamed x165 -> x134, local copies, waits for them, and re-layouts: 24.4 us -> 7.07 us
    all_to_all x3 -> x0, starting transfers between devices: 14.3 us -> none  [the longest x1 6.32 us: local(): lax.all_to_all(queries_local, 'head', split_axis=1, concat_axis=0, tiled=...]
  transfers between devices with their start and end apart: 27 -> 0, of which waited for: 14 -> 0; matrix products, arithmetic and copies ran while one was open for 28% -> 0% of each run, Pallas kernels for 0% -> 0%
where the time goes in v1:
time: 476 us; the launch traced here: 471 us
  Pallas kernels  340 us (71%)
  matrix products  58 us (12%)
  local copies, waits for them, and re-layouts  45.5 us (10%)
  other arithmetic  25.2 us (5%)
    pallas_call x3, Pallas kernels, scatter_all(): pl.pallas_call(kernel, out_shape=[jax.ShapeDtypeStruct(b, jnp.float32) fo...  184 us
    pallas_call x2, Pallas kernels, line_gather(): pl.pallas_call(functools.partial(line_gather_kernel, heads), out_shape=ja...  54.3 us
    pallas_call x2, Pallas kernels, line_scatter(): pl.pallas_call(functools.partial(line_scatter_kernel, heads), out_shape=j...  52.3 us
    pallas_call x1, Pallas kernels, gather_all(): pl.pallas_call(kernel, out_shape=[jax.ShapeDtypeStruct((nseq, heads) + a....  39.7 us
    convert_element_type x3, local copies, waits for them, and re-layouts, local(): d.astype(bf16).reshape(nseq, model // nseq, hidden_units)  19.7 us
    dot_general x7, matrix products, contract_last(): lax.dot_general(left, right, (((1,), (1,)), ((), ())), preferred_element_...  19.1 us
    dot_general x5, matrix products, contract_first(): lax.dot_general(left, right, (((0,), (0,)), ((), ())), preferred_element_...  18.7 us
    reduce_sum x9, other arithmetic, norm_rows(): return v * lax.rsqrt(jnp.mean(v * v, axis=-1, keepdims=True) + EPS) * gain  11.4 us

profile of v1, /device:TPU:0, one launch (start us, length us, event | category | flops | bytes accessed | tf_op | source)
XLA Modules:
  0.0 470.7 jit_solution(15300916387437436998)
XLA Ops:
  0.7 1.3 fusion.20
  2.0 2.4 fusion.56
  4.4 1.0 reshape.292
  5.4 1.2 copy.111
  6.7 1.4 multiply_reduce_fusion.9
  8.2 0.9 multiply_multiply_fusion.3
  9.2 1.4 multiply_reduce_fusion.12
  12.5 1.1 subtract_convert_fusion
  13.8 0.9 copy.114
  15.3 2.0 convolution_convert_fusion.7.refs_1_
  17.3 39.7 %gather_all.1 = (bf16[8,4,128,256]{3,2,1,0:T(8,128)(2,1)}, bf16[8,4,128,256]{3,2,1,0:T(8,128)(2,1)}) custom-call(bf16[128,256]{1,0:T(8,128)(2,1)} %pad_maximum_fusion.1.refs_0_, bf16[128,256]{1,0:T(8,128)(2,1)} %convolution_convert_fusion.7.refs_1_), custom_call_target="tpu_custom_call" | custom-call | tf_op jit(solution)/shard_map/gather_all/pallas_call | solution.py:146
  58.1 4.1 attend.1
  62.3 1.2 copy.115
  63.5 0.8 bitcast_convert_fusion
  64.4 1.1 copy.116
  66.4 0.8 multiply_convert_fusion.2.x_ref
  67.3 29.1 %line_gather.2 = bf16[4,128,1152]{2,1,0:T(8,128)(2,1)} custom-call(bf16[128,1152]{1,0:T(8,128)(2,1)} %multiply_convert_fusion.2.x_ref), custom_call_target="tpu_custom_call" | custom-call | tf_op jit(solution)/shard_map/line_gather/pallas_call | solution.py:205
  96.4 5.1 %fusion.59 = f32[512,1728]{0,1:T(8,128)S(1)} fusion(bf16[512,1152]{1,0:T(8,128)(2,1)} %bitcast.109, bf16[1152,1728]{0,1:T(8,128)(2,1)} %param.22), kind=kOutput, calls=%fused_computation.148 | convolution fusion | flops 2038431744 | bytes 8699904 | tf_op jit(solution)/shard_map/dot_general | solution.py:607
  101.6 5.0 %multiply_convert_fusion.1 = (bf16[512,1728]{0,1:T(8,128)(2,1)S(1)}, f32[512,1728]{0,1:T(8,128)}) fusion(f32[512,1728]{0,1:T(8,128)S(1)} %fusion.59, bf16[512,1152]{1,0:T(8,128)(2,1)S(1)} %bitcast.110, bf16[1152,1728]{0,1:T(8,128)(2,1)S(1)} %copy-done.2), kind=kOutput, calls=%fused_computation.15 | convolution fusion | flops 2047279104 | bytes 14008320 | tf_op jit(solution)/shard_map/dot_general | solution.py:608
  106.7 3.6 convolution_convert_fusion.5
  110.3 27.0 %line_scatter.2 = f32[128,1152]{1,0:T(8,128)} custom-call(bf16[4,128,1152]{2,1,0:T(8,128)(2,1)} %bitcast.115), custom_call_target="tpu_custom_call" | custom-call | tf_op jit(solution)/shard_map/line_scatter/pallas_call | solution.py:292
  137.3 1.2 multiply_reduce_fusion.4
  138.5 1.9 fusion.15
  140.4 2.2 fusion.16
  142.5 25.2 %line_gather.3 = bf16[4,128,1152]{2,1,0:T(8,128)(2,1)} custom-call(bf16[128,1152]{1,0:T(8,128)(2,1)} %get-tuple-element.66.x_ref), custom_call_target="tpu_custom_call" | custom-call | tf_op jit(solution)/shard_map/line_gather/pallas_call | solution.py:205
  167.8 9.7 %multiply_convert_fusion = (bf16[512,1728]{0,1:T(8,128)(2,1)S(1)}, bf16[512,1728]{0,1:T(8,128)(2,1)S(1)}) fusion(f32[512,1728]{0,1:T(8,128)} %copy-done.64, f32[512,1728]{0,1:T(8,128)} %get-tuple-element.87, bf16[512,1152]{1,0:T(8,128)(2,1)} %bitcast.113, bf16[1728,1152]{1,0:T(8,128)(2,1)} %param.24), kind=kOutput, calls=%fused_computation.14 | convolution fusion | flops 2059665408 | bytes 15777792 | tf_op jit(solution)/shard_map/dot_general | solution.py:44
  177.5 2.7 fusion.60
  180.2 3.7 fusion.7
  183.8 25.3 %line_scatter.3 = f32[128,1152]{1,0:T(8,128)} custom-call(bf16[4,128,1152]{2,1,0:T(8,128)(2,1)} %bitcast.98), custom_call_target="tpu_custom_call" | custom-call | tf_op jit(solution)/shard_map/line_scatter/pallas_call | solution.py:292
  209.1 1.8 multiply_reduce_fusion
  210.9 2.1 multiply_reduce_fusion.1
  213.3 0.9 convolution_convert_fusion.6
  214.2 0.8 fusion.23
  215.0 5.9 %attend_back.1 = (f32[256,512]{1,0:T(8,128)}, bf16[8,512,256]{2,1,0:T(8,128)(2,1)}, bf16[8,512,256]{2,1,0:T(8,128)(2,1)}) custom-call(bf16[512,256]{1,0:T(8,128)(2,1)} %bitcast.100, bf16[8,512,256]{2,1,0:T(8,128)(2,1)} %bitcast.95, bf16[8,512,256]{2,1,0:T(8,128)(2,1)} %bitcast.97, s32[1,512]{1,0:T(1,128)} %bitcast.120, s32[1,512]{1,0:T(1,128)} %bitcast.122, ...), custom_call_target="tpu_custom_call" | custom-call | tf_op jit(solution)/shard_map/attend_back/pallas_call | solution.py:512
  221.0 1.1 bitcast_bitcast_fusion
  222.2 0.7 multiply_reduce_fusion.7
  223.2 0.9 fusion.61
  224.1 47.4 %scatter_keys.1 = (f32[128,256]{1,0:T(8,128)}, f32[128,256]{1,0:T(8,128)}) custom-call(bf16[8,4,128,256]{3,2,1,0:T(8,128)(2,1)} %bitcast.107, bf16[8,4,128,256]{3,2,1,0:T(8,128)(2,1)} %bitcast.108), custom_call_target="tpu_custom_call" | custom-call | tf_op jit(solution)/shard_map/scatter_keys/pallas_call | solution.py:416
  271.5 1.2 fusion.43
  273.9 0.9 slice.51
  274.9 1.0 fusion.13
  275.9 0.9 fusion.19
  276.8 0.7 copy.122
  277.5 0.7 copy.121
  278.3 2.3 convolution_convert_fusion.3
  280.6 2.8 reshape.306.refs_0_
  283.4 3.2 convolution_convert_fusion.4
  286.7 0.8 stack_reshape.23
  287.4 0.8 stack_reshape.22
  288.5 0.8 stack_reshape.19
  289.3 0.8 stack_reshape.18
  290.9 65.9 %scatter_attn.1 = (f32[36,1536]{1,0:T(8,128)}, f32[32,1152]{1,0:T(8,128)}, f32[8,128]{1,0:T(8,128)}) custom-call(bf16[8,4,36,1536]{3,2,1,0:T(8,128)(2,1)} %reshape.306.refs_0_, bf16[8,4,32,1152]{3,2,1,0:T(8,128)(2,1)} %bitcast.93, f32[8,4,8,128]{3,2,1,0:T(8,128)} %pad_maximum_fusion.refs_2_), custom_call_target="tpu_custom_call" | custom-call | tf_op jit(solution)/shard_map/scatter_attn/pallas_call | solution.py:416
  356.9 1.6 slice.52
  358.5 1.4 fusion.58
  359.9 4.5 convolution_convert_fusion.2
  364.4 6.5 %copy.123 = bf16[1152,1728]{1,0:T(8,128)(2,1)} copy(bf16[1152,1728]{0,1:T(8,128)(2,1)} %convolution_convert_fusion.2) | data formatting | bytes 7962624 | tf_op jit(solution)/shard_map/convert_element_type | solution.py:706
  370.9 4.4 convolution_convert_fusion.1
  375.3 6.6 %copy.124 = bf16[1152,1728]{1,0:T(8,128)(2,1)} copy(bf16[1152,1728]{0,1:T(8,128)(2,1)} %convolution_convert_fusion.1) | data formatting | bytes 7962624 | tf_op jit(solution)/shard_map/convert_element_type | solution.py:706
  381.9 4.4 convolution_convert_fusion
  386.2 6.6 %copy.125 = bf16[1152,1728]{1,0:T(8,128)(2,1)} copy(bf16[1152,1728]{0,1:T(8,128)(2,1)} %convolution_convert_fusion) | data formatting | bytes 7962624 | tf_op jit(solution)/shard_map/convert_element_type | solution.py:706
  392.9 70.4 %scatter_ffn.1 = (f32[144,1728]{1,0:T(8,128)}, f32[144,1728]{1,0:T(8,128)}, f32[144,1728]{1,0:T(8,128)}) custom-call(bf16[8,144,1728]{2,1,0:T(8,128)(2,1)} %bitcast.90, bf16[8,144,1728]{2,1,0:T(8,128)(2,1)} %bitcast.91, bf16[8,144,1728]{2,1,0:T(8,128)(2,1)} %bitcast.92), custom_call_target="tpu_custom_call" | custom-call | tf_op jit(solution)/shard_map/scatter_ffn/pallas_call | solution.py:416
  465.0 2.2 copy.136
  467.3 2.2 copy.137
  469.5 1.0 copy.138
  (172 shorter events, 9.3 us)
Async XLA Ops:
  0.6 64.9 %copy-start = (bf16[1024,1152]{1,0:T(8,128)(2,1)S(1)}, bf16[1024,1152]{1,0:T(8,128)(2,1)}, u32[]{:S(2)}) copy-start(bf16[1024,1152]{1,0:T(8,128)(2,1)} %param.21) | copy-start | bytes 7077892
  0.7 7.6 %copy-start.43 = (f32[256]{0:T(256)S(1)}, f32[256]{0:T(256)}, u32[]{:S(2)}) copy-start(f32[256]{0:T(256)} %param.29) | copy-start | bytes 3076
  1.9 8.7 %copy-start.54 = (f32[128]{0:T(128)}, f32[128]{0:T(128)S(1)}, u32[]{:S(2)}) copy-start(f32[128]{0:T(128)S(1)} %fusion.20) | copy-start | bytes 1540
  1.9 7.2 %copy-start.3 = (bf16[128,1152]{1,0:T(8,128)(2,1)S(1)}, bf16[128,1152]{1,0:T(8,128)(2,1)}, u32[]{:S(2)}) copy-start(bf16[128,1152]{1,0:T(8,128)(2,1)} %param.16) | copy-start | bytes 884740
  1.9 7.2 %copy-start.29 = (f32[1152]{0:T(1024)S(1)}, f32[1152]{0:T(1024)}, u32[]{:S(2)}) copy-start(f32[1152]{0:T(1024)} %param.25) | copy-start | bytes 13828
  2.0 13.3 %copy-start.45 = (f32[128]{0:T(128)}, f32[128]{0:T(128)S(1)}, u32[]{:S(2)}) copy-start(f32[128]{0:T(128)S(1)} %fusion.46) | copy-start | bytes 1540
  2.0 9.3 %copy-start.41 = (f32[256]{0:T(256)S(1)}, f32[256]{0:T(256)}, u32[]{:S(2)}) copy-start(f32[256]{0:T(256)} %param.30) | copy-start | bytes 3076
  2.0 9.4 %copy-start.40 = (s32[4096]{0:T(1024)S(1)}, s32[4096]{0:T(1024)}, u32[]{:S(2)}) copy-start(s32[4096]{0:T(1024)} %param.17) | copy-start | bytes 49156
  6.7 55.6 %copy-start.5 = (f32[128,4,256]{0,2,1:T(8,128)}, f32[128,4,256]{0,2,1:T(8,128)S(1)}, u32[]{:S(2)}) copy-start(f32[128,4,256]{0,2,1:T(8,128)S(1)} %copy.111) | copy-start | bytes 1572868
  8.2 2.4 copy-start.38
  8.2 2.4 copy-start.34
  10.6 0.8 copy-start.58
  11.3 46.9 %copy-start.47 = (f32[128]{0:T(128)}, f32[128]{0:T(128)S(1)}, u32[]{:S(2)}) copy-start(f32[128]{0:T(128)S(1)} %fusion.47) | copy-start | bytes 1540
  11.4 50.9 %copy-start.52 = (f32[128]{0:T(128)}, f32[128]{0:T(128)S(1)}, u32[]{:S(2)}) copy-start(f32[128]{0:T(128)S(1)} %multiply_exponential_fusion) | copy-start | bytes 1540
  12.0 50.3 %copy-start.49 = (f32[128]{0:T(128)}, f32[128]{0:T(128)S(1)}, u32[]{:S(2)}) copy-start(f32[128]{0:T(128)S(1)} %get-tuple-element.89) | copy-start | bytes 1540
  12.4 1.3 copy-start.22
  12.5 1.2 copy-start.24
  62.3 3.9 copy-start.31
  62.3 4.2 copy-start.30
  63.5 1.9 copy-start.9
  65.5 30.9 %copy-start.15 = (bf16[4,128,256]{1,2,0:T(8,128)(2,1)}, bf16[4,128,256]{1,2,0:T(8,128)(2,1)S(1)}, u32[]{:S(2)}) copy-start(bf16[4,128,256]{1,2,0:T(8,128)(2,1)S(1)} %copy.116) | copy-start | bytes 786436
  96.4 5.2 %copy-start.2 = (bf16[1152,1728]{0,1:T(8,128)(2,1)S(1)}, bf16[1152,1728]{0,1:T(8,128)(2,1)}, u32[]{:S(2)}) copy-start(bf16[1152,1728]{0,1:T(8,128)(2,1)} %param.23) | copy-start | bytes 11943940
  96.4 5.2 %copy-start.16 = (bf16[4,128,1152]{2,1,0:T(8,128)(2,1)S(1)}, bf16[4,128,1152]{2,1,0:T(8,128)(2,1)}, u32[]{:S(2)}) copy-start(bf16[4,128,1152]{2,1,0:T(8,128)(2,1)} %line_gather.2) | copy-start | bytes 3538948
  101.6 5.0 %copy-start.64 = (f32[512,1728]{0,1:T(8,128)}, f32[512,1728]{0,1:T(8,128)S(1)}, u32[]{:S(2)}) copy-start(f32[512,1728]{0,1:T(8,128)S(1)} %fusion.59) | copy-start | bytes 10616836
  101.6 5.0 %copy-start.56 = (bf16[1728,1152]{1,0:T(8,128)(2,1)S(1)}, bf16[1728,1152]{1,0:T(8,128)(2,1)}, u32[]{:S(2)}) copy-start(bf16[1728,1152]{1,0:T(8,128)(2,1)} %param.24) | copy-start | bytes 11943940
  106.6 3.6 copy-start.62
  106.6 31.9 %copy-start.11 = (bf16[128,1152]{1,0:T(8,128)(2,1)S(1)}, bf16[128,1152]{1,0:T(8,128)(2,1)}, u32[]{:S(2)}) copy-start(bf16[128,1152]{1,0:T(8,128)(2,1)} %param.31) | copy-start | bytes 884740
  106.6 31.9 %copy-start.33 = (f32[1152]{0:T(1024)S(1)}, f32[1152]{0:T(1024)}, u32[]{:S(2)}) copy-start(f32[1152]{0:T(1024)} %param.28) | copy-start | bytes 13828
  167.8 9.7 %copy-start.57 = (bf16[1152,1728]{0,1:T(8,128)(2,1)S(1)}, bf16[1152,1728]{0,1:T(8,128)(2,1)}, u32[]{:S(2)}) copy-start(bf16[1152,1728]{0,1:T(8,128)(2,1)} %param.22) | copy-start | bytes 11943940
  177.4 2.7 copy-start.60
  177.4 2.7 copy-start.7
  180.1 30.8 %copy-start.32 = (f32[1152]{0:T(1024)S(1)}, f32[1152]{0:T(1024)}, u32[]{:S(2)}) copy-start(f32[1152]{0:T(1024)} %param.26) | copy-start | bytes 13828
  210.9 3.3 copy-start.10
  213.2 7.7 %copy-start.12 = (bf16[128,1152]{1,0:T(8,128)(2,1)}, bf16[128,1152]{1,0:T(8,128)(2,1)S(1)}, u32[]{:S(2)}) copy-start(bf16[128,1152]{1,0:T(8,128)(2,1)S(1)} %fusion.17) | copy-start | bytes 884740
  214.2 7.9 %copy-start.23 = (f32[128,128]{0,1:T(8,128)S(1)}, f32[128,128]{0,1:T(8,128)}, u32[]{:S(2)}) copy-start(f32[128,128]{0,1:T(8,128)} %copy-done.22) | copy-start | bytes 196612
  214.2 7.9 %copy-start.25 = (f32[128,128]{0,1:T(8,128)S(1)}, f32[128,128]{0,1:T(8,128)}, u32[]{:S(2)}) copy-start(f32[128,128]{0,1:T(8,128)} %copy-done.24) | copy-start | bytes 196612
  214.2 0.8 copy-start.13
  215.0 7.2 %copy-start.6 = (f32[128,4,256]{0,2,1:T(8,128)S(1)}, f32[128,4,256]{0,2,1:T(8,128)}, u32[]{:S(2)}) copy-start(f32[128,4,256]{0,2,1:T(8,128)} %copy-done.5) | copy-start | bytes 1572868
  215.0 7.2 %copy-start.35 = (f32[128,4]{0,1:T(4,128)S(1)}, f32[128,4]{0,1:T(4,128)}, u32[]{:S(2)}) copy-start(f32[128,4]{0,1:T(4,128)} %copy-done.34) | copy-start | bytes 6148
  215.0 7.2 %copy-start.44 = (f32[256]{0:T(256)S(1)}, f32[256]{0:T(256)}, u32[]{:S(2)}) copy-start(f32[256]{0:T(256)} %param.29) | copy-start | bytes 3076
  215.0 7.9 %copy-start.39 = (f32[128,4]{0,1:T(4,128)S(1)}, f32[128,4]{0,1:T(4,128)}, u32[]{:S(2)}) copy-start(f32[128,4]{0,1:T(4,128)} %copy-done.38) | copy-start | bytes 6148
  215.0 8.1 %copy-start.4 = (bf16[1152,1024]{1,0:T(8,128)(2,1)S(1)}, bf16[1152,1024]{1,0:T(8,128)(2,1)}, u32[]{:S(2)}) copy-start(bf16[1152,1024]{1,0:T(8,128)(2,1)} %param.18) | copy-start | bytes 7077892
  223.1 48.4 %copy-start.14 = (bf16[128,4,256]{0,2,1:T(8,128)(2,1)}, bf16[128,4,256]{0,2,1:T(8,128)(2,1)S(1)}, u32[]{:S(2)}) copy-start(bf16[128,4,256]{0,2,1:T(8,128)(2,1)S(1)} %fusion.22) | copy-start | bytes 786436
  223.1 48.4 %copy-start.50 = (f32[128]{0:T(128)S(1)}, f32[128]{0:T(128)}, u32[]{:S(2)}) copy-start(f32[128]{0:T(128)} %copy-done.49) | copy-start | bytes 1540
  223.2 48.4 %copy-start.53 = (f32[128]{0:T(128)S(1)}, f32[128]{0:T(128)}, u32[]{:S(2)}) copy-start(f32[128]{0:T(128)} %copy-done.52) | copy-start | bytes 1540
  223.2 49.6 %copy-start.20 = (f32[128,256]{1,0:T(8,128)S(1)}, f32[128,256]{1,0:T(8,128)}, u32[]{:S(2)}) copy-start(f32[128,256]{1,0:T(8,128)} %copy-done.19) | copy-start | bytes 393220
  223.2 49.6 %copy-start.42 = (f32[256]{0:T(256)S(1)}, f32[256]{0:T(256)}, u32[]{:S(2)}) copy-start(f32[256]{0:T(256)} %param.30) | copy-start | bytes 3076
  223.2 49.6 %copy-start.48 = (f32[128]{0:T(128)S(1)}, f32[128]{0:T(128)}, u32[]{:S(2)}) copy-start(f32[128]{0:T(128)} %copy-done.47) | copy-start | bytes 1540
  223.2 50.3 %copy-start.59 = (f32[128]{0:T(128)S(1)}, f32[128]{0:T(128)}, u32[]{:S(2)}) copy-start(f32[128]{0:T(128)} %copy-done.58) | copy-start | bytes 1540
  223.2 50.4 %copy-start.26 = (bf16[1152,256]{1,0:T(8,128)(2,1)S(1)}, bf16[1152,256]{1,0:T(8,128)(2,1)}, u32[]{:S(2)}) copy-start(bf16[1152,256]{1,0:T(8,128)(2,1)} %param.19) | copy-start | bytes 1769476
  224.1 50.7 %copy-start.27 = (bf16[1152,256]{1,0:T(8,128)(2,1)S(1)}, bf16[1152,256]{1,0:T(8,128)(2,1)}, u32[]{:S(2)}) copy-start(bf16[1152,256]{1,0:T(8,128)(2,1)} %param.20) | copy-start | bytes 1769476
  224.1 50.7 %copy-start.46 = (f32[128]{0:T(128)S(1)}, f32[128]{0:T(128)}, u32[]{:S(2)}) copy-start(f32[128]{0:T(128)} %copy-done.45) | copy-start | bytes 1540
  271.5 4.3 copy-start.55
  280.6 7.7 %copy-start.36 = (f32[1152]{0:T(1024)S(1)}, f32[1152]{0:T(1024)}, u32[]{:S(2)}) copy-start(f32[1152]{0:T(1024)} %get-tuple-element.53) | copy-start | bytes 13828
  280.6 7.8 %copy-start.37 = (f32[1152]{0:T(1024)S(1)}, f32[1152]{0:T(1024)}, u32[]{:S(2)}) copy-start(f32[1152]{0:T(1024)} %get-tuple-element.47) | copy-start | bytes 13828
  290.2 69.7 %copy-start.17 = (bf16[4,128,1152]{2,1,0:T(8,128)(2,1)S(1)}, bf16[4,128,1152]{2,1,0:T(8,128)(2,1)}, u32[]{:S(2)}) copy-start(bf16[4,128,1152]{2,1,0:T(8,128)(2,1)} %line_gather.2) | copy-start | bytes 3538948
  290.2 69.7 %copy-start.61 = (bf16[512,1728]{0,1:T(8,128)(2,1)S(1)}, bf16[512,1728]{0,1:T(8,128)(2,1)}, u32[]{:S(2)}) copy-start(bf16[512,1728]{0,1:T(8,128)(2,1)} %copy-done.60) | copy-start | bytes 5308420
  364.4 6.6 %copy-start.8 = (bf16[512,1728]{0,1:T(8,128)(2,1)S(1)}, bf16[512,1728]{0,1:T(8,128)(2,1)}, u32[]{:S(2)}) copy-start(bf16[512,1728]{0,1:T(8,128)(2,1)} %copy-done.7) | copy-start | bytes 5308420
  375.3 6.6 %copy-start.18 = (bf16[4,128,1152]{2,1,0:T(8,128)(2,1)S(1)}, bf16[4,128,1152]{2,1,0:T(8,128)(2,1)}, u32[]{:S(2)}) copy-start(bf16[4,128,1152]{2,1,0:T(8,128)(2,1)} %line_gather.3) | copy-start | bytes 3538948
  375.3 6.6 %copy-start.63 = (bf16[512,1728]{0,1:T(8,128)(2,1)S(1)}, bf16[512,1728]{0,1:T(8,128)(2,1)}, u32[]{:S(2)}) copy-start(bf16[512,1728]{0,1:T(8,128)(2,1)} %copy-done.62) | copy-start | bytes 5308420
  392.9 70.5 %copy-start.51 = (f32[8,128]{1,0:T(8,128)S(1)}, f32[8,128]{1,0:T(8,128)}, u32[]{:S(2)}) copy-start(f32[8,128]{1,0:T(8,128)} %get-tuple-element.44) | copy-start | bytes 12292
  392.9 71.5 %copy-start.28 = (f32[32,1152]{1,0:T(8,128)S(1)}, f32[32,1152]{1,0:T(8,128)}, u32[]{:S(2)}) copy-start(f32[32,1152]{1,0:T(8,128)} %get-tuple-element.111) | copy-start | bytes 442372
  392.9 77.6 %copy-start.1 = (bf16[1024,1152]{1,0:T(8,128)(2,1)S(1)}, bf16[1024,1152]{1,0:T(8,128)(2,1)}, u32[]{:S(2)}) copy-start(bf16[1024,1152]{1,0:T(8,128)(2,1)} %param.21) | copy-start | bytes 7077892
  463.3 6.2 %copy-start.21 = (f32[144,1728]{1,0:T(8,128)S(1)}, f32[144,1728]{1,0:T(8,128)}, u32[]{:S(2)}) copy-start(f32[144,1728]{1,0:T(8,128)} %get-tuple-element.43) | copy-start | bytes 2985988
  (1 other events, 0.7 us)

commit v2 on v1

--- a/solution.py
+++ b/solution.py
@@ -521,6 +521,455 @@
         name="attend_back",
         compiler_params=pltpu.CompilerParams(vmem_limit_bytes=LIMIT),
     )(q, k, v, start, index, log_total, dots, grads)
+
+
+class Sum:
+    def __init__(self, links, part, boxes, order):
+        self.links, self.part, self.boxes, self.order = links, part, boxes, order
+        self.stage = 0
+        self.used = 0
+        self.slot = {}
+        self.waiting = {}
+
+    def current(self, mask):
+        if mask in self.slot:
+            return self.boxes.at[self.slot[mask]]
+        return self.part(mask)
+
+    def launch(self):
+        bit = self.order[self.stage]
+        rest = self.order[self.stage + 1 :]
+        target = self.links.across(bit)
+        after = 1 << rest[0] if rest else 0
+        for mask in sorted(subsets(rest), key=lambda m: 0 if m & after else 1):
+            where = self.used
+            self.used += 1
+            copy = self.links.go(self.current(mask | (1 << bit)), self.boxes.at[where], target)
+            self.waiting[mask] = (copy, where)
+        self.stage += 1
+
+    def settle(self, kept=None):
+        for mask in list(self.waiting):
+            copy, where = self.waiting.pop(mask)
+            mine = kept(mask) if kept is not None else self.current(mask)
+            copy.wait_recv()
+            self.boxes[where] = self.boxes[where] + mine[...]
+            self.slot[mask] = where
+
+    def last(self, kept=None):
+        ((mask, (copy, where)),) = self.waiting.items()
+        self.waiting = {}
+        mine = kept(mask) if kept is not None else self.current(mask)
+        copy.wait_recv()
+        return self.boxes[where].astype(jnp.float32) + mine[...].astype(jnp.float32)
+
+
+class Links:
+    def __init__(self, nseq, heads, send, recv):
+        self.s, self.h = place()
+        self.nseq, self.heads = nseq, heads
+        self.send, self.recv = send, recv
+        self.count = 0
+        self.started = []
+        self.others = [lax.rem(self.h + d, heads) for d in range(1, heads)]
+
+    def greet(self):
+        bits = self.nseq.bit_length() - 1
+        greet([self.across(b) for b in range(bits)] + [(self.s, o) for o in self.others])
+
+    def across(self, bit):
+        return (related(self.s, 1 << bit), self.h)
+
+    def go(self, src, dst, target):
+        k = self.count
+        self.count += 1
+        copy = remote(src, dst, self.send.at[k], self.recv.at[k], target)
+        copy.start()
+        self.started.append(copy)
+        return copy
+
+    def over_heads(self, src, boxes):
+        return [self.go(src.at[o], boxes.at[d], (self.s, o)) for d, o in enumerate(self.others)]
+
+    def finish(self):
+        for copy in self.started:
+            copy.wait_send()
+
+
+def back_norm(v, gain, d_out):
+    scale = lax.rsqrt(jnp.mean(v * v, axis=-1, keepdims=True) + EPS)
+    unit = v * scale
+    inner = d_out * gain
+    d_v = scale * (inner - unit * jnp.mean(inner * unit, axis=-1, keepdims=True))
+    return d_v, jnp.sum(d_out * unit, axis=0, keepdims=True)
+
+
+def back_rotate(d, cosines, sines):
+    half = d.shape[-1] // 2
+    first, second = d[:, :half], d[:, half:]
+    return jnp.concatenate(
+        [first * cosines + second * sines, second * cosines - first * sines], axis=-1
+    )
+
+
+def tail_kernel(
+    nseq,
+    heads,
+    qcount,
+    scale,
+    q_ref,
+    k_ref,
+    v_ref,
+    start_ref,
+    index_ref,
+    log_ref,
+    att_ref,
+    mixed_t_ref,
+    d_proj_ref,
+    w_out_ref,
+    q_lin_ref,
+    k_lin_ref,
+    cos_ref,
+    sin_ref,
+    gain_q_ref,
+    gain_k_ref,
+    attn_t_ref,
+    w_qkv_ref,
+    x_ref,
+    gain_in_ref,
+    d_hid_ref,
+    gains_ref,
+    d_gate_ref,
+    d_up_ref,
+    d_down_ref,
+    o_tokens,
+    o_qkv,
+    o_out,
+    o_gate,
+    o_up,
+    o_down,
+    o_gains,
+    dk,
+    dv,
+    dq_t,
+    grads,
+    grads_t,
+    box_k,
+    box_v,
+    zbox_k,
+    zbox_v,
+    dw_out,
+    box_out,
+    zsrc_out,
+    zbox_out,
+    dw_a,
+    dw_b,
+    box_a,
+    box_b,
+    zsrc_qkv,
+    zbox_qkv,
+    d_qkv,
+    keep_gate,
+    keep_up,
+    keep_down,
+    box_gate,
+    box_up,
+    box_down,
+    gsum,
+    gbox,
+    gzbox,
+    send,
+    recv,
+    local_sem,
+):
+    f32, bf16 = jnp.float32, jnp.bfloat16
+    bits = nseq.bit_length() - 1
+    ups, downs = seq_orders(bits)
+    links = Links(nseq, heads, send, recv)
+    s, h = links.s, links.h
+    rows = d_proj_ref.shape[0]
+    width = gain_q_ref.shape[1]
+    groups, span = k_ref.shape[:2]
+    links.greet()
+
+    ffn = []
+    kept_copies = []
+    kept_masks = subsets(ups)
+    for n, (src, keep, box, order) in enumerate(
+        (
+            (d_gate_ref, keep_gate, box_gate, ups),
+            (d_up_ref, keep_up, box_up, downs),
+            (d_down_ref, keep_down, box_down, ups),
+        )
+    ):
+        total = Sum(links, lambda m, src=src: src.at[related(s, m)], box, [0] + order)
+        total.launch()
+        total.kept = lambda m, keep=keep: keep.at[kept_masks.index(m)]
+        ffn.append(total)
+        for i, m in enumerate(kept_masks):
+            copy = pltpu.make_async_copy(src.at[related(s, m)], keep.at[i], local_sem.at[n, i])
+            copy.start()
+            kept_copies.append(copy)
+
+    d_proj = d_proj_ref[...]
+
+    def out_block(j, carry):
+        dw_out[j] = jnp.dot(mixed_t_ref[j], d_proj, preferred_element_type=f32).astype(bf16)
+        return carry
+
+    lax.fori_loop(0, nseq, out_block, 0)
+    sum_out = Sum(links, lambda m: dw_out.at[related(s, m)], box_out, [0] + downs)
+    sum_out.launch()
+
+    for j in range(qcount):
+        part = w_out_ref[pl.ds(j * width, width), :]
+        grads[pl.ds(j * rows, rows), :] = contract_last(d_proj, part).astype(bf16)
+        grads_t[:, pl.ds(j * rows, rows)] = contract_last(part, d_proj).astype(bf16)
+    dots = jnp.sum(grads_t[...].astype(f32) * att_ref[...], axis=0, keepdims=True)
+    start = start_ref[...]
+    index = index_ref[...]
+    log_total = log_ref[...]
+    dq_t[...] = jnp.zeros_like(dq_t)
+
+    def step(g, carry):
+        keys = k_ref[g]
+        queries = q_ref[...]
+        scores = contract_last(keys, queries)
+        key = g * span + lax.broadcasted_iota(jnp.int32, scores.shape, 0)
+        probs = jnp.where((key >= start) & (key <= index), jnp.exp(scores - log_total), 0.0)
+        d_probs = jnp.dot(v_ref[g], grads_t[...], preferred_element_type=f32)
+        d_scores = (probs * (d_probs - dots)).astype(bf16)
+        dv[g] = (
+            jnp.dot(probs.astype(bf16), grads[...], preferred_element_type=f32)
+            .astype(bf16)
+            .reshape(dv.shape[1:])
+        )
+        dk[g] = (
+            jnp.dot(d_scores, queries, preferred_element_type=f32)
+            .astype(bf16)
+            .reshape(dk.shape[1:])
+        )
+        dq_t[...] += contract_first(keys, d_scores)
+        return carry
+
+    lax.fori_loop(0, s + 1, step, 0)
+
+    def blank(g, carry):
+        dk[g] = jnp.zeros(dk.shape[1:], bf16)
+        dv[g] = jnp.zeros(dv.shape[1:], bf16)
+        return carry
+
+    lax.fori_loop(s + 1, groups, blank, 0)
+    sum_k = Sum(links, lambda m: dk.at[related(s, m)], box_k, [0] + ups)
+    sum_v = Sum(links, lambda m: dv.at[related(s, m)], box_v, [0] + downs)
+    sum_k.launch()
+    sum_v.launch()
+
+    for copy in kept_copies:
+        copy.wait()
+    gate, up, down = ffn
+    gate.settle(gate.kept)
+    gate.launch()
+    up.settle(up.kept)
+    up.launch()
+    sum_k.settle()
+    sum_k.launch()
+    sum_v.settle()
+    sum_v.launch()
+    sum_out.settle()
+    sum_out.launch()
+
+    cosines, sines = cos_ref[...], sin_ref[...]
+    d_gain_q = jnp.zeros((1, width), f32)
+    for j in range(qcount):
+        d_rot = dq_t[:, pl.ds(j * rows, rows)].T * scale
+        d_lin, terms = back_norm(
+            q_lin_ref[:, pl.ds(j * width, width)],
+            gain_q_ref[...],
+            back_rotate(d_rot, cosines, sines),
+        )
+        d_qkv[:, pl.ds(j * width, width)] = d_lin.astype(bf16)
+        d_gain_q = d_gain_q + terms
+
+    sum_k.settle()
+    sum_k.launch()
+    sum_v.settle()
+    sum_v.launch()
+    down.settle(down.kept)
+    down.launch()
+    heads_shape = dk.shape[2:]
+
+    def over(total, zbox, shape):
+        where = total.waiting[0][1]
+        total.settle()
+        return links.over_heads(total.boxes.at[where], zbox), total.boxes.at[where]
+
+    z_k, own_k = over(sum_k, zbox_k, heads_shape)
+    z_v, own_v = over(sum_v, zbox_v, heads_shape)
+    sum_out.settle()
+    sum_out.launch()
+
+    def gathered(copies, zbox, own):
+        total = own[h].astype(f32)
+        for d, copy in enumerate(copies):
+            copy.wait_recv()
+            total = total + zbox[d].astype(f32)
+        return total
+
+    d_keys = gathered(z_k, zbox_k, own_k)
+    d_values = gathered(z_v, zbox_v, own_v)
+    d_lin, d_gain_k = back_norm(
+        k_lin_ref[...], gain_k_ref[...], back_rotate(d_keys, cosines, sines)
+    )
+    qw = qcount * width
+    d_qkv[:, pl.ds(qw, width)] = d_lin.astype(bf16)
+    d_qkv[:, pl.ds(qw + width, width)] = d_values.astype(bf16)
+    cut_at = dw_a.shape[2]
+
+    def qkv_block(j, carry):
+        dw_a[j] = jnp.dot(
+            attn_t_ref[j], d_qkv[:, :cut_at], preferred_element_type=f32
+        ).astype(bf16)
+        dw_b[j] = jnp.dot(
+            attn_t_ref[j], d_qkv[:, cut_at:], preferred_element_type=f32
+        ).astype(bf16)
+        return carry
+
+    lax.fori_loop(0, nseq, qkv_block, 0)
+    sum_a = Sum(links, lambda m: dw_a.at[related(s, m)], box_a, [0] + ups)
+    sum_b = Sum(links, lambda m: dw_b.at[related(s, m)], box_b, [0] + downs)
+    sum_a.launch()
+    sum_b.launch()
+
+    d_attn_in = contract_last(d_qkv[...], w_qkv_ref[...])
+    d_x, d_gain_in = back_norm(x_ref[...].astype(f32), gain_in_ref[...], d_attn_in)
+    o_tokens[...] = (d_hid_ref[...] + d_x).astype(o_tokens.dtype)
+
+    gsum[0] = gains_ref[...]
+    gsum[0, 0:1, :] = d_gain_in
+    gsum[0, 4:5, :width] = d_gain_q
+    gsum[0, 5:6, :width] = d_gain_k
+    gain_copies = [links.go(gsum.at[0], gbox.at[0], links.across(0))]
+
+    sum_a.settle()
+    sum_a.launch()
+    sum_b.settle()
+    sum_b.launch()
+    for bit in range(bits):
+        gain_copies[-1].wait_recv()
+        gsum[bit + 1] = gsum[bit] + gbox[bit]
+        if bit + 1 < bits:
+            gain_copies.append(
+                links.go(gsum.at[bit + 1], gbox.at[bit + 1], links.across(bit + 1))
+            )
+    gain_z = [
+        links.go(gsum.at[bits], gzbox.at[d], (s, o)) for d, o in enumerate(links.others)
+    ]
+
+    def pieces(total, zsrc, col, size):
+        value = total.last()
+        each = value.shape[0] // heads
+        for p in range(heads):
+            zsrc[p, :, pl.ds(col, size)] = value[p * each : (p + 1) * each].astype(bf16)
+
+    pieces(sum_out, zsrc_out, 0, dw_out.shape[2])
+    z_out = links.over_heads(zsrc_out, zbox_out)
+    gate.settle()
+    gate.launch()
+    up.settle()
+    up.launch()
+    sum_a.settle()
+    sum_a.launch()
+    sum_b.settle()
+    sum_b.launch()
+    pieces(sum_a, zsrc_qkv, 0, cut_at)
+    pieces(sum_b, zsrc_qkv, cut_at, dw_b.shape[2])
+    z_qkv = links.over_heads(zsrc_qkv, zbox_qkv)
+    down.settle()
+    down.launch()
+    o_gate[...] = gate.last()
+    o_up[...] = up.last()
+    total = gsum[bits]
+    for d, copy in enumerate(gain_z):
+        copy.wait_recv()
+        total = total + gzbox[d]
+    o_gains[...] = total
+    o_out[...] = gathered(z_out, zbox_out, zsrc_out)
+    o_qkv[...] = gathered(z_qkv, zbox_qkv, zsrc_qkv)
+    o_down[...] = down.last()
+    links.finish()
+
+
+def tail(nseq, heads, qcount, scale, cid, *arrays):
+    (q, k, v, _, _, _, att, mixed_t, d_proj, w_out, q_lin, k_lin, _, _, gain_q, _) = arrays[:16]
+    (attn_t, w_qkv, x, gain_in, d_hid, gains, d_gate, d_up, d_down) = arrays[16:]
+    f32, bf16 = jnp.float32, jnp.bfloat16
+    rows, model = d_proj.shape
+    width = gain_q.shape[1]
+    cols = w_qkv.shape[1]
+    cut_at = cols // 2
+    out_rows, qkv_rows = mixed_t.shape[1], attn_t.shape[1]
+    pieces_kv = (heads, rows, width)
+    ffn_block = d_gate.shape[1:]
+    some, all_but = nseq // 2, nseq - 1
+    bits = nseq.bit_length() - 1
+    copies = 8 * all_but + 5 * (heads - 1) + bits
+    vm = pl.BlockSpec(memory_space=VMEM)
+    anywhere = pl.BlockSpec(memory_space=pl.ANY)
+
+    def kernel(*refs):
+        tail_kernel(nseq, heads, qcount, scale, *refs)
+
+    return pl.pallas_call(
+        kernel,
+        out_shape=[
+            jax.ShapeDtypeStruct((rows, model), bf16),
+            jax.ShapeDtypeStruct((qkv_rows // heads, cols), f32),
+            jax.ShapeDtypeStruct((out_rows // heads, model), f32),
+            jax.ShapeDtypeStruct(ffn_block, f32),
+            jax.ShapeDtypeStruct(ffn_block, f32),
+            jax.ShapeDtypeStruct(ffn_block, f32),
+            jax.ShapeDtypeStruct(gains.shape, f32),
+        ],
+        in_specs=[vm] * (len(arrays) - 3) + [anywhere] * 3,
+        out_specs=[vm] * 7,
+        scratch_shapes=[
+            VMEM((nseq,) + pieces_kv, bf16),
+            VMEM((nseq,) + pieces_kv, bf16),
+            VMEM((width, qcount * rows), f32),
+            VMEM((qcount * rows, width), bf16),
+            VMEM((width, qcount * rows), bf16),
+            VMEM((all_but,) + pieces_kv, bf16),
+            VMEM((all_but,) + pieces_kv, bf16),
+            VMEM((heads - 1, rows, width), bf16),
+            VMEM((heads - 1, rows, width), bf16),
+            VMEM((nseq, out_rows, model), bf16),
+            VMEM((all_but, out_rows, model), bf16),
+            VMEM((heads, out_rows // heads, model), bf16),
+            VMEM((heads - 1, out_rows // heads, model), bf16),
+            VMEM((nseq, qkv_rows, cut_at), bf16),
+            VMEM((nseq, qkv_rows, cols - cut_at), bf16),
+            VMEM((all_but, qkv_rows, cut_at), bf16),
+            VMEM((all_but, qkv_rows, cols - cut_at), bf16),
+            VMEM((heads, qkv_rows // heads, cols), bf16),
+            VMEM((heads - 1, qkv_rows // heads, cols), bf16),
+            VMEM((rows, cols), bf16),
+        ]
+        + [VMEM((some,) + ffn_block, bf16)] * 3
+        + [VMEM((all_but,) + ffn_block, bf16)] * 3
+        + [
+            VMEM((bits + 1,) + gains.shape, f32),
+            VMEM((bits,) + gains.shape, f32),
+            VMEM((heads - 1,) + gains.shape, f32),
+            pltpu.SemaphoreType.DMA((copies,)),
+            pltpu.SemaphoreType.DMA((copies,)),
+            pltpu.SemaphoreType.DMA((3, some)),
+        ],
+        name="tail",
+        compiler_params=pltpu.CompilerParams(
+            collective_id=cid, has_side_effects=True, vmem_limit_bytes=62 * 2**20
+        ),
+    )(*arrays)
 
 
 def local(
@@ -640,6 +1089,73 @@
     unused, back_two = jax.vjp(norm_rows, projected, gain_attn_out)
     d_projected, d_gain_two = back_two(d_hidden)
     d_projected = d_projected.astype(bf16)
+    qw = qcount * width
+    each, few = model // (nseq * heads), width // (nseq * heads)
+    if nseq <= 8:
+        gains = jnp.concatenate(
+            [
+                jnp.zeros((1, model), jnp.float32),
+                d_gain_two[None],
+                d_gain_three[None],
+                d_gain_four[None],
+                jnp.zeros((4, model), jnp.float32),
+            ]
+        )
+        w_qkv = jnp.concatenate([w_query, w_key, w_value], axis=1)
+        blocks = [
+            d.astype(bf16).reshape(nseq, model // nseq, hidden_units)
+            for d in (d_w_gate, d_w_up, d_w_down)
+        ]
+        grad_tokens, sum_qkv, sum_out, sum_gate, sum_up, sum_down, sum_gains = tail(
+            nseq,
+            heads,
+            qcount,
+            scale,
+            9,
+            queries,
+            keys,
+            values,
+            starts,
+            index,
+            log_total,
+            attended_t,
+            mixed_local.T.reshape(nseq, -1, local_rows),
+            d_projected,
+            w_out,
+            q_linear,
+            k_linear,
+            cosines,
+            sines,
+            gain_query[None],
+            gain_key[None],
+            attn_in.T.reshape(nseq, -1, local_rows),
+            w_qkv,
+            tokens,
+            gain_attn_in[None],
+            d_hidden,
+            gains,
+            *blocks,
+        )
+        which = seq_index * heads + head_index
+        wide = lax.dynamic_slice_in_dim(sum_gains[:4], which * each, each, 1)
+        narrow = lax.dynamic_slice_in_dim(sum_gains[4:6], which * few, few, 1)
+        return (
+            output.astype(bf16),
+            grad_tokens,
+            sum_qkv[:, :qw],
+            sum_qkv[:, qw : qw + width],
+            sum_qkv[:, qw + width :],
+            sum_out,
+            sum_gate,
+            sum_up,
+            sum_down.T,
+            wide[0],
+            wide[1],
+            wide[2],
+            wide[3],
+            narrow[0],
+            narrow[1],
+        )
     d_w_out = contract_first(mixed_local, d_projected)
     d_mixed = contract_last(d_projected, w_out).astype(bf16)
     grad_attended = stacked(d_mixed)

time: 476 us -> 402 us (0.84)
  Pallas kernels: 340 us -> 288 us
  matrix products: 58 us -> 50.1 us
  local copies, waits for them, and re-layouts: 45.5 us -> 37.6 us
  other arithmetic: 25.2 us -> 20 us
    pallas_call x4 -> x1, Pallas kernels: 190 us -> 137 us  [tail(): pl.pallas_call(kernel, out_shape=[jax.ShapeDtypeStruct((rows, model), bf1...]
    dot_general x5 -> x3, matrix products: 18.7 us -> 14.9 us  [contract_first(): lax.dot_general(left, right, (((0,), (0,)), ((), ())), preferred_element_...]
    dot_general x7 -> x3, matrix products: 19.1 us -> 15.9 us  [contract_last(): lax.dot_general(left, right, (((1,), (1,)), ((), ())), preferred_element_...]
    reduce_sum x9 -> x7, other arithmetic: 11.4 us -> 9.36 us  [norm_rows(): return v * lax.rsqrt(jnp.mean(v * v, axis=-1, keepdims=True) + EPS) * gain]
where the time goes in v2:
time: 402 us; the launch traced here: 397 us
  Pallas kernels  288 us (72%)
  matrix products  50.1 us (12%)
  local copies, waits for them, and re-layouts  37.6 us (9%)
  other arithmetic  20 us (5%)
    pallas_call x1, Pallas kernels, tail(): pl.pallas_call(kernel, out_shape=[jax.ShapeDtypeStruct((rows, model), bf1...  137 us
    pallas_call x2, Pallas kernels, line_gather(): pl.pallas_call(functools.partial(line_gather_kernel, heads), out_shape=ja...  54.3 us
    pallas_call x2, Pallas kernels, line_scatter(): pl.pallas_call(functools.partial(line_scatter_kernel, heads), out_shape=j...  52.1 us
    pallas_call x1, Pallas kernels, gather_all(): pl.pallas_call(kernel, out_shape=[jax.ShapeDtypeStruct((nseq, heads) + a....  39.7 us
    convert_element_type x3, local copies, waits for them, and re-layouts, local(): d.astype(bf16).reshape(nseq, model // nseq, hidden_units)  19.6 us
    dot_general x3, matrix products, contract_last(): lax.dot_general(left, right, (((1,), (1,)), ((), ())), preferred_element_...  15.9 us
    dot_general x3, matrix products, contract_first(): lax.dot_general(left, right, (((0,), (0,)), ((), ())), preferred_element_...  14.9 us
    reduce_sum x7, other arithmetic, norm_rows(): return v * lax.rsqrt(jnp.mean(v * v, axis=-1, keepdims=True) + EPS) * gain  9.36 us

profile of v2, /device:TPU:0, one launch (start us, length us, event | category | flops | bytes accessed | tf_op | source)
XLA Modules:
  0.0 397.3 jit_solution(9934254996325482881)
XLA Ops:
  0.7 1.2 fusion.11
  1.9 2.4 fusion.25.refs_10_
  4.3 0.2 reshape.237
  4.5 0.2 multiply_reduce_fusion.7
  4.8 0.2 multiply_multiply_fusion.3
  5.0 0.4 multiply_reduce_fusion.8
  5.4 0.1 multiply_multiply_fusion.4
  5.5 0.1 dynamic_slice.9
  5.6 0.5 select_reduce_fusion
  6.1 0.3 subtract_convert_fusion.1
  6.5 0.1 subtract_convert_fusion
  6.6 0.2 fusion.17
  6.8 0.8 copy.57
  7.6 0.6 pad_maximum_fusion.1.refs_0_
  8.2 2.1 convolution_convert_fusion.4.refs_1_
  10.4 39.7 %gather_all.1 = (bf16[8,4,128,256]{3,2,1,0:T(8,128)(2,1)}, bf16[8,4,128,256]{3,2,1,0:T(8,128)(2,1)}) custom-call(bf16[128,256]{1,0:T(8,128)(2,1)} %pad_maximum_fusion.1.refs_0_, bf16[128,256]{1,0:T(8,128)(2,1)} %convolution_convert_fusion.4.refs_1_), custom_call_target="tpu_custom_call" | custom-call | tf_op jit(solution)/shard_map/gather_all/pallas_call | solution.py:146
  50.1 0.6 tile.4
  50.6 0.6 tile.5
  51.2 4.4 %attend.1 = (f32[256,512]{1,0:T(8,128)}, f32[1,512]{1,0:T(1,128)}) custom-call(bf16[512,256]{1,0:T(8,128)(2,1)} %bitcast.73, bf16[8,512,256]{2,1,0:T(8,128)(2,1)} %bitcast.68, bf16[8,512,256]{2,1,0:T(8,128)(2,1)} %bitcast.70, s32[1,512]{1,0:T(1,128)} %bitcast.87, s32[1,512]{1,0:T(1,128)} %bitcast.89), custom_call_target="tpu_custom_call" | custom-call | tf_op jit(solution)/shard_map/attend/pallas_call | solution.py:457
  55.6 1.1 convert_bitcast_fusion
  56.7 0.1 reshape.240
  56.9 0.6 multiply_reduce_fusion.6
  57.5 1.0 multiply_reduce_fusion.5
  58.6 0.8 multiply_convert_fusion.2.x_ref
  59.4 29.1 %line_gather.2 = bf16[4,128,1152]{2,1,0:T(8,128)(2,1)} custom-call(bf16[128,1152]{1,0:T(8,128)(2,1)} %multiply_convert_fusion.2.x_ref), custom_call_target="tpu_custom_call" | custom-call | tf_op jit(solution)/shard_map/line_gather/pallas_call | solution.py:205
  88.5 5.1 %fusion.28 = f32[512,1728]{0,1:T(8,128)S(1)} fusion(bf16[512,1152]{1,0:T(8,128)(2,1)} %bitcast.77, bf16[1152,1728]{0,1:T(8,128)(2,1)} %param.22), kind=kOutput, calls=%fused_computation.89 | convolution fusion | flops 2038431744 | bytes 8699904 | tf_op jit(solution)/shard_map/dot_general | solution.py:1056
  93.7 5.1 %multiply_convert_fusion.1 = (bf16[512,1728]{0,1:T(8,128)(2,1)S(1)}, f32[512,1728]{0,1:T(8,128)}) fusion(f32[512,1728]{0,1:T(8,128)S(1)} %fusion.28, bf16[512,1152]{1,0:T(8,128)(2,1)S(1)} %bitcast.79, bf16[1152,1728]{0,1:T(8,128)(2,1)S(1)} %copy-done), kind=kOutput, calls=%fused_computation.14 | convolution fusion | flops 2047279104 | bytes 14008320 | tf_op jit(solution)/shard_map/dot_general | solution.py:1057
  98.8 3.6 convolution_convert_fusion.3
  102.4 27.0 %line_scatter.2 = f32[128,1152]{1,0:T(8,128)} custom-call(bf16[4,128,1152]{2,1,0:T(8,128)(2,1)} %bitcast.83), custom_call_target="tpu_custom_call" | custom-call | tf_op jit(solution)/shard_map/line_scatter/pallas_call | solution.py:292
  129.4 1.2 multiply_reduce_fusion.4
  130.6 1.9 fusion.14
  132.5 2.2 fusion.15
  134.6 25.2 %line_gather.3 = bf16[4,128,1152]{2,1,0:T(8,128)(2,1)} custom-call(bf16[128,1152]{1,0:T(8,128)(2,1)} %get-tuple-element.50.x_ref), custom_call_target="tpu_custom_call" | custom-call | tf_op jit(solution)/shard_map/line_gather/pallas_call | solution.py:205
  159.9 9.7 %multiply_convert_fusion = (bf16[512,1728]{0,1:T(8,128)(2,1)S(1)}, bf16[512,1728]{0,1:T(8,128)(2,1)S(1)}) fusion(f32[512,1728]{0,1:T(8,128)} %copy-done.41, f32[512,1728]{0,1:T(8,128)} %get-tuple-element.70, bf16[512,1152]{1,0:T(8,128)(2,1)} %bitcast.81, bf16[1728,1152]{1,0:T(8,128)(2,1)} %param.24), kind=kOutput, calls=%fused_computation.13 | convolution fusion | flops 2059665408 | bytes 15777792 | tf_op jit(solution)/shard_map/dot_general | solution.py:44
  169.6 2.6 fusion.29
  172.2 3.6 fusion.7
  175.9 25.2 %line_scatter.3 = f32[128,1152]{1,0:T(8,128)} custom-call(bf16[4,128,1152]{2,1,0:T(8,128)(2,1)} %bitcast.72), custom_call_target="tpu_custom_call" | custom-call | tf_op jit(solution)/shard_map/line_scatter/pallas_call | solution.py:292
  201.1 1.8 multiply_reduce_fusion
  202.9 2.1 multiply_reduce_fusion.1
  205.0 0.9 fusion.16.refs_8_
  205.9 0.9 copy.59
  206.8 3.5 pad_maximum_fusion.refs_17_
  210.3 0.6 broadcast_in_dim.35.refs_19_
  211.0 0.7 concatenate.17.refs_21_
  211.6 6.2 %convolution_convert_fusion.2 = bf16[1152,1728]{0,1:T(8,128)(2,1)} fusion(bf16[512,1728]{0,1:T(8,128)(2,1)} %copy-done.38, bf16[512,1152]{1,0:T(8,128)(2,1)} %bitcast.78), kind=kOutput, calls=%fused_computation.2 | convolution fusion | flops 2040422400 | bytes 6930432 | tf_op jit(solution)/shard_map/dot_general | solution.py:38
  217.8 6.6 %copy.60 = bf16[1152,1728]{1,0:T(8,128)(2,1)} copy(bf16[1152,1728]{0,1:T(8,128)(2,1)} %convolution_convert_fusion.2) | data formatting | bytes 7962624 | tf_op jit(solution)/shard_map/convert_element_type | solution.py:1106
  224.4 4.4 %convolution_convert_fusion.1 = bf16[1152,1728]{0,1:T(8,128)(2,1)} fusion(bf16[512,1728]{0,1:T(8,128)(2,1)S(1)} %copy-done.4, bf16[512,1152]{1,0:T(8,128)(2,1)S(1)} %bitcast.80), kind=kOutput, calls=%fused_computation.1 | convolution fusion | flops 2040422400 | bytes 6930432 | tf_op jit(solution)/shard_map/dot_general | solution.py:38
  228.8 6.6 %copy.61 = bf16[1152,1728]{1,0:T(8,128)(2,1)} copy(bf16[1152,1728]{0,1:T(8,128)(2,1)} %convolution_convert_fusion.1) | data formatting | bytes 7962624 | tf_op jit(solution)/shard_map/convert_element_type | solution.py:1106
  235.3 4.4 %convolution_convert_fusion = bf16[1152,1728]{0,1:T(8,128)(2,1)} fusion(bf16[512,1728]{0,1:T(8,128)(2,1)S(1)} %copy-done.40, bf16[512,1152]{1,0:T(8,128)(2,1)S(1)} %bitcast.82), kind=kOutput, calls=%fused_computation | convolution fusion | flops 2040422400 | bytes 6930432 | tf_op jit(solution)/shard_map/dot_general | solution.py:38
  239.7 6.4 %copy.62 = bf16[1152,1728]{1,0:T(8,128)(2,1)} copy(bf16[1152,1728]{0,1:T(8,128)(2,1)} %convolution_convert_fusion) | data formatting | bytes 7962624 | tf_op jit(solution)/shard_map/convert_element_type | solution.py:1106
  246.1 137.5 %tail.1 = (bf16[128,1152]{1,0:T(8,128)(2,1)}, f32[36,1536]{1,0:T(8,128)}, f32[32,1152]{1,0:T(8,128)}, f32[144,1728]{1,0:T(8,128)}, f32[144,1728]{1,0:T(8,128)}, /*index=5*/f32[144,1728]{1,0:T(8,128)}, f32[8,1152]{1,0:T(8,128)}) custom-call(bf16[512,256]{1,0:T(8,128)(2,1)} %bitcast.74, bf16[8,512,256]{2,1,0:T(8,128)(2,1)} %bitcast.69, ...), custom_call_target="tpu_custom_call" | custom-call | tf_op jit(solution)/shard_map/tail/pallas_call | solution.py:923
  383.6 1.7 slice.49
  385.4 1.4 fusion.27
  386.8 0.8 slice.52
  387.6 0.1 constant_dynamic-slice_fusion.1
  387.7 0.5 slice_bitcast_fusion.2
  388.2 0.8 slice.57
  389.0 0.1 constant_dynamic-slice_fusion
  389.0 0.5 slice_bitcast_fusion
  389.6 1.7 copy.69
  391.3 1.6 copy.70
  392.8 2.2 copy.71
  395.1 1.0 copy.72
  396.0 1.0 copy.73
  (101 shorter events, 0.4 us)
Async XLA Ops:
  0.6 4.3 %copy-start.7 = (bf16[128,1152]{1,0:T(8,128)(2,1)S(1)}, bf16[128,1152]{1,0:T(8,128)(2,1)}, u32[]{:S(2)}) copy-start(bf16[128,1152]{1,0:T(8,128)(2,1)} %refs_18_.1) | copy-start | bytes 884740
  0.7 4.3 %copy-start.22 = (f32[1152]{0:T(1024)S(1)}, f32[1152]{0:T(1024)}, u32[]{:S(2)}) copy-start(f32[1152]{0:T(1024)} %param.25) | copy-start | bytes 13828
  0.7 4.1 %copy-start.32 = (f32[256]{0:T(256)S(1)}, f32[256]{0:T(256)}, u32[]{:S(2)}) copy-start(f32[256]{0:T(256)} %param.29) | copy-start | bytes 3076
  0.7 4.3 %copy-start.18 = (bf16[1152,256]{1,0:T(8,128)(2,1)S(1)}, bf16[1152,256]{1,0:T(8,128)(2,1)}, u32[]{:S(2)}) copy-start(bf16[1152,256]{1,0:T(8,128)(2,1)} %param.19) | copy-start | bytes 1769476
  1.9 3.5 copy-start.33
  1.9 3.7 copy-start.28
  4.3 6.1 %copy-start.6 = (f32[128,1024]{1,0:T(8,128)}, f32[128,1024]{1,0:T(8,128)S(1)}, u32[]{:S(2)}) copy-start(f32[128,1024]{1,0:T(8,128)S(1)} %fusion.25.refs_10_) | copy-start | bytes 1572868
  5.4 0.7 copy-start.19
  6.5 1.1 copy-start.16
  6.5 1.1 copy-start.17
  8.2 48.6 %copy-start.1 = (bf16[1024,1152]{1,0:T(8,128)(2,1)S(1)}, bf16[1024,1152]{1,0:T(8,128)(2,1)}, u32[]{:S(2)}) copy-start(bf16[1024,1152]{1,0:T(8,128)(2,1)} %refs_9_.1) | copy-start | bytes 7077892
  55.6 1.9 copy-start.21
  55.6 2.9 copy-start.20
  56.8 31.7 %copy-start.9 = (bf16[128,4,256]{0,2,1:T(8,128)(2,1)}, bf16[128,4,256]{0,2,1:T(8,128)(2,1)S(1)}, u32[]{:S(2)}) copy-start(bf16[128,4,256]{0,2,1:T(8,128)(2,1)S(1)} %copy.58) | copy-start | bytes 786436
  57.5 36.2 %copy-start.34 = (f32[128]{0:T(128)}, f32[128]{0:T(128)S(1)}, u32[]{:S(2)}) copy-start(f32[128]{0:T(128)S(1)} %get-tuple-element.67) | copy-start | bytes 1540
  57.5 36.2 %copy-start.29 = (f32[128]{0:T(128)}, f32[128]{0:T(128)S(1)}, u32[]{:S(2)}) copy-start(f32[128]{0:T(128)S(1)} %fusion.18) | copy-start | bytes 1540
  58.6 142.5 %copy-start.31 = (f32[128]{0:T(128)}, f32[128]{0:T(128)S(1)}, u32[]{:S(2)}) copy-start(f32[128]{0:T(128)S(1)} %fusion.19) | copy-start | bytes 1540
  88.5 5.2 %copy-start = (bf16[1152,1728]{0,1:T(8,128)(2,1)S(1)}, bf16[1152,1728]{0,1:T(8,128)(2,1)}, u32[]{:S(2)}) copy-start(bf16[1152,1728]{0,1:T(8,128)(2,1)} %param.23) | copy-start | bytes 11943940
  88.5 5.2 %copy-start.11 = (bf16[4,128,1152]{2,1,0:T(8,128)(2,1)S(1)}, bf16[4,128,1152]{2,1,0:T(8,128)(2,1)}, u32[]{:S(2)}) copy-start(bf16[4,128,1152]{2,1,0:T(8,128)(2,1)} %line_gather.2) | copy-start | bytes 3538948
  93.7 5.1 %copy-start.41 = (f32[512,1728]{0,1:T(8,128)}, f32[512,1728]{0,1:T(8,128)S(1)}, u32[]{:S(2)}) copy-start(f32[512,1728]{0,1:T(8,128)S(1)} %fusion.28) | copy-start | bytes 10616836
  93.7 5.1 %copy-start.36 = (bf16[1728,1152]{1,0:T(8,128)(2,1)S(1)}, bf16[1728,1152]{1,0:T(8,128)(2,1)}, u32[]{:S(2)}) copy-start(bf16[1728,1152]{1,0:T(8,128)(2,1)} %param.24) | copy-start | bytes 11943940
  98.8 3.6 copy-start.39
  98.8 31.8 %copy-start.8 = (bf16[128,1152]{1,0:T(8,128)(2,1)S(1)}, bf16[128,1152]{1,0:T(8,128)(2,1)}, u32[]{:S(2)}) copy-start(bf16[128,1152]{1,0:T(8,128)(2,1)} %param.31) | copy-start | bytes 884740
  98.8 31.8 %copy-start.24 = (f32[1152]{0:T(1024)S(1)}, f32[1152]{0:T(1024)}, u32[]{:S(2)}) copy-start(f32[1152]{0:T(1024)} %param.28) | copy-start | bytes 13828
  159.9 9.7 %copy-start.37 = (bf16[1152,1728]{0,1:T(8,128)(2,1)S(1)}, bf16[1152,1728]{0,1:T(8,128)(2,1)}, u32[]{:S(2)}) copy-start(bf16[1152,1728]{0,1:T(8,128)(2,1)} %param.22) | copy-start | bytes 11943940
  169.6 2.7 copy-start.38
  169.6 2.7 copy-start.3
  175.9 29.1 %copy-start.35 = (f32[128]{0:T(128)S(1)}, f32[128]{0:T(128)}, u32[]{:S(2)}) copy-start(f32[128]{0:T(128)} %copy-done.34) | copy-start | bytes 1540
  175.9 29.1 %copy-start.30 = (f32[128]{0:T(128)S(1)}, f32[128]{0:T(128)}, u32[]{:S(2)}) copy-start(f32[128]{0:T(128)} %copy-done.29) | copy-start | bytes 1540
  175.9 30.0 %copy-start.10 = (bf16[1152,128]{0,1:T(8,128)(2,1)S(1)}, bf16[1152,128]{0,1:T(8,128)(2,1)}, u32[]{:S(2)}) copy-start(bf16[1152,128]{0,1:T(8,128)(2,1)} %get-tuple-element.52) | copy-start | bytes 884740
  175.9 30.9 %copy-start.2 = (bf16[1152,1024]{1,0:T(8,128)(2,1)S(1)}, bf16[1152,1024]{1,0:T(8,128)(2,1)}, u32[]{:S(2)}) copy-start(bf16[1152,1024]{1,0:T(8,128)(2,1)} %param.18) | copy-start | bytes 7077892
  205.0 5.3 %copy-start.5 = (f32[128,1152]{1,0:T(8,128)}, f32[128,1152]{1,0:T(8,128)S(1)}, u32[]{:S(2)}) copy-start(f32[128,1152]{1,0:T(8,128)S(1)} %get-tuple-element.43.refs_20_) | copy-start | bytes 1769476
  206.8 3.5 copy-start.23
  206.8 4.1 %copy-start.27 = (f32[1152]{0:T(1024)S(1)}, f32[1152]{0:T(1024)}, u32[]{:S(2)}) copy-start(f32[1152]{0:T(1024)} %get-tuple-element.39) | copy-start | bytes 13828
  206.8 4.1 %copy-start.26 = (f32[1152]{0:T(1024)S(1)}, f32[1152]{0:T(1024)}, u32[]{:S(2)}) copy-start(f32[1152]{0:T(1024)} %get-tuple-element.37) | copy-start | bytes 13828
  206.8 4.1 %copy-start.25 = (f32[1152]{0:T(1024)S(1)}, f32[1152]{0:T(1024)}, u32[]{:S(2)}) copy-start(f32[1152]{0:T(1024)} %get-tuple-element.41) | copy-start | bytes 13828
  217.8 6.6 %copy-start.4 = (bf16[512,1728]{0,1:T(8,128)(2,1)S(1)}, bf16[512,1728]{0,1:T(8,128)(2,1)}, u32[]{:S(2)}) copy-start(bf16[512,1728]{0,1:T(8,128)(2,1)} %copy-done.3) | copy-start | bytes 5308420
  217.8 6.6 %copy-start.12 = (bf16[4,128,1152]{2,1,0:T(8,128)(2,1)S(1)}, bf16[4,128,1152]{2,1,0:T(8,128)(2,1)}, u32[]{:S(2)}) copy-start(bf16[4,128,1152]{2,1,0:T(8,128)(2,1)} %line_gather.2) | copy-start | bytes 3538948
  228.8 6.6 %copy-start.13 = (bf16[4,128,1152]{2,1,0:T(8,128)(2,1)S(1)}, bf16[4,128,1152]{2,1,0:T(8,128)(2,1)}, u32[]{:S(2)}) copy-start(bf16[4,128,1152]{2,1,0:T(8,128)(2,1)} %line_gather.3) | copy-start | bytes 3538948
  228.8 6.6 %copy-start.40 = (bf16[512,1728]{0,1:T(8,128)(2,1)S(1)}, bf16[512,1728]{0,1:T(8,128)(2,1)}, u32[]{:S(2)}) copy-start(bf16[512,1728]{0,1:T(8,128)(2,1)} %copy-done.39) | copy-start | bytes 5308420
  383.6 11.5 %copy-start.15 = (f32[144,1728]{1,0:T(8,128)S(1)}, f32[144,1728]{1,0:T(8,128)}, u32[]{:S(2)}) copy-start(f32[144,1728]{1,0:T(8,128)} %get-tuple-element.95) | copy-start | bytes 2985988
  383.6 12.4 %copy-start.14 = (f32[144,1728]{1,0:T(8,128)S(1)}, f32[144,1728]{1,0:T(8,128)}, u32[]{:S(2)}) copy-start(f32[144,1728]{1,0:T(8,128)} %get-tuple-element.35) | copy-start | bytes 2985988

commit v3 on v2

--- a/solution.py
+++ b/solution.py
@@ -972,6 +972,447 @@
     )(*arrays)
 
 
+BLOCK_US, HOP_US = 3.5, 0.8
+WORK_US = {"fa": 2.0, "fb": 1.4, "fc": 2.0, "ga": 0.8, "gb": 0.5, "gc": 2.0, "n": 0.3, "e": 0.4}
+WORK_US.update({"wd": 3.3, "wg": 3.3, "wu": 3.3})
+
+
+def plan(chunks, spans, last, block_us, hop_us, work_us):
+    needs = {}
+    each = chunks // spans
+    for c in range(chunks):
+        p = c // each
+        for k in range(2):
+            for t in range(last):
+                needs["ags", k, c, t] = [("agw", k, c, t - 1)] if t else ([("n", c)] if k else [])
+                needs["agw", k, c, t] = [("ags", k, c, t)]
+                before = ("gc", p) if k else ("fc", p)
+                needs["rss", k, c, t] = [("rsw", k, c, t - 1)] if t else [before]
+                needs["rsw", k, c, t] = [("rss", k, c, t)]
+        needs["n", c] = [("rsw", 0, c, last - 1)]
+        needs["e", c] = [("rsw", 1, c, last - 1)]
+    for p in range(spans):
+        mine = range(p * each, (p + 1) * each)
+        needs["fa", p] = [("agw", 0, c, last - 1) for c in mine]
+        needs["fb", p] = [("fa", p)]
+        needs["fc", p] = [("fb", p)]
+        needs["ga", p] = [("agw", 1, c, last - 1) for c in mine]
+        needs["gb", p] = [("ga", p)]
+        needs["gc", p] = [("gb", p)]
+    needs[("wd",)] = [("ga", p) for p in range(spans)]
+    needs[("wg",)] = [("gb", p) for p in range(spans)] + [("wd",)]
+    needs[("wu",)] = [("wg",)]
+    rank = {"ags": 0, "rss": 0, "agw": 1, "rsw": 1, "n": 2, "e": 3}
+    rank.update({"ga": 4, "gb": 4, "gc": 4, "fa": 5, "fb": 5, "fc": 5, "wd": 6, "wg": 6, "wu": 6})
+    now, link, done, order = 0.0, 0.0, {}, []
+    while len(order) < len(needs):
+        ready = []
+        for event, before in needs.items():
+            if event in done or any(b not in done for b in before):
+                continue
+            at = max([done[b] for b in before], default=0.0)
+            start = max(now, at)
+            if event[0] in ("agw", "rsw") and start <= now + 0.4:
+                start = now
+            ready.append((start, rank[event[0]], event[2:3] or event[1:2], event, at))
+        start, _, _, event, at = min(ready)
+        kind = event[0]
+        now = max(start, at)
+        order.append(event)
+        if kind in ("ags", "rss"):
+            link = max(link, now) + block_us * 2 / 3
+            done[event] = link + block_us / 3 + hop_us
+            now += 0.1
+        elif kind in ("agw", "rsw"):
+            now += 0.1
+            done[event] = now
+        else:
+            now += work_us[kind]
+            done[event] = now
+    return order
+
+
+def ffn_kernel(
+    heads,
+    chunks,
+    spans,
+    proj_ref,
+    x_ref,
+    cot_ref,
+    gain_two_ref,
+    gain_three_ref,
+    gain_four_ref,
+    w_gate_ref,
+    w_up_ref,
+    w_down_ref,
+    o_out,
+    o_hid,
+    o_proj,
+    o_gains,
+    o_gate,
+    o_up,
+    o_down,
+    hidden,
+    w_gate,
+    w_up,
+    w_down,
+    u_all,
+    d_all,
+    by_gate,
+    by_up,
+    act,
+    d_gate,
+    d_up,
+    parts,
+    from_left,
+    from_right,
+    flipped,
+    dw_gate,
+    dw_up,
+    dw_down,
+    ag_send,
+    ag_recv,
+    rs_send,
+    rs_recv,
+    local_sem,
+):
+    f32, bf16 = jnp.float32, jnp.bfloat16
+    s, h = place()
+    last = heads - 1
+    right = (s, lax.rem(h + 1, heads))
+    left = (s, lax.rem(h + last, heads))
+    rows, model = x_ref.shape
+    units = w_gate.shape[0]
+    rc = rows // chunks
+    each = chunks // spans
+    many = rc * heads * each
+    tile = 256
+    whole_tiles, rest = units // tile, units % tile
+
+    loads = []
+    for n, (src, dst) in enumerate(
+        ((w_gate_ref, w_gate), (w_up_ref, w_up), (w_down_ref, w_down))
+    ):
+        copy = pltpu.make_async_copy(src, dst, local_sem.at[n])
+        copy.start()
+        loads.append(copy)
+    greet([right, left])
+
+    proj = proj_ref[...]
+    hid = x_ref[...].astype(f32) + norm_rows(proj, gain_two_ref[...])
+    hidden[...] = hid
+    u_local = norm_rows(hid, gain_three_ref[...]).astype(bf16)
+    for c in range(chunks):
+        u_all[c, h] = u_local[c * rc : (c + 1) * rc]
+    o_gains[...] = jnp.zeros_like(o_gains)
+
+    def lanes(k, c, t):
+        buf = d_all if k else u_all
+        return (
+            (
+                (h - t >= 0) & (h < last),
+                buf.at[c, jnp.maximum(h - t, 0)],
+                0,
+                right,
+                h - 1 - t >= 0,
+                buf.at[c, jnp.maximum(h - 1 - t, 0)],
+            ),
+            (
+                (h + t <= last) & (h > 0),
+                buf.at[c, jnp.minimum(h + t, last)],
+                1,
+                left,
+                h + 1 + t <= last,
+                buf.at[c, jnp.minimum(h + 1 + t, last)],
+            ),
+        )
+
+    def ags(k, c, t):
+        for on, block, lane, target, _, _ in lanes(k, c, t):
+            i = (k, c, lane, t)
+            pl.when(on)(remote(block, block, ag_send.at[i], ag_recv.at[i], target).start)
+
+    def agw(k, c, t):
+        for _, _, lane, target, on, block in lanes(k, c, t):
+            i = (k, c, lane, t)
+            pl.when(on)(remote(block, block, ag_send.at[i], ag_recv.at[i], target).wait_recv)
+
+    def rss(k, c, t):
+        for on, dest, box, lane, target, at_end in (
+            ((t >= h) & (h < last), last - (t - h), from_left, 0, right, h == 0),
+            ((t >= last - h) & (h > 0), t - (last - h), from_right, 1, left, h == last),
+        ):
+            dest = jnp.clip(dest, 0, last)
+            i = (k, c, lane, t)
+            if t > 0:
+
+                def forward(box=box, dest=dest, i=i, target=target):
+                    box[k, c, t - 1] = box[k, c, t - 1] + parts[k, c, dest]
+                    remote(
+                        box.at[k, c, t - 1], box.at[k, c, t], rs_send.at[i], rs_recv.at[i], target
+                    ).start()
+
+                pl.when(on & jnp.logical_not(at_end))(forward)
+            pl.when(on & at_end)(
+                remote(
+                    parts.at[k, c, dest], box.at[k, c, t], rs_send.at[i], rs_recv.at[i], target
+                ).start
+            )
+
+    def rsw(k, c, t):
+        for on, box, lane, target in (
+            ((t >= h - 1) & (h > 0), from_left, 0, right),
+            ((t >= last - h - 1) & (h < last), from_right, 1, left),
+        ):
+            i = (k, c, lane, t)
+            block = box.at[k, c, t]
+            pl.when(on)(remote(block, block, rs_send.at[i], rs_recv.at[i], target).wait_recv)
+
+    def summed(k, c):
+        zero = jnp.zeros((rc, model), f32)
+        return (
+            parts[k, c, h].astype(f32)
+            + jnp.where(h > 0, from_left[k, c, last - 1].astype(f32), zero)
+            + jnp.where(h < last, from_right[k, c, last - 1].astype(f32), zero)
+        )
+
+    def over_tiles(lo, hi, body):
+        def step(i, carry):
+            body(pl.ds(pl.multiple_of(i * tile, tile), tile))
+            return carry
+
+        lax.fori_loop(lo, hi, step, 0)
+        if hi == whole_tiles and rest:
+            body(pl.ds(whole_tiles * tile, rest))
+
+    arrived = set()
+
+    def need(n):
+        if n not in arrived:
+            arrived.add(n)
+            loads[n].wait()
+
+    def held(buf, p):
+        return buf[pl.ds(p * each, each)].reshape(many, model)
+
+    def place_parts(k, p, cols, value):
+        parts[k, pl.ds(p * each, each), :, :, cols] = value.astype(bf16).reshape(
+            each, heads, rc, value.shape[1]
+        )
+
+    def forward_tiles(c, lo, hi):
+        need(0)
+        need(1)
+
+        def body(cols):
+            u = held(u_all, c)
+            gate = contract_last(u, w_gate[cols, :])
+            up = contract_last(u, w_up[cols, :])
+            root = math.sqrt(2.0 / math.pi)
+            square = gate * gate
+            curve = jnp.tanh(root * gate * (1.0 + 0.044715 * square))
+            half = 0.5 * (1.0 + curve)
+            gelu = gate * half
+            slope = half + 0.5 * gate * (1.0 - curve * curve) * (
+                root * (1.0 + 3 * 0.044715 * square)
+            )
+            by_gate[pl.ds(c * many, many), cols] = slope * up
+            by_up[pl.ds(c * many, many), cols] = gelu
+            act[pl.ds(c * many, many), cols] = (gelu * up).astype(bf16)
+
+        over_tiles(lo, hi, body)
+
+    out_tile = model // 3
+
+    def down_rows(c):
+        need(2)
+
+        def body(i, carry):
+            cols = pl.ds(pl.multiple_of(i * out_tile, out_tile), out_tile)
+            part = jnp.dot(
+                act[pl.ds(c * many, many), :], w_down[:, cols], preferred_element_type=f32
+            )
+            place_parts(0, c, cols, part)
+            return carry
+
+        lax.fori_loop(0, 3, body, 0)
+
+    def turn(c):
+        here = pl.ds(c * rc, rc)
+        ffn_out = summed(0, c)
+        upstream = cot_ref[here, :].astype(f32)
+        o_out[here, :] = (hidden[here, :] + norm_rows(ffn_out, gain_four_ref[...])).astype(
+            o_out.dtype
+        )
+        d_out, terms = back_norm(ffn_out, gain_four_ref[...], upstream)
+        d_all[c, h] = d_out.astype(bf16)
+        o_gains[3:4, :] += terms
+
+    def back_tiles(c, lo, hi):
+        def body(cols):
+            d_act = contract_last(held(d_all, c), w_down[cols, :])
+            d_gate[pl.ds(c * many, many), cols] = (
+                d_act * by_gate[pl.ds(c * many, many), cols]
+            ).astype(bf16)
+            d_up[pl.ds(c * many, many), cols] = (
+                d_act * by_up[pl.ds(c * many, many), cols]
+            ).astype(bf16)
+
+        over_tiles(lo, hi, body)
+
+    def back_rows(c):
+        def body(i, carry):
+            cols = pl.ds(pl.multiple_of(i * out_tile, out_tile), out_tile)
+            part = jnp.dot(
+                d_gate[pl.ds(c * many, many), :], w_gate[:, cols], preferred_element_type=f32
+            )
+            part = part + jnp.dot(
+                d_up[pl.ds(c * many, many), :], w_up[:, cols], preferred_element_type=f32
+            )
+            place_parts(1, c, cols, part)
+            return carry
+
+        lax.fori_loop(0, 3, body, 0)
+
+    def finish_rows(c):
+        here = pl.ds(c * rc, rc)
+        d_in, terms = back_norm(hidden[here, :], gain_three_ref[...], summed(1, c))
+        o_gains[2:3, :] += terms
+        d_hid = cot_ref[here, :].astype(f32) + d_in
+        o_hid[here, :] = d_hid
+        d_proj, terms = back_norm(proj_ref[here, :], gain_two_ref[...], d_hid)
+        o_proj[here, :] = d_proj.astype(o_proj.dtype)
+        o_gains[1:2, :] += terms
+
+    stores = []
+
+    def flip(source):
+        for p in range(spans):
+            flipped[:, pl.ds(p * many, many)] = held(source, p).T
+
+    def weight_grad(right_ref, dst, out, n):
+        def body(cols):
+            value = jnp.dot(flipped[...], right_ref[:, cols], preferred_element_type=f32)
+            dst[:, :, cols] = value.astype(bf16).reshape(dst.shape[:2] + (value.shape[1],))
+
+        over_tiles(0, whole_tiles, body)
+        copy = pltpu.make_async_copy(dst, out, local_sem.at[n])
+        copy.start()
+        stores.append(copy)
+
+    half_tiles = (whole_tiles + 1) // 2
+    events = plan(chunks, spans, last, BLOCK_US / chunks, HOP_US, WORK_US)
+    for event in events:
+        kind, args = event[0], event[1:]
+        if kind == "ags":
+            ags(*args)
+        elif kind == "agw":
+            agw(*args)
+        elif kind == "rss":
+            rss(*args)
+        elif kind == "rsw":
+            rsw(*args)
+        elif kind == "fa":
+            forward_tiles(args[0], 0, half_tiles)
+        elif kind == "fb":
+            forward_tiles(args[0], half_tiles, whole_tiles)
+        elif kind == "fc":
+            down_rows(args[0])
+        elif kind == "n":
+            turn(args[0])
+        elif kind == "ga":
+            back_tiles(args[0], 0, half_tiles)
+        elif kind == "gb":
+            back_tiles(args[0], half_tiles, whole_tiles)
+        elif kind == "gc":
+            back_rows(args[0])
+        elif kind == "e":
+            finish_rows(args[0])
+        elif kind == "wd":
+            flip(d_all)
+            weight_grad(act, dw_down, o_down, 3)
+        elif kind == "wg":
+            flip(u_all)
+            weight_grad(d_gate, dw_gate, o_gate, 4)
+        else:
+            weight_grad(d_up, dw_up, o_up, 5)
+
+    for event in events:
+        if event[0] == "ags":
+            k, c, t = event[1:]
+            for on, block, lane, target, _, _ in lanes(k, c, t):
+                i = (k, c, lane, t)
+                pl.when(on)(remote(block, block, ag_send.at[i], ag_recv.at[i], target).wait_send)
+        elif event[0] == "rss":
+            k, c, t = event[1:]
+            for on, box, lane, target in (
+                ((t >= h) & (h < last), from_left, 0, right),
+                ((t >= last - h) & (h > 0), from_right, 1, left),
+            ):
+                i = (k, c, lane, t)
+                block = box.at[k, c, t]
+                pl.when(on)(remote(block, block, rs_send.at[i], rs_recv.at[i], target).wait_send)
+    for n in range(3):
+        need(n)
+    for copy in stores:
+        copy.wait()
+
+
+def feed_forward(nseq, heads, chunks, spans, cid, proj, x, cot, gains, w_gate, w_up, w_down):
+    f32, bf16 = jnp.float32, jnp.bfloat16
+    rows, model = x.shape
+    units = w_gate.shape[0]
+    rc = rows // chunks
+    group = rows * heads
+    vm = pl.BlockSpec(memory_space=VMEM)
+    anywhere = pl.BlockSpec(memory_space=pl.ANY)
+    grad = jax.ShapeDtypeStruct((nseq, model // nseq, units), bf16)
+    hops = (2, chunks, 2, heads - 1)
+    return pl.pallas_call(
+        functools.partial(ffn_kernel, heads, chunks, spans),
+        out_shape=[
+            jax.ShapeDtypeStruct((rows, model), bf16),
+            jax.ShapeDtypeStruct((rows, model), f32),
+            jax.ShapeDtypeStruct((rows, model), bf16),
+            jax.ShapeDtypeStruct((8, model), f32),
+            grad,
+            grad,
+            grad,
+        ],
+        in_specs=[vm] * 6 + [anywhere] * 3,
+        out_specs=[vm] * 4 + [anywhere] * 3,
+        scratch_shapes=[
+            VMEM((rows, model), f32),
+            VMEM(w_gate.shape, bf16),
+            VMEM(w_up.shape, bf16),
+            VMEM(w_down.shape, bf16),
+            VMEM((chunks, heads, rc, model), bf16),
+            VMEM((chunks, heads, rc, model), bf16),
+            VMEM((group, units), f32),
+            VMEM((group, units), f32),
+            VMEM((group, units), bf16),
+            VMEM((group, units), bf16),
+            VMEM((group, units), bf16),
+            VMEM((2, chunks, heads, rc, model), bf16),
+            VMEM((2, chunks, heads - 1, rc, model), bf16),
+            VMEM((2, chunks, heads - 1, rc, model), bf16),
+            VMEM((model, group), bf16),
+            VMEM(grad.shape, bf16),
+            VMEM(grad.shape, bf16),
+            VMEM(grad.shape, bf16),
+            pltpu.SemaphoreType.DMA(hops),
+            pltpu.SemaphoreType.DMA(hops),
+            pltpu.SemaphoreType.DMA(hops),
+            pltpu.SemaphoreType.DMA(hops),
+            pltpu.SemaphoreType.DMA((6,)),
+        ],
+        name="feed_forward",
+        compiler_params=pltpu.CompilerParams(
+            collective_id=cid, has_side_effects=True, vmem_limit_bytes=62 * 2**20
+        ),
+    )(proj, x, cot, *[g[None] for g in gains], w_gate, w_up, w_down)
+
+
 def local(
     tokens,
     segment_ids,
@@ -1050,6 +1491,74 @@
     attended = attended_t.T
     mixed_local = unstacked(attended.astype(bf16))
     projected = jnp.dot(mixed_local, w_out, preferred_element_type=jnp.float32)
+    if nseq <= 8 and (model // nseq) % 16 == 0:
+        qw = qcount * width
+        each, few = model // (nseq * heads), width // (nseq * heads)
+        output, d_hidden, d_projected, gains, *blocks = feed_forward(
+            nseq,
+            heads,
+            4,
+            2,
+            10,
+            projected,
+            tokens,
+            cotangent,
+            (gain_attn_out, gain_ffn_in, gain_ffn_out),
+            w_gate.T,
+            w_up.T,
+            w_down,
+        )
+        w_qkv = jnp.concatenate([w_query, w_key, w_value], axis=1)
+        grad_tokens, sum_qkv, sum_out, sum_gate, sum_up, sum_down, sum_gains = tail(
+            nseq,
+            heads,
+            qcount,
+            scale,
+            9,
+            queries,
+            keys,
+            values,
+            starts,
+            index,
+            log_total,
+            attended_t,
+            mixed_local.T.reshape(nseq, -1, local_rows),
+            d_projected,
+            w_out,
+            q_linear,
+            k_linear,
+            cosines,
+            sines,
+            gain_query[None],
+            gain_key[None],
+            attn_in.T.reshape(nseq, -1, local_rows),
+            w_qkv,
+            tokens,
+            gain_attn_in[None],
+            d_hidden,
+            gains,
+            *blocks,
+        )
+        which = seq_index * heads + head_index
+        wide = lax.dynamic_slice_in_dim(sum_gains[:4], which * each, each, 1)
+        narrow = lax.dynamic_slice_in_dim(sum_gains[4:6], which * few, few, 1)
+        return (
+            output,
+            grad_tokens,
+            sum_qkv[:, :qw],
+            sum_qkv[:, qw : qw + width],
+            sum_qkv[:, qw + width :],
+            sum_out,
+            sum_gate,
+            sum_up,
+            sum_down.T,
+            wide[0],
+            wide[1],
+            wide[2],
+            wide[3],
+            narrow[0],
+            narrow[1],
+        )
     hidden = inputs + norm_rows(projected, gain_attn_out)
     ffn_in = norm_rows(hidden, gain_ffn_in).astype(bf16)
     ffn_rows = line_gather(ffn_in, heads, 2).reshape(group, model)
@@ -1090,72 +1599,6 @@
     d_projected, d_gain_two = back_two(d_hidden)
     d_projected = d_projected.astype(bf16)
     qw = qcount * width
-    each, few = model // (nseq * heads), width // (nseq * heads)
-    if nseq <= 8:
-        gains = jnp.concatenate(
-            [
-                jnp.zeros((1, model), jnp.float32),
-                d_gain_two[None],
-                d_gain_three[None],
-                d_gain_four[None],
-                jnp.zeros((4, model), jnp.float32),
-            ]
-        )
-        w_qkv = jnp.concatenate([w_query, w_key, w_value], axis=1)
-        blocks = [
-            d.astype(bf16).reshape(nseq, model // nseq, hidden_units)
-            for d in (d_w_gate, d_w_up, d_w_down)
-        ]
-        grad_tokens, sum_qkv, sum_out, sum_gate, sum_up, sum_down, sum_gains = tail(
-            nseq,
-            heads,
-            qcount,
-            scale,
-            9,
-            queries,
-            keys,
-            values,
-            starts,
-            index,
-            log_total,
-            attended_t,
-            mixed_local.T.reshape(nseq, -1, local_rows),
-            d_projected,
-            w_out,
-            q_linear,
-            k_linear,
-            cosines,
-            sines,
-            gain_query[None],
-            gain_key[None],
-            attn_in.T.reshape(nseq, -1, local_rows),
-            w_qkv,
-            tokens,
-            gain_attn_in[None],
-            d_hidden,
-            gains,
-            *blocks,
-        )
-        which = seq_index * heads + head_index
-        wide = lax.dynamic_slice_in_dim(sum_gains[:4], which * each, each, 1)
-        narrow = lax.dynamic_slice_in_dim(sum_gains[4:6], which * few, few, 1)
-        return (
-            output.astype(bf16),
-            grad_tokens,
-            sum_qkv[:, :qw],
-            sum_qkv[:, qw : qw + width],
-            sum_qkv[:, qw + width :],
-            sum_out,
-            sum_gate,
-            sum_up,
-            sum_down.T,
-            wide[0],
-            wide[1],
-            wide[2],
-            wide[3],
-            narrow[0],
-            narrow[1],
-        )
     d_w_out = contract_first(mixed_local, d_projected)
     d_mixed = contract_last(d_projected, w_out).astype(bf16)
     grad_attended = stacked(d_mixed)

time: 402 us -> 314 us (0.78); the launches traced: 397 us -> 314 us
  matrix products: 50.1 us -> 6.23 us
  local copies, waits for them, and re-layouts: 37.6 us -> 20.3 us
  other arithmetic: 20 us -> 7.86 us
  Pallas kernels: 288 us -> 278 us
    dot_general x9 -> x0, matrix products: 44.6 us -> none  [the longest x3 15.9 us: contract_last(): lax.dot_general(left, right, (((1,), (1,)), ((), ())), preferred_element_...]
    convert_element_type x3 -> x0, local copies, waits for them, and re-layouts: 19.6 us -> none  [local(): d.astype(bf16).reshape(nseq, model // nseq, hidden_units)]
    pallas_call x4 -> x1, Pallas kernels: 106 us -> 96.6 us  [feed_forward(): pl.pallas_call(functools.partial(ffn_kernel, heads, chunks, spans), out_s...]
    reduce_sum x7 -> x2, other arithmetic: 9.36 us -> 1.39 us  [norm_rows(): return v * lax.rsqrt(jnp.mean(v * v, axis=-1, keepdims=True) + EPS) * gain]
    unnamed x89 -> x48, local copies, waits for them, and re-layouts: 7.63 us -> 8.9 us
where the time goes in v3:
time: 314 us
  Pallas kernels  278 us (89%)
  local copies, waits for them, and re-layouts  20.3 us (6%)
  other arithmetic  7.86 us (3%)
  matrix products  6.23 us (2%)
    pallas_call x1, Pallas kernels, tail(): pl.pallas_call(kernel, out_shape=[jax.ShapeDtypeStruct((rows, model), bf1...  138 us
    pallas_call x1, Pallas kernels, feed_forward(): pl.pallas_call(functools.partial(ffn_kernel, heads, chunks, spans), out_s...  96.6 us
    pallas_call x1, Pallas kernels, gather_all(): pl.pallas_call(kernel, out_shape=[jax.ShapeDtypeStruct((nseq, heads) + a....  39.7 us
    unnamed x48, local copies, waits for them, and re-layouts  8.9 us

profile of v3, /device:TPU:0, one launch (start us, length us, event | category | flops | bytes accessed | tf_op | source)
XLA Modules:
  0.0 313.7 jit_solution(12288477497210952572)
XLA Ops:
  0.6 0.0 copy-start.1
  0.7 0.0 copy-start.14
  0.7 0.0 copy-start.19
  0.7 0.0 copy-start.9
  0.7 1.2 fusion
  1.9 0.0 copy-start.15
  1.9 2.4 fusion.8.refs_10_
  4.3 0.0 copy-start.3
  4.3 0.2 reshape.150
  4.5 0.2 multiply_reduce_fusion
  4.8 0.0 copy-done.19
  4.8 0.2 multiply_multiply_fusion
  5.0 0.0 copy-done.1
  5.0 0.0 copy-done.14
  5.0 0.0 copy-done.9
  5.0 0.4 multiply_reduce_fusion.1
  5.4 0.0 copy-start.12
  5.4 0.6 copy-done.12
  6.1 0.0 copy-done.20
  6.1 0.1 multiply_multiply_fusion.1
  6.2 0.1 dynamic_slice.9
  6.3 0.5 select_reduce_fusion
  6.8 0.3 subtract_convert_fusion.1
  7.1 0.1 subtract_convert_fusion
  7.3 0.2 fusion.3
  7.4 0.7 copy.42
  8.2 0.6 pad_maximum_fusion.1.refs_0_
  8.8 2.1 convolution_convert_fusion.refs_1_
  11.0 39.7 %gather_all.1 = (bf16[8,4,128,256]{3,2,1,0:T(8,128)(2,1)}, bf16[8,4,128,256]{3,2,1,0:T(8,128)(2,1)}) custom-call(bf16[128,256]{1,0:T(8,128)(2,1)} %pad_maximum_fusion.1.refs_0_, bf16[128,256]{1,0:T(8,128)(2,1)} %convolution_convert_fusion.refs_1_), custom_call_target="tpu_custom_call" | custom-call | tf_op jit(solution)/shard_map/gather_all/pallas_call | solution.py:146
  50.6 0.5 tile.4
  51.2 0.6 tile.5
  51.7 3.9 %attend.1 = (f32[256,512]{1,0:T(8,128)}, f32[1,512]{1,0:T(1,128)}) custom-call(bf16[512,256]{1,0:T(8,128)(2,1)} %bitcast.48, bf16[8,512,256]{2,1,0:T(8,128)(2,1)} %bitcast.42, bf16[8,512,256]{2,1,0:T(8,128)(2,1)} %bitcast.44, s32[1,512]{1,0:T(1,128)} %bitcast.55, s32[1,512]{1,0:T(1,128)} %bitcast.57), custom_call_target="tpu_custom_call" | custom-call | tf_op jit(solution)/shard_map/attend/pallas_call | solution.py:457
  55.7 0.0 copy-start.16
  55.7 0.0 copy-start.17
  55.7 0.0 copy-start.18
  55.7 1.1 convert_bitcast_fusion
  56.8 0.1 reshape.153
  56.9 1.4 fusion.11.proj_ref
  58.3 0.6 broadcast_in_dim.26.gain_two_ref
  58.9 0.6 broadcast_in_dim.46.gain_three_ref
  59.5 0.6 broadcast_in_dim.47.gain_four_ref
  60.1 96.6 %feed_forward.1 = (bf16[128,1152]{1,0:T(8,128)(2,1)}, f32[128,1152]{1,0:T(8,128)}, bf16[128,1152]{1,0:T(8,128)(2,1)}, f32[8,1152]{1,0:T(8,128)}, bf16[8,144,1728...) custom-call(f32[128,1152]{1,0:T(8,128)} %fusion.11.proj_ref, ...), custom_call_target="tpu_custom_call" | custom-call | tf_op jit(solution)/shard_map/feed_forward/pallas_call | solution.py:1371
  156.7 0.0 copy-done.4
  156.7 0.0 copy-done.2
  156.7 0.1 fusion.4
  156.9 0.9 copy.44
  157.8 0.0 copy-done.11
  157.8 3.2 %pad_maximum_fusion.refs_17_ = bf16[1152,1536]{1,0:T(8,128)(2,1)} fusion(bf16[1152,256]{1,0:T(8,128)(2,1)S(1)} %copy-done.11, bf16[1152,256]{1,0:T(8,128)(2,1)S(1)} %copy-done.10, bf16[1152,1024]{1,0:T(8,128)(2,1)} %param.18), kind=kLoop, calls=%fused_computation | loop fusion | flops 10616832 | bytes 7077888 | tf_op jit(solution)/shard_map/concatenate | solution.py:1511
  160.9 0.6 broadcast_in_dim.50.refs_19_
  161.5 138.0 %tail.1 = (bf16[128,1152]{1,0:T(8,128)(2,1)}, f32[36,1536]{1,0:T(8,128)}, f32[32,1152]{1,0:T(8,128)}, f32[144,1728]{1,0:T(8,128)}, f32[144,1728]{1,0:T(8,128)}, /*index=5*/f32[144,1728]{1,0:T(8,128)}, f32[8,1152]{1,0:T(8,128)}) custom-call(bf16[512,256]{1,0:T(8,128)(2,1)} %bitcast.49, bf16[8,512,256]{2,1,0:T(8,128)(2,1)} %bitcast.43, ...), custom_call_target="tpu_custom_call" | custom-call | tf_op jit(solution)/shard_map/tail/pallas_call | solution.py:923
  299.6 1.7 slice.49
  301.3 1.4 fusion.10
  302.8 0.8 slice.52
  303.5 0.1 constant_dynamic-slice_fusion.1
  303.6 0.5 slice_bitcast_fusion.2
  304.1 0.8 slice.57
  304.9 0.1 constant_dynamic-slice_fusion
  305.0 0.5 slice_bitcast_fusion
  305.5 0.7 copy.52
  306.2 1.7 copy.53
  307.9 1.6 copy.54
  309.5 2.2 copy.55
  311.7 1.0 copy.56
  312.7 1.0 copy.57
  (29 shorter events, 0.1 us)
Async XLA Ops:
  0.6 4.3 %copy-start.1 = (bf16[128,1152]{1,0:T(8,128)(2,1)S(1)}, bf16[128,1152]{1,0:T(8,128)(2,1)}, u32[]{:S(2)}) copy-start(bf16[128,1152]{1,0:T(8,128)(2,1)} %refs_18_.1) | copy-start | bytes 884740
  0.7 4.3 %copy-start.14 = (f32[1152]{0:T(1024)S(1)}, f32[1152]{0:T(1024)}, u32[]{:S(2)}) copy-start(f32[1152]{0:T(1024)} %param.25) | copy-start | bytes 13828
  0.7 4.1 %copy-start.19 = (f32[256]{0:T(256)S(1)}, f32[256]{0:T(256)}, u32[]{:S(2)}) copy-start(f32[256]{0:T(256)} %param.29) | copy-start | bytes 3076
  0.7 4.3 %copy-start.9 = (bf16[1152,256]{1,0:T(8,128)(2,1)S(1)}, bf16[1152,256]{1,0:T(8,128)(2,1)}, u32[]{:S(2)}) copy-start(bf16[1152,256]{1,0:T(8,128)(2,1)} %param.19) | copy-start | bytes 1769476
  1.9 4.2 %copy-start.20 = (f32[256]{0:T(256)S(1)}, f32[256]{0:T(256)}, u32[]{:S(2)}) copy-start(f32[256]{0:T(256)} %param.30) | copy-start | bytes 3076
  1.9 4.3 %copy-start.15 = (s32[4096]{0:T(1024)S(1)}, s32[4096]{0:T(1024)}, u32[]{:S(2)}) copy-start(s32[4096]{0:T(1024)} %param.17) | copy-start | bytes 49156
  4.3 6.7 %copy-start.3 = (f32[128,1024]{1,0:T(8,128)}, f32[128,1024]{1,0:T(8,128)S(1)}, u32[]{:S(2)}) copy-start(f32[128,1024]{1,0:T(8,128)S(1)} %fusion.8.refs_10_) | copy-start | bytes 1572868
  5.4 0.7 copy-start.12
  7.1 48.5 %copy-start.7 = (f32[128,128]{1,0:T(8,128)}, f32[128,128]{1,0:T(8,128)S(1)}, u32[]{:S(2)}) copy-start(f32[128,128]{1,0:T(8,128)S(1)} %get-tuple-element.63.refs_13_) | copy-start | bytes 196612
  7.1 48.5 %copy-start.8 = (f32[128,128]{1,0:T(8,128)}, f32[128,128]{1,0:T(8,128)S(1)}, u32[]{:S(2)}) copy-start(f32[128,128]{1,0:T(8,128)S(1)} %get-tuple-element.64.refs_12_) | copy-start | bytes 196612
  8.8 48.1 %copy-start = (bf16[1024,1152]{1,0:T(8,128)(2,1)S(1)}, bf16[1024,1152]{1,0:T(8,128)(2,1)}, u32[]{:S(2)}) copy-start(bf16[1024,1152]{1,0:T(8,128)(2,1)} %refs_9_.1) | copy-start | bytes 7077892
  55.7 2.6 copy-start.16
  55.7 3.2 %copy-start.17 = (f32[1152]{0:T(1024)S(1)}, f32[1152]{0:T(1024)}, u32[]{:S(2)}) copy-start(f32[1152]{0:T(1024)} %param.27) | copy-start | bytes 13828
  55.7 3.8 %copy-start.18 = (f32[1152]{0:T(1024)S(1)}, f32[1152]{0:T(1024)}, u32[]{:S(2)}) copy-start(f32[1152]{0:T(1024)} %param.28) | copy-start | bytes 13828
  56.9 99.8 %copy-start.4 = (bf16[128,4,256]{0,2,1:T(8,128)(2,1)}, bf16[128,4,256]{0,2,1:T(8,128)(2,1)S(1)}, u32[]{:S(2)}) copy-start(bf16[128,4,256]{0,2,1:T(8,128)(2,1)S(1)} %copy.43) | copy-start | bytes 786436
  60.1 96.7 %copy-start.2 = (bf16[128,1152]{1,0:T(8,128)(2,1)S(1)}, bf16[128,1152]{1,0:T(8,128)(2,1)}, u32[]{:S(2)}) copy-start(bf16[128,1152]{1,0:T(8,128)(2,1)} %refs_18_.1) | copy-start | bytes 884740
  60.1 97.7 %copy-start.10 = (bf16[1152,256]{1,0:T(8,128)(2,1)S(1)}, bf16[1152,256]{1,0:T(8,128)(2,1)}, u32[]{:S(2)}) copy-start(bf16[1152,256]{1,0:T(8,128)(2,1)} %param.19) | copy-start | bytes 1769476
  60.1 97.7 %copy-start.11 = (bf16[1152,256]{1,0:T(8,128)(2,1)S(1)}, bf16[1152,256]{1,0:T(8,128)(2,1)}, u32[]{:S(2)}) copy-start(bf16[1152,256]{1,0:T(8,128)(2,1)} %param.20) | copy-start | bytes 1769476
  161.5 144.0 %copy-start.13 = (bf16[128,1152]{1,0:T(8,128)(2,1)S(1)}, bf16[128,1152]{1,0:T(8,128)(2,1)}, u32[]{:S(2)}) copy-start(bf16[128,1152]{1,0:T(8,128)(2,1)} %get-tuple-element.84) | copy-start | bytes 884740
  299.6 12.2 %copy-start.6 = (f32[144,1728]{1,0:T(8,128)S(1)}, f32[144,1728]{1,0:T(8,128)}, u32[]{:S(2)}) copy-start(f32[144,1728]{1,0:T(8,128)} %get-tuple-element.91) | copy-start | bytes 2985988
  299.6 13.1 %copy-start.5 = (f32[144,1728]{1,0:T(8,128)S(1)}, f32[144,1728]{1,0:T(8,128)}, u32[]{:S(2)}) copy-start(f32[144,1728]{1,0:T(8,128)} %get-tuple-element.49) | copy-start | bytes 2985988

commit v4 on v3

--- a/solution.py
+++ b/solution.py
@@ -1,4 +1,5 @@
 import functools
+import itertools
 import math
 
 import jax
@@ -526,7 +527,6 @@
 class Sum:
     def __init__(self, links, part, boxes, order):
         self.links, self.part, self.boxes, self.order = links, part, boxes, order
-        self.stage = 0
         self.used = 0
         self.slot = {}
         self.waiting = {}
@@ -536,32 +536,50 @@
             return self.boxes.at[self.slot[mask]]
         return self.part(mask)
 
-    def launch(self):
-        bit = self.order[self.stage]
-        rest = self.order[self.stage + 1 :]
-        target = self.links.across(bit)
-        after = 1 << rest[0] if rest else 0
-        for mask in sorted(subsets(rest), key=lambda m: 0 if m & after else 1):
-            where = self.used
-            self.used += 1
-            copy = self.links.go(self.current(mask | (1 << bit)), self.boxes.at[where], target)
-            self.waiting[mask] = (copy, where)
-        self.stage += 1
-
-    def settle(self, kept=None):
-        for mask in list(self.waiting):
-            copy, where = self.waiting.pop(mask)
+    def masks(self, stage):
+        rest = self.order[stage + 1 :]
+        weight = lambda m: sum(1 << (len(rest) - i) for i, b in enumerate(rest) if m >> b & 1)
+        return sorted(subsets(rest), key=weight, reverse=True)
+
+    def send(self, stage, mask):
+        bit = self.order[stage]
+        where = self.used
+        self.used += 1
+        copy = self.links.go(
+            self.current(mask | (1 << bit)), self.boxes.at[where], self.links.across(bit)
+        )
+        self.waiting[stage, mask] = (copy, where)
+
+    def start(self):
+        for mask in self.masks(0):
+            self.send(0, mask)
+
+    def steps(self, stage, kept=None):
+        def step(mask):
+            copy, where = self.waiting.pop((stage, mask))
             mine = kept(mask) if kept is not None else self.current(mask)
             copy.wait_recv()
             self.boxes[where] = self.boxes[where] + mine[...]
             self.slot[mask] = where
+            if stage + 1 < len(self.order):
+                bit = 1 << self.order[stage + 1]
+                if mask & bit:
+                    self.send(stage + 1, mask & ~bit)
+
+        return [functools.partial(step, mask) for mask in self.masks(stage)]
 
     def last(self, kept=None):
-        ((mask, (copy, where)),) = self.waiting.items()
-        self.waiting = {}
-        mine = kept(mask) if kept is not None else self.current(mask)
+        copy, where = self.waiting.pop((len(self.order) - 1, 0))
+        mine = kept(0) if kept is not None else self.current(0)
         copy.wait_recv()
         return self.boxes[where].astype(jnp.float32) + mine[...].astype(jnp.float32)
+
+
+def in_turn(*lists):
+    for group in itertools.zip_longest(*lists):
+        for step in group:
+            if step is not None:
+                step()
 
 
 class Links:
@@ -618,8 +636,6 @@
     qcount,
     scale,
     q_ref,
-    k_ref,
-    v_ref,
     start_ref,
     index_ref,
     log_ref,
@@ -634,11 +650,13 @@
     gain_q_ref,
     gain_k_ref,
     attn_t_ref,
-    w_qkv_ref,
     x_ref,
     gain_in_ref,
     d_hid_ref,
     gains_ref,
+    k_far,
+    v_far,
+    w_qkv_far,
     d_gate_ref,
     d_up_ref,
     d_down_ref,
@@ -649,6 +667,9 @@
     o_up,
     o_down,
     o_gains,
+    k_ref,
+    v_ref,
+    w_qkv_ref,
     dk,
     dv,
     dq_t,
@@ -660,21 +681,22 @@
     zbox_v,
     dw_out,
     box_out,
-    zsrc_out,
     zbox_out,
-    dw_a,
-    dw_b,
-    box_a,
-    box_b,
+    mid_out,
+    end_out,
+    dw_qkv,
+    box_qkv,
     zsrc_qkv,
     zbox_qkv,
     d_qkv,
     keep_gate,
     keep_up,
-    keep_down,
+    keep_first,
+    keep_second,
     box_gate,
     box_up,
-    box_down,
+    box_first,
+    box_second,
     gsum,
     gbox,
     gzbox,
@@ -690,46 +712,73 @@
     rows = d_proj_ref.shape[0]
     width = gain_q_ref.shape[1]
     groups, span = k_ref.shape[:2]
+    loads = []
+
+    def load(src, dst):
+        copy = pltpu.make_async_copy(src, dst, local_sem.at[len(loads)])
+        copy.start()
+        loads.append(copy)
+        return copy
+
+    load_k = load(k_far, k_ref)
+    load_v = load(v_far, v_ref)
     links.greet()
 
+    held = subsets(ups)
     ffn = []
-    kept_copies = []
-    kept_masks = subsets(ups)
-    for n, (src, keep, box, order) in enumerate(
-        (
-            (d_gate_ref, keep_gate, box_gate, ups),
-            (d_up_ref, keep_up, box_up, downs),
-            (d_down_ref, keep_down, box_down, ups),
-        )
+    split = keep_first.shape[1]
+    for src, keep, box, order, low in (
+        (d_gate_ref, keep_gate, box_gate, ups, 0),
+        (d_up_ref, keep_up, box_up, [0] + downs, 0),
+        (d_down_ref, keep_first, box_first, ups, 0),
+        (d_down_ref, keep_second, box_second, downs, split),
     ):
-        total = Sum(links, lambda m, src=src: src.at[related(s, m)], box, [0] + order)
-        total.launch()
-        total.kept = lambda m, keep=keep: keep.at[kept_masks.index(m)]
+        here = pl.ds(low, keep.shape[1])
+
+        def part(m, src=src, here=here):
+            if src is d_up_ref:
+                return src.at[related(s, m)]
+            return src.at[held.index(m), here]
+
+        total = Sum(links, part, box, order)
+        kept = subsets(order[1:])
+        total.loads = [load(part(m), keep.at[i]) for i, m in enumerate(kept)]
+        total.kept = lambda m, keep=keep, kept=kept: keep.at[kept.index(m)]
         ffn.append(total)
-        for i, m in enumerate(kept_masks):
-            copy = pltpu.make_async_copy(src.at[related(s, m)], keep.at[i], local_sem.at[n, i])
-            copy.start()
-            kept_copies.append(copy)
+    gate, up, first, second = ffn
+    up.start()
+    gate.start()
+    load_w = load(w_qkv_far, w_qkv_ref)
 
     d_proj = d_proj_ref[...]
 
     def out_block(j, carry):
-        dw_out[j] = jnp.dot(mixed_t_ref[j], d_proj, preferred_element_type=f32).astype(bf16)
+        dw_out[j] = (
+            jnp.dot(mixed_t_ref[j], d_proj, preferred_element_type=f32)
+            .astype(bf16)
+            .reshape(dw_out.shape[1:])
+        )
         return carry
 
     lax.fori_loop(0, nseq, out_block, 0)
-    sum_out = Sum(links, lambda m: dw_out.at[related(s, m)], box_out, [0] + downs)
-    sum_out.launch()
+    sum_out = Sum(links, lambda m: dw_out.at[related(s, m)], box_out, [0])
+    sum_out.masks = lambda stage: held
+    sum_out.start()
 
     for j in range(qcount):
         part = w_out_ref[pl.ds(j * width, width), :]
         grads[pl.ds(j * rows, rows), :] = contract_last(d_proj, part).astype(bf16)
         grads_t[:, pl.ds(j * rows, rows)] = contract_last(part, d_proj).astype(bf16)
+    for copy in up.loads:
+        copy.wait()
+    in_turn(up.steps(0, up.kept))
     dots = jnp.sum(grads_t[...].astype(f32) * att_ref[...], axis=0, keepdims=True)
     start = start_ref[...]
     index = index_ref[...]
     log_total = log_ref[...]
     dq_t[...] = jnp.zeros_like(dq_t)
+    load_k.wait()
+    load_v.wait()
 
     def step(g, carry):
         keys = k_ref[g]
@@ -760,24 +809,29 @@
         return carry
 
     lax.fori_loop(s + 1, groups, blank, 0)
-    sum_k = Sum(links, lambda m: dk.at[related(s, m)], box_k, [0] + ups)
-    sum_v = Sum(links, lambda m: dv.at[related(s, m)], box_v, [0] + downs)
-    sum_k.launch()
-    sum_v.launch()
-
-    for copy in kept_copies:
-        copy.wait()
-    gate, up, down = ffn
-    gate.settle(gate.kept)
-    gate.launch()
-    up.settle(up.kept)
-    up.launch()
-    sum_k.settle()
-    sum_k.launch()
-    sum_v.settle()
-    sum_v.launch()
-    sum_out.settle()
-    sum_out.launch()
+
+    kv = []
+    for j in list(range(1, heads)) + [0]:
+        owner = lax.rem(h + j, heads)
+        for far, box, order in ((dk, box_k, ups), (dv, box_v, downs)):
+            kv.append(
+                Sum(
+                    links,
+                    lambda m, far=far, owner=owner: far.at[related(s, m), owner],
+                    box.at[j],
+                    [0] + order,
+                )
+            )
+    for mask_index in range(len(held)):
+        for total in kv:
+            total.send(0, total.masks(0)[mask_index])
+
+    for m in sum_out.steps(0):
+        m()
+    z_out = [
+        links.go(box_out.at[:, o], zbox_out.at[d], (s, o)) for d, o in enumerate(links.others)
+    ]
+    in_turn(*[total.steps(0) for total in kv])
 
     cosines, sines = cos_ref[...], sin_ref[...]
     d_gain_q = jnp.zeros((1, width), f32)
@@ -791,57 +845,74 @@
         d_qkv[:, pl.ds(j * width, width)] = d_lin.astype(bf16)
         d_gain_q = d_gain_q + terms
 
-    sum_k.settle()
-    sum_k.launch()
-    sum_v.settle()
-    sum_v.launch()
-    down.settle(down.kept)
-    down.launch()
-    heads_shape = dk.shape[2:]
-
-    def over(total, zbox, shape):
-        where = total.waiting[0][1]
-        total.settle()
-        return links.over_heads(total.boxes.at[where], zbox), total.boxes.at[where]
-
-    z_k, own_k = over(sum_k, zbox_k, heads_shape)
-    z_v, own_v = over(sum_v, zbox_v, heads_shape)
-    sum_out.settle()
-    sum_out.launch()
-
-    def gathered(copies, zbox, own):
-        total = own[h].astype(f32)
-        for d, copy in enumerate(copies):
-            copy.wait_recv()
-            total = total + zbox[d].astype(f32)
+    for stage in range(1, bits - 1):
+        in_turn(*[total.steps(stage) for total in kv])
+    for total in (gate, first, second):
+        for copy in total.loads:
+            copy.wait()
+    in_turn(gate.steps(0, gate.kept), up.steps(1))
+    first.start()
+    second.start()
+
+    arriving = {}
+    for i, total in enumerate(kv):
+        for m in total.steps(bits - 1):
+            m()
+        j = (i // 2 + 1) % heads
+        if j:
+            zbox = (zbox_k, zbox_v)[i % 2]
+            arriving[i % 2, j] = links.go(
+                total.current(0), zbox.at[j - 1], (s, links.others[j - 1])
+            )
+    for d, copy in enumerate(z_out):
+        copy.wait_recv()
+    own = box_out[:, h].astype(f32)
+    for d in range(heads - 1):
+        own = own + zbox_out[d].astype(f32)
+    mid_out[...] = own.astype(bf16)
+    sum_end = Sum(links, lambda m: mid_out.at[held.index(m)], end_out, downs)
+    sum_end.start()
+
+    def whole(i, zbox):
+        total = kv[len(kv) - 2 + i].current(0)[...].astype(f32)
+        for j in range(1, heads):
+            arriving[i, j].wait_recv()
+            total = total + zbox[j - 1].astype(f32)
         return total
 
-    d_keys = gathered(z_k, zbox_k, own_k)
-    d_values = gathered(z_v, zbox_v, own_v)
+    d_keys = whole(0, zbox_k)
     d_lin, d_gain_k = back_norm(
         k_lin_ref[...], gain_k_ref[...], back_rotate(d_keys, cosines, sines)
     )
     qw = qcount * width
     d_qkv[:, pl.ds(qw, width)] = d_lin.astype(bf16)
+    d_values = whole(1, zbox_v)
     d_qkv[:, pl.ds(qw + width, width)] = d_values.astype(bf16)
-    cut_at = dw_a.shape[2]
-
-    def qkv_block(j, carry):
-        dw_a[j] = jnp.dot(
-            attn_t_ref[j], d_qkv[:, :cut_at], preferred_element_type=f32
-        ).astype(bf16)
-        dw_b[j] = jnp.dot(
-            attn_t_ref[j], d_qkv[:, cut_at:], preferred_element_type=f32
-        ).astype(bf16)
-        return carry
-
-    lax.fori_loop(0, nseq, qkv_block, 0)
-    sum_a = Sum(links, lambda m: dw_a.at[related(s, m)], box_a, [0] + ups)
-    sum_b = Sum(links, lambda m: dw_b.at[related(s, m)], box_b, [0] + downs)
-    sum_a.launch()
-    sum_b.launch()
-
+
+    pieces, _, block_rows, cut = dw_qkv.shape
+    qkv = []
+    for j in range(pieces):
+        cols = pl.ds(j * cut, cut)
+
+        def qkv_block(g, carry, j=j, cols=cols):
+            dw_qkv[j, g] = jnp.dot(
+                attn_t_ref[g], d_qkv[:, cols], preferred_element_type=f32
+            ).astype(bf16)
+            return carry
+
+        lax.fori_loop(0, nseq, qkv_block, 0)
+        total = Sum(
+            links,
+            lambda m, j=j: dw_qkv.at[j, related(s, m)],
+            box_qkv.at[j],
+            [0] + (downs if j % 2 else ups),
+        )
+        total.start()
+        qkv.append(total)
+
+    load_w.wait()
     d_attn_in = contract_last(d_qkv[...], w_qkv_ref[...])
+    in_turn(*[total.steps(0) for total in qkv])
     d_x, d_gain_in = back_norm(x_ref[...].astype(f32), gain_in_ref[...], d_attn_in)
     o_tokens[...] = (d_hid_ref[...] + d_x).astype(o_tokens.dtype)
 
@@ -849,71 +920,74 @@
     gsum[0, 0:1, :] = d_gain_in
     gsum[0, 4:5, :width] = d_gain_q
     gsum[0, 5:6, :width] = d_gain_k
-    gain_copies = [links.go(gsum.at[0], gbox.at[0], links.across(0))]
-
-    sum_a.settle()
-    sum_a.launch()
-    sum_b.settle()
-    sum_b.launch()
+    gain_copy = links.go(gsum.at[0], gbox.at[0], links.across(0))
+    for stage in range(1, bits - 1):
+        in_turn(*[total.steps(stage) for total in qkv])
     for bit in range(bits):
-        gain_copies[-1].wait_recv()
+        gain_copy.wait_recv()
         gsum[bit + 1] = gsum[bit] + gbox[bit]
         if bit + 1 < bits:
-            gain_copies.append(
-                links.go(gsum.at[bit + 1], gbox.at[bit + 1], links.across(bit + 1))
-            )
+            gain_copy = links.go(gsum.at[bit + 1], gbox.at[bit + 1], links.across(bit + 1))
     gain_z = [
         links.go(gsum.at[bits], gzbox.at[d], (s, o)) for d, o in enumerate(links.others)
     ]
-
-    def pieces(total, zsrc, col, size):
+    in_turn(sum_end.steps(0))
+    in_turn(first.steps(0, first.kept), second.steps(0, second.kept))
+
+    each = block_rows // heads
+    z_qkv = []
+    for j, total in enumerate(qkv):
         value = total.last()
-        each = value.shape[0] // heads
         for p in range(heads):
-            zsrc[p, :, pl.ds(col, size)] = value[p * each : (p + 1) * each].astype(bf16)
-
-    pieces(sum_out, zsrc_out, 0, dw_out.shape[2])
-    z_out = links.over_heads(zsrc_out, zbox_out)
-    gate.settle()
-    gate.launch()
-    up.settle()
-    up.launch()
-    sum_a.settle()
-    sum_a.launch()
-    sum_b.settle()
-    sum_b.launch()
-    pieces(sum_a, zsrc_qkv, 0, cut_at)
-    pieces(sum_b, zsrc_qkv, cut_at, dw_b.shape[2])
-    z_qkv = links.over_heads(zsrc_qkv, zbox_qkv)
-    down.settle()
-    down.launch()
+            zsrc_qkv[j, p] = value[p * each : (p + 1) * each].astype(bf16)
+        z_qkv.append(links.over_heads(zsrc_qkv.at[j], zbox_qkv.at[j]))
     o_gate[...] = gate.last()
     o_up[...] = up.last()
+    o_down[pl.ds(0, split), :] = first.last()
+    o_down[pl.ds(split, o_down.shape[0] - split), :] = second.last()
+    o_out[...] = sum_end.last()
     total = gsum[bits]
     for d, copy in enumerate(gain_z):
         copy.wait_recv()
         total = total + gzbox[d]
     o_gains[...] = total
-    o_out[...] = gathered(z_out, zbox_out, zsrc_out)
-    o_qkv[...] = gathered(z_qkv, zbox_qkv, zsrc_qkv)
-    o_down[...] = down.last()
+    for j, copies in enumerate(z_qkv):
+        total = zsrc_qkv[j, h].astype(f32)
+        for d, copy in enumerate(copies):
+            copy.wait_recv()
+            total = total + zbox_qkv[j, d].astype(f32)
+        o_qkv[:, pl.ds(j * cut, cut)] = total
     links.finish()
 
 
 def tail(nseq, heads, qcount, scale, cid, *arrays):
-    (q, k, v, _, _, _, att, mixed_t, d_proj, w_out, q_lin, k_lin, _, _, gain_q, _) = arrays[:16]
-    (attn_t, w_qkv, x, gain_in, d_hid, gains, d_gate, d_up, d_down) = arrays[16:]
+    (q, _, _, _, att, mixed_t, d_proj, w_out, q_lin, k_lin, _, _, gain_q, _) = arrays[:14]
+    (attn_t, x, gain_in, d_hid, gains, k, v, w_qkv, d_gate, _, _) = arrays[14:]
     f32, bf16 = jnp.float32, jnp.bfloat16
     rows, model = d_proj.shape
     width = gain_q.shape[1]
     cols = w_qkv.shape[1]
-    cut_at = cols // 2
+    pieces = 4
+    cut = cols // pieces
     out_rows, qkv_rows = mixed_t.shape[1], attn_t.shape[1]
-    pieces_kv = (heads, rows, width)
     ffn_block = d_gate.shape[1:]
     some, all_but = nseq // 2, nseq - 1
     bits = nseq.bit_length() - 1
-    copies = 8 * all_but + 5 * (heads - 1) + bits
+    out_block = (heads, out_rows // heads, model)
+    split = (ffn_block[0] // 2 + 15) // 16 * 16
+    parts = [ffn_block, ffn_block, (split, ffn_block[1]), (ffn_block[0] - split, ffn_block[1])]
+    copies = (
+        3 * (some - 1)
+        + all_but
+        + some
+        + (heads - 1)
+        + (some - 1)
+        + 2 * heads * all_but
+        + 2 * (heads - 1)
+        + pieces * (all_but + heads - 1)
+        + bits
+        + (heads - 1)
+    )
     vm = pl.BlockSpec(memory_space=VMEM)
     anywhere = pl.BlockSpec(memory_space=pl.ANY)
 
@@ -925,45 +999,47 @@
         out_shape=[
             jax.ShapeDtypeStruct((rows, model), bf16),
             jax.ShapeDtypeStruct((qkv_rows // heads, cols), f32),
-            jax.ShapeDtypeStruct((out_rows // heads, model), f32),
+            jax.ShapeDtypeStruct(out_block[1:], f32),
             jax.ShapeDtypeStruct(ffn_block, f32),
             jax.ShapeDtypeStruct(ffn_block, f32),
             jax.ShapeDtypeStruct(ffn_block, f32),
             jax.ShapeDtypeStruct(gains.shape, f32),
         ],
-        in_specs=[vm] * (len(arrays) - 3) + [anywhere] * 3,
+        in_specs=[vm] * (len(arrays) - 6) + [anywhere] * 6,
         out_specs=[vm] * 7,
         scratch_shapes=[
-            VMEM((nseq,) + pieces_kv, bf16),
-            VMEM((nseq,) + pieces_kv, bf16),
+            VMEM(k.shape, bf16),
+            VMEM(v.shape, bf16),
+            VMEM(w_qkv.shape, bf16),
+            VMEM((nseq, heads, rows, width), bf16),
+            VMEM((nseq, heads, rows, width), bf16),
             VMEM((width, qcount * rows), f32),
             VMEM((qcount * rows, width), bf16),
             VMEM((width, qcount * rows), bf16),
-            VMEM((all_but,) + pieces_kv, bf16),
-            VMEM((all_but,) + pieces_kv, bf16),
+            VMEM((heads, all_but, rows, width), bf16),
+            VMEM((heads, all_but, rows, width), bf16),
             VMEM((heads - 1, rows, width), bf16),
             VMEM((heads - 1, rows, width), bf16),
-            VMEM((nseq, out_rows, model), bf16),
-            VMEM((all_but, out_rows, model), bf16),
-            VMEM((heads, out_rows // heads, model), bf16),
-            VMEM((heads - 1, out_rows // heads, model), bf16),
-            VMEM((nseq, qkv_rows, cut_at), bf16),
-            VMEM((nseq, qkv_rows, cols - cut_at), bf16),
-            VMEM((all_but, qkv_rows, cut_at), bf16),
-            VMEM((all_but, qkv_rows, cols - cut_at), bf16),
-            VMEM((heads, qkv_rows // heads, cols), bf16),
-            VMEM((heads - 1, qkv_rows // heads, cols), bf16),
+            VMEM((nseq,) + out_block, bf16),
+            VMEM((some,) + out_block, bf16),
+            VMEM((heads - 1, some) + out_block[1:], bf16),
+            VMEM((some,) + out_block[1:], bf16),
+            VMEM((some - 1,) + out_block[1:], bf16),
+            VMEM((pieces, nseq, qkv_rows, cut), bf16),
+            VMEM((pieces, all_but, qkv_rows, cut), bf16),
+            VMEM((pieces, heads, qkv_rows // heads, cut), bf16),
+            VMEM((pieces, heads - 1, qkv_rows // heads, cut), bf16),
             VMEM((rows, cols), bf16),
         ]
-        + [VMEM((some,) + ffn_block, bf16)] * 3
-        + [VMEM((all_but,) + ffn_block, bf16)] * 3
+        + [VMEM((some if i == 1 else some // 2,) + part, bf16) for i, part in enumerate(parts)]
+        + [VMEM((all_but if i == 1 else some - 1,) + part, bf16) for i, part in enumerate(parts)]
         + [
             VMEM((bits + 1,) + gains.shape, f32),
             VMEM((bits,) + gains.shape, f32),
             VMEM((heads - 1,) + gains.shape, f32),
             pltpu.SemaphoreType.DMA((copies,)),
             pltpu.SemaphoreType.DMA((copies,)),
-            pltpu.SemaphoreType.DMA((3, some)),
+            pltpu.SemaphoreType.DMA((3 + 3 * some,)),
         ],
         name="tail",
         compiler_params=pltpu.CompilerParams(
@@ -972,67 +1048,37 @@
     )(*arrays)
 
 
-BLOCK_US, HOP_US = 3.5, 0.8
-WORK_US = {"fa": 2.0, "fb": 1.4, "fc": 2.0, "ga": 0.8, "gb": 0.5, "gc": 2.0, "n": 0.3, "e": 0.4}
-WORK_US.update({"wd": 3.3, "wg": 3.3, "wu": 3.3})
-
-
-def plan(chunks, spans, last, block_us, hop_us, work_us):
-    needs = {}
-    each = chunks // spans
-    for c in range(chunks):
-        p = c // each
-        for k in range(2):
-            for t in range(last):
-                needs["ags", k, c, t] = [("agw", k, c, t - 1)] if t else ([("n", c)] if k else [])
-                needs["agw", k, c, t] = [("ags", k, c, t)]
-                before = ("gc", p) if k else ("fc", p)
-                needs["rss", k, c, t] = [("rsw", k, c, t - 1)] if t else [before]
-                needs["rsw", k, c, t] = [("rss", k, c, t)]
-        needs["n", c] = [("rsw", 0, c, last - 1)]
-        needs["e", c] = [("rsw", 1, c, last - 1)]
-    for p in range(spans):
-        mine = range(p * each, (p + 1) * each)
-        needs["fa", p] = [("agw", 0, c, last - 1) for c in mine]
-        needs["fb", p] = [("fa", p)]
-        needs["fc", p] = [("fb", p)]
-        needs["ga", p] = [("agw", 1, c, last - 1) for c in mine]
-        needs["gb", p] = [("ga", p)]
-        needs["gc", p] = [("gb", p)]
-    needs[("wd",)] = [("ga", p) for p in range(spans)]
-    needs[("wg",)] = [("gb", p) for p in range(spans)] + [("wd",)]
-    needs[("wu",)] = [("wg",)]
-    rank = {"ags": 0, "rss": 0, "agw": 1, "rsw": 1, "n": 2, "e": 3}
-    rank.update({"ga": 4, "gb": 4, "gc": 4, "fa": 5, "fb": 5, "fc": 5, "wd": 6, "wg": 6, "wu": 6})
-    now, link, done, order = 0.0, 0.0, {}, []
-    while len(order) < len(needs):
-        ready = []
-        for event, before in needs.items():
-            if event in done or any(b not in done for b in before):
-                continue
-            at = max([done[b] for b in before], default=0.0)
-            start = max(now, at)
-            if event[0] in ("agw", "rsw") and start <= now + 0.4:
-                start = now
-            ready.append((start, rank[event[0]], event[2:3] or event[1:2], event, at))
-        start, _, _, event, at = min(ready)
-        kind = event[0]
-        now = max(start, at)
-        order.append(event)
-        if kind in ("ags", "rss"):
-            link = max(link, now) + block_us * 2 / 3
-            done[event] = link + block_us / 3 + hop_us
-            now += 0.1
-        elif kind in ("agw", "rsw"):
-            now += 0.1
-            done[event] = now
-        else:
-            now += work_us[kind]
-            done[event] = now
-    return order
+CHUNKS, SPANS = 4, 2
+ORDER = (
+    ("ags", 0, 0, 0), ("ags", 0, 1, 0), ("agw", 0, 0, 0), ("ags", 0, 0, 1), ("agw", 0, 1, 0),
+    ("ags", 0, 1, 1), ("ags", 0, 2, 0), ("agw", 0, 0, 1), ("ags", 0, 0, 2), ("agw", 0, 1, 1),
+    ("ags", 0, 1, 2), ("ags", 0, 3, 0), ("agw", 0, 0, 2), ("agw", 0, 1, 2), ("fa", 0), ("fb", 0),
+    ("agw", 0, 3, 0), ("agw", 0, 2, 0), ("ags", 0, 3, 1), ("ags", 0, 2, 1), ("fc", 0),
+    ("agw", 0, 3, 1), ("rss", 0, 0, 0), ("ags", 0, 3, 2), ("agw", 0, 3, 2), ("agw", 0, 2, 1),
+    ("rss", 0, 1, 0), ("ags", 0, 2, 2), ("rsw", 0, 0, 0), ("rss", 0, 0, 1), ("rsw", 0, 1, 0),
+    ("rss", 0, 1, 1), ("agw", 0, 2, 2), ("fa", 1), ("rsw", 0, 0, 1), ("fb", 1), ("rss", 0, 0, 2),
+    ("fc", 1), ("rss", 0, 2, 0), ("rsw", 0, 1, 1), ("rss", 0, 3, 0), ("rss", 0, 1, 2),
+    ("rsw", 0, 2, 0), ("rss", 0, 2, 1), ("rsw", 0, 0, 2), ("rsw", 0, 3, 0), ("n", 0),
+    ("ags", 1, 0, 0), ("rsw", 0, 1, 2), ("rss", 0, 3, 1), ("rsw", 0, 2, 1), ("rss", 0, 2, 2),
+    ("n", 1), ("agw", 1, 0, 0), ("ags", 1, 1, 0), ("ags", 1, 0, 1), ("rsw", 0, 3, 1),
+    ("rss", 0, 3, 2), ("agw", 1, 1, 0), ("ags", 1, 1, 1), ("rsw", 0, 2, 2), ("n", 2),
+    ("agw", 1, 0, 1), ("ags", 1, 0, 2), ("ags", 1, 2, 0), ("rsw", 0, 3, 2), ("n", 3),
+    ("agw", 1, 1, 1), ("ags", 1, 1, 2), ("ags", 1, 3, 0), ("agw", 1, 0, 2), ("agw", 1, 2, 0),
+    ("agw", 1, 1, 2), ("ga", 0), ("ags", 1, 2, 1), ("gb", 0), ("agw", 1, 3, 0), ("ags", 1, 3, 1),
+    ("gc", 0), ("agw", 1, 2, 1), ("ags", 1, 2, 2), ("rss", 1, 1, 0), ("rss", 1, 0, 0),
+    ("agw", 1, 3, 1), ("ags", 1, 3, 2), ("rsw", 1, 1, 0), ("rss", 1, 1, 1), ("agw", 1, 2, 2),
+    ("agw", 1, 3, 2), ("ga", 1), ("rsw", 1, 0, 0), ("gb", 1), ("rss", 1, 0, 1), ("gc", 1),
+    ("rss", 1, 3, 0), ("wd", 0), ("rsw", 1, 1, 1), ("rss", 1, 2, 0), ("wd", 1), ("rss", 1, 1, 2),
+    ("dd", 0), ("rsw", 1, 3, 0), ("rss", 1, 3, 1), ("wg", 0), ("rsw", 1, 2, 0), ("rsw", 1, 0, 1),
+    ("rss", 1, 2, 1), ("wg", 1), ("dg", 0), ("rss", 1, 0, 2), ("rsw", 1, 1, 2), ("wu", 0),
+    ("rsw", 1, 3, 1), ("e", 1), ("rss", 1, 3, 2), ("rsw", 1, 2, 1), ("rss", 1, 2, 2), ("wu", 1),
+    ("rsw", 1, 0, 2), ("Dd", 0), ("Dg", 0), ("e", 0), ("rsw", 1, 3, 2), ("e", 3), ("rsw", 1, 2, 2),
+    ("e", 2),
+)
 
 
 def ffn_kernel(
+    nseq,
     heads,
     chunks,
     spans,
@@ -1049,9 +1095,9 @@
     o_hid,
     o_proj,
     o_gains,
+    o_down,
     o_gate,
     o_up,
-    o_down,
     hidden,
     w_gate,
     w_up,
@@ -1070,6 +1116,10 @@
     dw_gate,
     dw_up,
     dw_down,
+    box_gate,
+    box_down,
+    sum_send,
+    sum_recv,
     ag_send,
     ag_recv,
     rs_send,
@@ -1096,7 +1146,10 @@
         copy = pltpu.make_async_copy(src, dst, local_sem.at[n])
         copy.start()
         loads.append(copy)
-    greet([right, left])
+    bits = nseq.bit_length() - 1
+    ups, downs = seq_orders(bits)
+    links = Links(nseq, heads, sum_send, sum_recv)
+    greet([right, left] + [links.across(b) for b in range(bits)])
 
     proj = proj_ref[...]
     hid = x_ref[...].astype(f32) + norm_rows(proj, gain_two_ref[...])
@@ -1192,7 +1245,7 @@
             arrived.add(n)
             loads[n].wait()
 
-    def held(buf, p):
+    def span_rows(buf, p):
         return buf[pl.ds(p * each, each)].reshape(many, model)
 
     def place_parts(k, p, cols, value):
@@ -1205,7 +1258,7 @@
         need(1)
 
         def body(cols):
-            u = held(u_all, c)
+            u = span_rows(u_all, c)
             gate = contract_last(u, w_gate[cols, :])
             up = contract_last(u, w_up[cols, :])
             root = math.sqrt(2.0 / math.pi)
@@ -1250,7 +1303,7 @@
 
     def back_tiles(c, lo, hi):
         def body(cols):
-            d_act = contract_last(held(d_all, c), w_down[cols, :])
+            d_act = contract_last(span_rows(d_all, c), w_down[cols, :])
             d_gate[pl.ds(c * many, many), cols] = (
                 d_act * by_gate[pl.ds(c * many, many), cols]
             ).astype(bf16)
@@ -1288,21 +1341,29 @@
 
     def flip(source):
         for p in range(spans):
-            flipped[:, pl.ds(p * many, many)] = held(source, p).T
-
-    def weight_grad(right_ref, dst, out, n):
+            flipped[:, pl.ds(p * many, many)] = span_rows(source, p).T
+
+    def weight_grad(right_ref, dst, half):
         def body(cols):
             value = jnp.dot(flipped[...], right_ref[:, cols], preferred_element_type=f32)
             dst[:, :, cols] = value.astype(bf16).reshape(dst.shape[:2] + (value.shape[1],))
 
-        over_tiles(0, whole_tiles, body)
-        copy = pltpu.make_async_copy(dst, out, local_sem.at[n])
-        copy.start()
-        stores.append(copy)
+        over_tiles(half_tiles if half else 0, whole_tiles if half else half_tiles, body)
 
     half_tiles = (whole_tiles + 1) // 2
-    events = plan(chunks, spans, last, BLOCK_US / chunks, HOP_US, WORK_US)
-    for event in events:
+    held = subsets(ups)
+    sum_gate = Sum(links, lambda m: dw_gate.at[related(s, m)], box_gate, [0])
+    sum_down = Sum(links, lambda m: dw_down.at[related(s, m)], box_down, [0])
+    for total in (sum_gate, sum_down):
+        total.masks = lambda stage: held
+    def keep(total, out, n):
+        for i, step in enumerate(total.steps(0)):
+            step()
+            copy = pltpu.make_async_copy(total.boxes.at[i], out.at[i], local_sem.at[n + i])
+            copy.start()
+            stores.append(copy)
+
+    for event in ORDER:
         kind, args = event[0], event[1:]
         if kind == "ags":
             ags(*args)
@@ -1329,15 +1390,29 @@
         elif kind == "e":
             finish_rows(args[0])
         elif kind == "wd":
-            flip(d_all)
-            weight_grad(act, dw_down, o_down, 3)
+            if args[0] == 0:
+                flip(d_all)
+            weight_grad(act, dw_down, args[0])
         elif kind == "wg":
-            flip(u_all)
-            weight_grad(d_gate, dw_gate, o_gate, 4)
+            if args[0] == 0:
+                flip(u_all)
+            weight_grad(d_gate, dw_gate, args[0])
+        elif kind == "wu":
+            weight_grad(d_up, dw_up, args[0])
+            if args[0] == 1:
+                copy = pltpu.make_async_copy(dw_up, o_up, local_sem.at[3 + 2 * len(held)])
+                copy.start()
+                stores.append(copy)
+        elif kind == "dd":
+            sum_down.start()
+        elif kind == "dg":
+            sum_gate.start()
+        elif kind == "Dd":
+            keep(sum_down, o_down, 3)
         else:
-            weight_grad(d_up, dw_up, o_up, 5)
-
-    for event in events:
+            keep(sum_gate, o_gate, 3 + len(held))
+
+    for event in ORDER:
         if event[0] == "ags":
             k, c, t = event[1:]
             for on, block, lane, target, _, _ in lanes(k, c, t):
@@ -1356,28 +1431,33 @@
         need(n)
     for copy in stores:
         copy.wait()
-
-
-def feed_forward(nseq, heads, chunks, spans, cid, proj, x, cot, gains, w_gate, w_up, w_down):
+    links.finish()
+
+
+def feed_forward(nseq, heads, cid, proj, x, cot, gains, w_gate, w_up, w_down):
     f32, bf16 = jnp.float32, jnp.bfloat16
     rows, model = x.shape
     units = w_gate.shape[0]
+    chunks = CHUNKS
     rc = rows // chunks
     group = rows * heads
     vm = pl.BlockSpec(memory_space=VMEM)
     anywhere = pl.BlockSpec(memory_space=pl.ANY)
-    grad = jax.ShapeDtypeStruct((nseq, model // nseq, units), bf16)
+    block = (model // nseq, units)
+    some = nseq // 2
+    half = jax.ShapeDtypeStruct((some,) + block, bf16)
+    messages = 2 * some
     hops = (2, chunks, 2, heads - 1)
     return pl.pallas_call(
-        functools.partial(ffn_kernel, heads, chunks, spans),
+        functools.partial(ffn_kernel, nseq, heads, CHUNKS, SPANS),
         out_shape=[
             jax.ShapeDtypeStruct((rows, model), bf16),
             jax.ShapeDtypeStruct((rows, model), f32),
             jax.ShapeDtypeStruct((rows, model), bf16),
             jax.ShapeDtypeStruct((8, model), f32),
-            grad,
-            grad,
-            grad,
+            half,
+            half,
+            jax.ShapeDtypeStruct((nseq,) + block, bf16),
         ],
         in_specs=[vm] * 6 + [anywhere] * 3,
         out_specs=[vm] * 4 + [anywhere] * 3,
@@ -1397,14 +1477,18 @@
             VMEM((2, chunks, heads - 1, rc, model), bf16),
             VMEM((2, chunks, heads - 1, rc, model), bf16),
             VMEM((model, group), bf16),
-            VMEM(grad.shape, bf16),
-            VMEM(grad.shape, bf16),
-            VMEM(grad.shape, bf16),
+            VMEM((nseq,) + block, bf16),
+            VMEM((nseq,) + block, bf16),
+            VMEM((nseq,) + block, bf16),
+            VMEM((some,) + block, bf16),
+            VMEM((some,) + block, bf16),
+            pltpu.SemaphoreType.DMA((messages,)),
+            pltpu.SemaphoreType.DMA((messages,)),
             pltpu.SemaphoreType.DMA(hops),
             pltpu.SemaphoreType.DMA(hops),
             pltpu.SemaphoreType.DMA(hops),
             pltpu.SemaphoreType.DMA(hops),
-            pltpu.SemaphoreType.DMA((6,)),
+            pltpu.SemaphoreType.DMA((4 + 2 * some,)),
         ],
         name="feed_forward",
         compiler_params=pltpu.CompilerParams(
@@ -1491,14 +1575,12 @@
     attended = attended_t.T
     mixed_local = unstacked(attended.astype(bf16))
     projected = jnp.dot(mixed_local, w_out, preferred_element_type=jnp.float32)
-    if nseq <= 8 and (model // nseq) % 16 == 0:
+    if (nseq, heads) == (8, 4) and (model // nseq) % 16 == 0:
         qw = qcount * width
         each, few = model // (nseq * heads), width // (nseq * heads)
-        output, d_hidden, d_projected, gains, *blocks = feed_forward(
+        output, d_hidden, d_projected, gains, half_down, half_gate, all_up = feed_forward(
             nseq,
             heads,
-            4,
-            2,
             10,
             projected,
             tokens,
@@ -1516,8 +1598,6 @@
             scale,
             9,
             queries,
-            keys,
-            values,
             starts,
             index,
             log_total,
@@ -1532,12 +1612,16 @@
             gain_query[None],
             gain_key[None],
             attn_in.T.reshape(nseq, -1, local_rows),
-            w_qkv,
             tokens,
             gain_attn_in[None],
             d_hidden,
             gains,
-            *blocks,
+            keys,
+            values,
+            w_qkv,
+            half_gate,
+            all_up,
+            half_down,
         )
         which = seq_index * heads + head_index
         wide = lax.dynamic_slice_in_dim(sum_gains[:4], which * each, each, 1)

time: 314 us -> 278 us (0.89)
  Pallas kernels: 278 us -> 245 us
    pallas_call x1, Pallas kernels: 138 us -> 107 us  [tail(): pl.pallas_call(kernel, out_shape=[jax.ShapeDtypeStruct((rows, model), bf1...]
    unnamed x48 -> x50, local copies, waits for them, and re-layouts: 8.9 us -> 7.07 us
where the time goes in v4:
time: 278 us
  Pallas kernels  245 us (88%)
  local copies, waits for them, and re-layouts  18.6 us (7%)
  other arithmetic  7.89 us (3%)
  matrix products  5.07 us (2%)
    pallas_call x1, Pallas kernels, tail(): pl.pallas_call(kernel, out_shape=[jax.ShapeDtypeStruct((rows, model), bf1...  107 us
    pallas_call x1, Pallas kernels, feed_forward(): pl.pallas_call(functools.partial(ffn_kernel, nseq, heads, CHUNKS, SPANS),...  94.2 us
    pallas_call x1, Pallas kernels, gather_all(): pl.pallas_call(kernel, out_shape=[jax.ShapeDtypeStruct((nseq, heads) + a....  39.8 us
    unnamed x50, local copies, waits for them, and re-layouts  7.07 us

profile of v4, /device:TPU:0, one launch (start us, length us, event | category | flops | bytes accessed | tf_op | source)
XLA Modules:
  0.0 277.7 jit_solution(14005649697599226807)
XLA Ops:
  0.6 1.1 fusion
  1.8 0.0 copy-start.1
  1.8 0.0 copy-start.10
  1.8 0.0 copy-start.15
  1.8 2.4 fusion.8.refs_8_
  4.2 0.0 copy-start.3
  4.2 0.0 copy-start.21
  4.2 0.0 copy-start.16
  4.2 0.2 reshape.150
  4.5 0.2 multiply_reduce_fusion
  4.7 0.0 copy-done.20
  4.8 0.0 copy-start.12
  4.8 0.2 multiply_multiply_fusion
  5.0 0.0 copy-done.1
  5.0 0.0 copy-done.10
  5.0 0.0 copy-done.15
  5.0 0.4 multiply_reduce_fusion.1
  5.4 0.0 copy-start.13
  5.4 0.0 copy-done.21
  5.4 0.1 multiply_multiply_fusion.1
  5.5 0.1 dynamic_slice.9
  5.6 0.5 select_reduce_fusion
  6.1 0.3 subtract_convert_fusion.1
  6.5 0.1 subtract_convert_fusion
  6.6 0.0 copy-done.3
  6.6 0.2 fusion.3
  6.8 0.7 copy.42
  7.5 0.6 pad_maximum_fusion.1.refs_0_
  8.2 0.9 convolution_convert_fusion.refs_1_
  9.1 39.8 %gather_all.1 = (bf16[8,4,128,256]{3,2,1,0:T(8,128)(2,1)}, bf16[8,4,128,256]{3,2,1,0:T(8,128)(2,1)}) custom-call(bf16[128,256]{1,0:T(8,128)(2,1)} %pad_maximum_fusion.1.refs_0_, bf16[128,256]{1,0:T(8,128)(2,1)} %convolution_convert_fusion.refs_1_), custom_call_target="tpu_custom_call" | custom-call | tf_op jit(solution)/shard_map/gather_all/pallas_call | solution.py:147
  48.9 0.6 tile.4
  49.5 0.6 tile.5
  50.1 4.0 %attend.1 = (f32[256,512]{1,0:T(8,128)}, f32[1,512]{1,0:T(1,128)}) custom-call(bf16[512,256]{1,0:T(8,128)(2,1)} %bitcast.48, bf16[8,512,256]{2,1,0:T(8,128)(2,1)} %bitcast.42, bf16[8,512,256]{2,1,0:T(8,128)(2,1)} %bitcast.44, s32[1,512]{1,0:T(1,128)} %bitcast.55, s32[1,512]{1,0:T(1,128)} %bitcast.57), custom_call_target="tpu_custom_call" | custom-call | tf_op jit(solution)/shard_map/attend/pallas_call | solution.py:458
  54.1 0.0 copy-start.17
  54.1 0.0 copy-start.18
  54.1 0.0 copy-start.19
  54.2 1.1 convert_bitcast_fusion
  55.2 0.1 reshape.153
  55.4 1.4 fusion.11.proj_ref
  56.7 0.6 broadcast_in_dim.26.gain_two_ref
  57.3 0.6 broadcast_in_dim.46.gain_three_ref
  57.9 0.0 copy-done.19
  57.9 0.6 broadcast_in_dim.47.gain_four_ref
  58.5 94.2 %feed_forward.1 = (bf16[128,1152]{1,0:T(8,128)(2,1)}, f32[128,1152]{1,0:T(8,128)}, bf16[128,1152]{1,0:T(8,128)(2,1)}, f32[8,1152]{1,0:T(8,128)}, bf16[4,144,1728...) custom-call(f32[128,1152]{1,0:T(8,128)} %fusion.11.proj_ref, ...), custom_call_target="tpu_custom_call" | custom-call | tf_op jit(solution)/shard_map/feed_forward/pallas_call | solution.py:1451
  152.8 0.1 fusion.4
  152.9 0.9 copy.44
  153.8 0.6 broadcast_in_dim.50.refs_16_
  154.4 3.3 %pad_maximum_fusion.refs_21_ = bf16[1152,1536]{1,0:T(8,128)(2,1)} fusion(bf16[1152,256]{1,0:T(8,128)(2,1)} %param.20, bf16[1152,256]{1,0:T(8,128)(2,1)S(1)} %copy-done.11, bf16[1152,1024]{1,0:T(8,128)(2,1)} %param.18), kind=kLoop, calls=%fused_computation | loop fusion | flops 10616832 | bytes 7077888 | tf_op jit(solution)/shard_map/concatenate | solution.py:1593
  157.7 107.2 %tail.1 = (bf16[128,1152]{1,0:T(8,128)(2,1)}, f32[36,1536]{1,0:T(8,128)}, f32[32,1152]{1,0:T(8,128)}, f32[144,1728]{1,0:T(8,128)}, f32[144,1728]{1,0:T(8,128)}, /*index=5*/f32[144,1728]{1,0:T(8,128)}, f32[8,1152]{1,0:T(8,128)}) custom-call(bf16[512,256]{1,0:T(8,128)(2,1)} %bitcast.49, s32[1,512]{1,0:T(1,128)} %bitcast.56, s32[1,512]{1,0:T(1,128)} %bitcast.58, ...), custom_call_target="tpu_custom_call" | custom-call | tf_op jit(solution)/shard_map/tail/pallas_call | solution.py:997
  264.8 1.7 slice.49
  266.6 1.4 fusion.10
  268.0 0.8 slice.52
  268.8 0.1 constant_dynamic-slice_fusion.1
  268.9 0.5 slice_bitcast_fusion.2
  269.4 0.8 slice.57
  270.2 0.1 constant_dynamic-slice_fusion
  270.2 0.5 slice_bitcast_fusion
  270.8 0.7 copy.52
  271.5 1.7 copy.53
  273.2 1.7 copy.54
  274.8 1.0 copy.55
  275.8 1.0 copy.56
  276.8 0.0 copy-done.5
  276.8 1.0 copy.57
  (31 shorter events, 0.1 us)
Async XLA Ops:
  1.8 3.0 %copy-start.20 = (f32[256]{0:T(256)S(1)}, f32[256]{0:T(256)}, u32[]{:S(2)}) copy-start(f32[256]{0:T(256)} %param.29) | copy-start | bytes 3076
  1.8 3.2 %copy-start.1 = (bf16[128,1152]{1,0:T(8,128)(2,1)S(1)}, bf16[128,1152]{1,0:T(8,128)(2,1)}, u32[]{:S(2)}) copy-start(bf16[128,1152]{1,0:T(8,128)(2,1)} %refs_15_.1) | copy-start | bytes 884740
  1.8 3.2 %copy-start.10 = (bf16[1152,256]{1,0:T(8,128)(2,1)S(1)}, bf16[1152,256]{1,0:T(8,128)(2,1)}, u32[]{:S(2)}) copy-start(bf16[1152,256]{1,0:T(8,128)(2,1)} %param.19) | copy-start | bytes 1769476
  1.8 3.2 %copy-start.15 = (f32[1152]{0:T(1024)S(1)}, f32[1152]{0:T(1024)}, u32[]{:S(2)}) copy-start(f32[1152]{0:T(1024)} %param.25) | copy-start | bytes 13828
  4.2 2.4 copy-start.3
  4.2 1.2 copy-start.21
  4.2 1.3 copy-start.16
  4.8 3.4 %copy-start.12 = (bf16[1152,256]{1,0:T(8,128)(2,1)S(1)}, bf16[1152,256]{1,0:T(8,128)(2,1)}, u32[]{:S(2)}) copy-start(bf16[1152,256]{1,0:T(8,128)(2,1)} %param.20) | copy-start | bytes 1769476
  5.4 48.7 %copy-start.13 = (f32[128,256]{1,0:T(8,128)}, f32[128,256]{1,0:T(8,128)S(1)}, u32[]{:S(2)}) copy-start(f32[128,256]{1,0:T(8,128)S(1)} %get-tuple-element.66.refs_9_) | copy-start | bytes 393220
  6.5 47.7 %copy-start.8 = (f32[128,128]{1,0:T(8,128)}, f32[128,128]{1,0:T(8,128)S(1)}, u32[]{:S(2)}) copy-start(f32[128,128]{1,0:T(8,128)S(1)} %get-tuple-element.63.refs_11_) | copy-start | bytes 196612
  6.5 47.7 %copy-start.9 = (f32[128,128]{1,0:T(8,128)}, f32[128,128]{1,0:T(8,128)S(1)}, u32[]{:S(2)}) copy-start(f32[128,128]{1,0:T(8,128)S(1)} %get-tuple-element.64.refs_10_) | copy-start | bytes 196612
  50.1 5.3 %copy-start = (bf16[1024,1152]{1,0:T(8,128)(2,1)S(1)}, bf16[1024,1152]{1,0:T(8,128)(2,1)}, u32[]{:S(2)}) copy-start(bf16[1024,1152]{1,0:T(8,128)(2,1)} %refs_7_.1) | copy-start | bytes 7077892
  54.1 2.6 copy-start.17
  54.1 3.2 %copy-start.18 = (f32[1152]{0:T(1024)S(1)}, f32[1152]{0:T(1024)}, u32[]{:S(2)}) copy-start(f32[1152]{0:T(1024)} %param.27) | copy-start | bytes 13828
  54.1 3.8 %copy-start.19 = (f32[1152]{0:T(1024)S(1)}, f32[1152]{0:T(1024)}, u32[]{:S(2)}) copy-start(f32[1152]{0:T(1024)} %param.28) | copy-start | bytes 13828
  55.4 97.4 %copy-start.4 = (bf16[128,4,256]{0,2,1:T(8,128)(2,1)}, bf16[128,4,256]{0,2,1:T(8,128)(2,1)S(1)}, u32[]{:S(2)}) copy-start(bf16[128,4,256]{0,2,1:T(8,128)(2,1)S(1)} %copy.43) | copy-start | bytes 786436
  58.5 94.2 %copy-start.2 = (bf16[128,1152]{1,0:T(8,128)(2,1)S(1)}, bf16[128,1152]{1,0:T(8,128)(2,1)}, u32[]{:S(2)}) copy-start(bf16[128,1152]{1,0:T(8,128)(2,1)} %refs_15_.1) | copy-start | bytes 884740
  58.5 95.9 %copy-start.11 = (bf16[1152,256]{1,0:T(8,128)(2,1)S(1)}, bf16[1152,256]{1,0:T(8,128)(2,1)}, u32[]{:S(2)}) copy-start(bf16[1152,256]{1,0:T(8,128)(2,1)} %param.19) | copy-start | bytes 1769476
  157.7 113.1 %copy-start.14 = (bf16[128,1152]{1,0:T(8,128)(2,1)S(1)}, bf16[128,1152]{1,0:T(8,128)(2,1)}, u32[]{:S(2)}) copy-start(bf16[128,1152]{1,0:T(8,128)(2,1)} %get-tuple-element.84) | copy-start | bytes 884740
  264.8 10.0 %copy-start.7 = (f32[144,1728]{1,0:T(8,128)S(1)}, f32[144,1728]{1,0:T(8,128)}, u32[]{:S(2)}) copy-start(f32[144,1728]{1,0:T(8,128)} %get-tuple-element.90) | copy-start | bytes 2985988
  264.8 11.0 %copy-start.6 = (f32[144,1728]{1,0:T(8,128)S(1)}, f32[144,1728]{1,0:T(8,128)}, u32[]{:S(2)}) copy-start(f32[144,1728]{1,0:T(8,128)} %get-tuple-element.91) | copy-start | bytes 2985988
  273.2 3.6 %copy-start.5 = (f32[144,1728]{1,0:T(8,128)S(1)}, f32[144,1728]{1,0:T(8,128)}, u32[]{:S(2)}) copy-start(f32[144,1728]{1,0:T(8,128)} %get-tuple-element.49) | copy-start | bytes 2985988

commit v5 on v4

--- a/solution.py
+++ b/solution.py
@@ -524,6 +524,257 @@
     )(q, k, v, start, index, log_total, dots, grads)
 
 
+def flat(ref):
+    return ref[...].reshape(1, ref.shape[0])
+
+
+def front_kernel(
+    nseq,
+    heads,
+    qcount,
+    scale,
+    x_ref,
+    ids_ref,
+    w_key_ref,
+    w_value_ref,
+    gain_in_ref,
+    gain_q_ref,
+    gain_k_ref,
+    w_query_far,
+    w_out_far,
+    o_proj,
+    o_q,
+    o_k,
+    o_v,
+    o_start,
+    o_index,
+    o_log,
+    o_att,
+    o_q_lin,
+    o_k_lin,
+    o_cos,
+    o_sin,
+    o_attn_t,
+    w_query,
+    w_out,
+    k_all,
+    v_all,
+    send,
+    recv,
+    local_sem,
+):
+    f32, bf16 = jnp.float32, jnp.bfloat16
+    bits = nseq.bit_length() - 1
+    ups, downs = seq_orders(bits)
+    links = Links(nseq, heads, send, recv)
+    s, h = links.s, links.h
+    rows, model = x_ref.shape
+    width = w_key_ref.shape[1]
+    gain_q, gain_k = flat(gain_q_ref), flat(gain_k_ref)
+    half = width // 2
+    total = ids_ref.shape[0] * ids_ref.shape[1]
+    load_q = pltpu.make_async_copy(w_query_far, w_query, local_sem.at[0])
+    load_q.start()
+    load_o = pltpu.make_async_copy(w_out_far, w_out, local_sem.at[1])
+    load_o.start()
+    partners = [related(h, j) for j in range(1, heads)]
+    greet([links.across(b) for b in range(bits)] + [(s, o) for o in partners])
+
+    which = s * heads + h
+    mine = ids_ref[pl.ds(which, 1), :].astype(f32)
+    column = jnp.broadcast_to(mine, (rows, rows)).T[:, 0:1]
+    first = jnp.full((rows, rows), float(total), f32)
+    for r in range(ids_ref.shape[0]):
+        here = ids_ref[r : r + 1, :].astype(f32)
+        at = (r * rows + lax.broadcasted_iota(jnp.int32, (1, rows), 1)).astype(f32)
+        first = jnp.minimum(first, jnp.where(column == here, at, float(total)))
+    start = jnp.min(first, axis=1, keepdims=True)
+    index = (which * rows + lax.broadcasted_iota(jnp.int32, (rows, 1), 0)).astype(f32)
+    freq = jnp.exp(
+        lax.broadcasted_iota(jnp.int32, (1, half), 1).astype(f32)
+        * (-2.0 * math.log(1000000.0) / width)
+    )
+    angle = (index - start) * freq
+    turns = jnp.round(angle * (1.0 / (2.0 * math.pi)))
+    angle = (angle - turns * 6.28125) - turns * (2.0 * math.pi - 6.28125)
+    cosines, sines = jnp.cos(angle), jnp.sin(angle)
+    o_cos[...] = cosines
+    o_sin[...] = sines
+    start_row = jnp.broadcast_to(start, (rows, rows)).T[0:1, :].astype(jnp.int32)
+    index_row = which * rows + lax.broadcasted_iota(jnp.int32, (1, rows), 1)
+    for j in range(qcount):
+        o_start[:, pl.ds(j * rows, rows)] = start_row
+        o_index[:, pl.ds(j * rows, rows)] = index_row
+
+    attn_in = norm_rows(x_ref[...].astype(f32), flat(gain_in_ref)).astype(bf16)
+    k_lin = jnp.dot(attn_in, w_key_ref[...], preferred_element_type=f32)
+    k_all[s, h] = rotate(norm_rows(k_lin, gain_k), cosines, sines).astype(bf16)
+    o_k_lin[...] = k_lin
+    v_all[s, h] = jnp.dot(attn_in, w_value_ref[...], preferred_element_type=f32).astype(bf16)
+
+    both = ((k_all, ups), (v_all, downs))
+
+    def pass_on(a, mask, j, bit):
+        buf = both[a][0]
+        block = buf.at[related(s, mask), related(h, j)]
+        return links.go(block, block, links.across(bit))
+
+    over_head = {}
+    for j in range(1, heads):
+        for a in range(2):
+            block = both[a][0].at[s, h]
+            over_head[a, j] = links.go(block, block, (s, partners[j - 1]))
+    arriving = {}
+
+    def spread(a, mask, j, stage):
+        order = both[a][1]
+        for later in range(stage, len(order)):
+            bit = order[later]
+            arriving[a, mask | (1 << bit), j] = pass_on(a, mask, j, bit)
+
+    for a in range(2):
+        spread(a, 0, 0, 0)
+
+    load_q.wait()
+    q_lin = jnp.dot(attn_in, w_query[...], preferred_element_type=f32)
+    o_q_lin[...] = q_lin
+    for j in range(1, heads):
+        for a in range(2):
+            over_head[a, j].wait_recv()
+            spread(a, 0, j, 0)
+    for j in range(qcount):
+        part = norm_rows(q_lin[:, j * width : (j + 1) * width], gain_q)
+        o_q[pl.ds(j * rows, rows), :] = (rotate(part, cosines, sines) * scale).astype(bf16)
+
+    pairs = []
+
+    def to_pair(a, mask):
+        block = both[a][0].at[related(s, mask)]
+        pairs.append(links.go(block, block, links.across(0)))
+
+    for a in range(2):
+        to_pair(a, 0)
+    for stage in range(len(ups)):
+        for lower in subsets(range(stage)):
+            masks = []
+            for a in range(2):
+                order = both[a][1]
+                mask = sum(1 << order[i] for i in range(stage) if lower >> i & 1)
+                masks.append(mask | (1 << order[stage]))
+            for j in range(heads):
+                for a in range(2):
+                    arriving[a, masks[a], j].wait_recv()
+                    spread(a, masks[a], j, stage + 1)
+            for a in range(2):
+                to_pair(a, masks[a])
+    for j in range(1):
+        o_attn_t[...] = attn_in.T.reshape(o_attn_t.shape)
+
+    queries = o_q[...]
+    starts = o_start[...]
+    indices = o_index[...]
+    o_att[...] = jnp.zeros_like(o_att)
+    span = heads * rows
+    low = lax.rem(s, 2)
+
+    def attend_group(g, mass):
+        scores = contract_last(k_all[g].reshape(span, width), queries)
+        key = g * span + lax.broadcasted_iota(jnp.int32, scores.shape, 0)
+        terms = jnp.where((key >= starts) & (key <= indices), jnp.exp(scores), 0.0)
+        o_att[...] += contract_first(v_all[g].reshape(span, width), terms.astype(bf16))
+        return mass + jnp.sum(terms, axis=0, keepdims=True)
+
+    mass = lax.fori_loop(
+        0,
+        s // 2 + 1,
+        lambda i, m: attend_group(2 * i + low, m),
+        jnp.zeros((1, qcount * rows), f32),
+    )
+    for copy in pairs:
+        copy.wait_recv()
+    mass = lax.fori_loop(
+        0, s // 2 + low, lambda i, m: attend_group(2 * i + 1 - low, m), mass
+    )
+    keep_k = pltpu.make_async_copy(k_all, o_k, local_sem.at[2])
+    keep_v = pltpu.make_async_copy(v_all, o_v, local_sem.at[3])
+    keep_k.start()
+    keep_v.start()
+    o_log[...] = jnp.log(mass)
+    attended = o_att[...] / mass
+    o_att[...] = attended
+    load_o.wait()
+    proj = jnp.zeros((rows, model), f32)
+    for j in range(qcount):
+        part = attended[:, j * rows : (j + 1) * rows].T.astype(bf16)
+        proj = proj + jnp.dot(
+            part, w_out[pl.ds(j * width, width), :], preferred_element_type=f32
+        )
+    o_proj[...] = proj
+    keep_k.wait()
+    keep_v.wait()
+    links.finish()
+
+
+def front(nseq, heads, qcount, scale, cid, x, ids, w_key, w_value, gain_in, gain_q, gain_k, w_query, w_out):
+    f32, bf16, i32 = jnp.float32, jnp.bfloat16, jnp.int32
+    rows, model = x.shape
+    width = w_key.shape[1]
+    stacked = qcount * rows
+    some = nseq // 2
+    messages = 2 * (heads - 1) + 2 * heads * (some - 1) + 2 * some
+    vm = pl.BlockSpec(memory_space=VMEM)
+    anywhere = pl.BlockSpec(memory_space=pl.ANY)
+    everyone = (nseq, heads, rows, width)
+
+    def kernel(*refs):
+        front_kernel(nseq, heads, qcount, scale, *refs)
+
+    shape = jax.ShapeDtypeStruct
+    return pl.pallas_call(
+        kernel,
+        out_shape=[
+            shape((rows, model), f32),
+            shape((stacked, width), bf16),
+            shape(everyone, bf16),
+            shape(everyone, bf16),
+            shape((1, stacked), i32),
+            shape((1, stacked), i32),
+            shape((1, stacked), f32),
+            shape((width, stacked), f32),
+            shape((rows, qcount * width), f32),
+            shape((rows, width), f32),
+            shape((rows, width // 2), f32),
+            shape((rows, width // 2), f32),
+            shape((nseq, model // nseq, rows), bf16),
+        ],
+        in_specs=[vm] * 7 + [anywhere] * 2,
+        out_specs=[vm] * 2 + [anywhere] * 2 + [vm] * 9,
+        scratch_shapes=[
+            VMEM(w_query.shape, bf16),
+            VMEM(w_out.shape, bf16),
+            VMEM(everyone, bf16),
+            VMEM(everyone, bf16),
+            pltpu.SemaphoreType.DMA((messages,)),
+            pltpu.SemaphoreType.DMA((messages,)),
+            pltpu.SemaphoreType.DMA((4,)),
+        ],
+        name="front",
+        compiler_params=pltpu.CompilerParams(
+            collective_id=cid, has_side_effects=True, vmem_limit_bytes=LIMIT
+        ),
+    )(
+        x,
+        ids.reshape(nseq * heads, rows),
+        w_key,
+        w_value,
+        gain_in,
+        gain_q,
+        gain_k,
+        w_query,
+        w_out,
+    )
+
+
 class Sum:
     def __init__(self, links, part, boxes, order):
         self.links, self.part, self.boxes, self.order = links, part, boxes, order
@@ -640,7 +891,6 @@
     index_ref,
     log_ref,
     att_ref,
-    mixed_t_ref,
     d_proj_ref,
     w_out_ref,
     q_lin_ref,
@@ -649,14 +899,16 @@
     sin_ref,
     gain_q_ref,
     gain_k_ref,
+    gain_in_ref,
     attn_t_ref,
     x_ref,
-    gain_in_ref,
     d_hid_ref,
     gains_ref,
     k_far,
     v_far,
-    w_qkv_far,
+    w_query_far,
+    w_key_far,
+    w_value_far,
     d_gate_ref,
     d_up_ref,
     d_down_ref,
@@ -709,8 +961,9 @@
     ups, downs = seq_orders(bits)
     links = Links(nseq, heads, send, recv)
     s, h = links.s, links.h
-    rows = d_proj_ref.shape[0]
-    width = gain_q_ref.shape[1]
+    rows, model = d_proj_ref.shape
+    width = k_lin_ref.shape[1]
+    gain_q, gain_k = flat(gain_q_ref), flat(gain_k_ref)
     groups, span = k_ref.shape[:2]
     loads = []
 
@@ -748,19 +1001,24 @@
     gate, up, first, second = ffn
     up.start()
     gate.start()
-    load_w = load(w_qkv_far, w_qkv_ref)
+    load_w = []
+    at = 0
+    for far in (w_query_far, w_key_far, w_value_far):
+        load_w.append(load(far, w_qkv_ref.at[:, pl.ds(at, far.shape[1])]))
+        at += far.shape[1]
 
     d_proj = d_proj_ref[...]
 
-    def out_block(j, carry):
+    out_rows = dw_out.shape[1] * dw_out.shape[2]
+    for j in range(nseq):
+        head, low = divmod(j * out_rows, width)
+        mixed_t = att_ref[low : low + out_rows, pl.ds(head * rows, rows)].astype(bf16)
         dw_out[j] = (
-            jnp.dot(mixed_t_ref[j], d_proj, preferred_element_type=f32)
+            jnp.dot(mixed_t, d_proj, preferred_element_type=f32)
             .astype(bf16)
             .reshape(dw_out.shape[1:])
         )
-        return carry
-
-    lax.fori_loop(0, nseq, out_block, 0)
+
     sum_out = Sum(links, lambda m: dw_out.at[related(s, m)], box_out, [0])
     sum_out.masks = lambda stage: held
     sum_out.start()
@@ -839,7 +1097,7 @@
         d_rot = dq_t[:, pl.ds(j * rows, rows)].T * scale
         d_lin, terms = back_norm(
             q_lin_ref[:, pl.ds(j * width, width)],
-            gain_q_ref[...],
+            gain_q,
             back_rotate(d_rot, cosines, sines),
         )
         d_qkv[:, pl.ds(j * width, width)] = d_lin.astype(bf16)
@@ -882,7 +1140,7 @@
 
     d_keys = whole(0, zbox_k)
     d_lin, d_gain_k = back_norm(
-        k_lin_ref[...], gain_k_ref[...], back_rotate(d_keys, cosines, sines)
+        k_lin_ref[...], gain_k, back_rotate(d_keys, cosines, sines)
     )
     qw = qcount * width
     d_qkv[:, pl.ds(qw, width)] = d_lin.astype(bf16)
@@ -910,10 +1168,11 @@
         total.start()
         qkv.append(total)
 
-    load_w.wait()
+    for copy in load_w:
+        copy.wait()
     d_attn_in = contract_last(d_qkv[...], w_qkv_ref[...])
     in_turn(*[total.steps(0) for total in qkv])
-    d_x, d_gain_in = back_norm(x_ref[...].astype(f32), gain_in_ref[...], d_attn_in)
+    d_x, d_gain_in = back_norm(x_ref[...].astype(f32), flat(gain_in_ref), d_attn_in)
     o_tokens[...] = (d_hid_ref[...] + d_x).astype(o_tokens.dtype)
 
     gsum[0] = gains_ref[...]
@@ -961,15 +1220,15 @@
 
 
 def tail(nseq, heads, qcount, scale, cid, *arrays):
-    (q, _, _, _, att, mixed_t, d_proj, w_out, q_lin, k_lin, _, _, gain_q, _) = arrays[:14]
-    (attn_t, x, gain_in, d_hid, gains, k, v, w_qkv, d_gate, _, _) = arrays[14:]
+    (q, _, _, _, att, d_proj, w_out, q_lin, k_lin, _, _, _, _, _) = arrays[:14]
+    (attn_t, x, d_hid, gains, k, v, w_query, w_key, w_value, d_gate, _, _) = arrays[14:]
     f32, bf16 = jnp.float32, jnp.bfloat16
     rows, model = d_proj.shape
-    width = gain_q.shape[1]
-    cols = w_qkv.shape[1]
+    width = k_lin.shape[1]
+    cols = w_query.shape[1] + w_key.shape[1] + w_value.shape[1]
     pieces = 4
     cut = cols // pieces
-    out_rows, qkv_rows = mixed_t.shape[1], attn_t.shape[1]
+    out_rows, qkv_rows = w_out.shape[0] // nseq, attn_t.shape[1]
     ffn_block = d_gate.shape[1:]
     some, all_but = nseq // 2, nseq - 1
     bits = nseq.bit_length() - 1
@@ -1005,12 +1264,12 @@
             jax.ShapeDtypeStruct(ffn_block, f32),
             jax.ShapeDtypeStruct(gains.shape, f32),
         ],
-        in_specs=[vm] * (len(arrays) - 6) + [anywhere] * 6,
+        in_specs=[vm] * (len(arrays) - 8) + [anywhere] * 8,
         out_specs=[vm] * 7,
         scratch_shapes=[
             VMEM(k.shape, bf16),
             VMEM(v.shape, bf16),
-            VMEM(w_qkv.shape, bf16),
+            VMEM((model, cols), bf16),
             VMEM((nseq, heads, rows, width), bf16),
             VMEM((nseq, heads, rows, width), bf16),
             VMEM((width, qcount * rows), f32),
@@ -1039,7 +1298,7 @@
             VMEM((heads - 1,) + gains.shape, f32),
             pltpu.SemaphoreType.DMA((copies,)),
             pltpu.SemaphoreType.DMA((copies,)),
-            pltpu.SemaphoreType.DMA((3 + 3 * some,)),
+            pltpu.SemaphoreType.DMA((5 + 3 * some,)),
         ],
         name="tail",
         compiler_params=pltpu.CompilerParams(
@@ -1152,9 +1411,9 @@
     greet([right, left] + [links.across(b) for b in range(bits)])
 
     proj = proj_ref[...]
-    hid = x_ref[...].astype(f32) + norm_rows(proj, gain_two_ref[...])
+    hid = x_ref[...].astype(f32) + norm_rows(proj, flat(gain_two_ref))
     hidden[...] = hid
-    u_local = norm_rows(hid, gain_three_ref[...]).astype(bf16)
+    u_local = norm_rows(hid, flat(gain_three_ref)).astype(bf16)
     for c in range(chunks):
         u_all[c, h] = u_local[c * rc : (c + 1) * rc]
     o_gains[...] = jnp.zeros_like(o_gains)
@@ -1294,10 +1553,10 @@
         here = pl.ds(c * rc, rc)
         ffn_out = summed(0, c)
         upstream = cot_ref[here, :].astype(f32)
-        o_out[here, :] = (hidden[here, :] + norm_rows(ffn_out, gain_four_ref[...])).astype(
+        o_out[here, :] = (hidden[here, :] + norm_rows(ffn_out, flat(gain_four_ref))).astype(
             o_out.dtype
         )
-        d_out, terms = back_norm(ffn_out, gain_four_ref[...], upstream)
+        d_out, terms = back_norm(ffn_out, flat(gain_four_ref), upstream)
         d_all[c, h] = d_out.astype(bf16)
         o_gains[3:4, :] += terms
 
@@ -1329,11 +1588,11 @@
 
     def finish_rows(c):
         here = pl.ds(c * rc, rc)
-        d_in, terms = back_norm(hidden[here, :], gain_three_ref[...], summed(1, c))
+        d_in, terms = back_norm(hidden[here, :], flat(gain_three_ref), summed(1, c))
         o_gains[2:3, :] += terms
         d_hid = cot_ref[here, :].astype(f32) + d_in
         o_hid[here, :] = d_hid
-        d_proj, terms = back_norm(proj_ref[here, :], gain_two_ref[...], d_hid)
+        d_proj, terms = back_norm(proj_ref[here, :], flat(gain_two_ref), d_hid)
         o_proj[here, :] = d_proj.astype(o_proj.dtype)
         o_gains[1:2, :] += terms
 
@@ -1434,7 +1693,8 @@
     links.finish()
 
 
-def feed_forward(nseq, heads, cid, proj, x, cot, gains, w_gate, w_up, w_down):
+def feed_forward(nseq, heads, cid, *arrays):
+    _, x, _, _, _, _, w_gate, w_up, w_down = arrays
     f32, bf16 = jnp.float32, jnp.bfloat16
     rows, model = x.shape
     units = w_gate.shape[0]
@@ -1494,7 +1754,52 @@
         compiler_params=pltpu.CompilerParams(
             collective_id=cid, has_side_effects=True, vmem_limit_bytes=62 * 2**20
         ),
-    )(proj, x, cot, *[g[None] for g in gains], w_gate, w_up, w_down)
+    )(*arrays)
+
+
+def finish_kernel(nseq, qw, width, each, few, *refs):
+    out, tokens, qkv, w_out, gate, up, down, gains = refs[:8]
+    o_out, o_tokens, o_query, o_key, o_value, o_w_out, o_gate, o_up, o_down = refs[8:17]
+    o_gains = refs[17:]
+    s, h = place()
+    which = s * lax.axis_size("head") + h
+    o_out[...] = out[...]
+    o_tokens[...] = tokens[...]
+    o_query[...] = qkv[:, :qw]
+    o_key[...] = qkv[:, qw : qw + width]
+    o_value[...] = qkv[:, qw + width :]
+    o_w_out[...] = w_out[...]
+    o_gate[...] = gate[...]
+    o_up[...] = up[...]
+    o_down[...] = down[...]
+    model = gains.shape[1]
+    wide = pltpu.roll(gains[...], lax.rem(model - which * each, model), 1)
+    narrow = pltpu.roll(gains[...], lax.rem(model - which * few, model), 1)
+    for i in range(4):
+        o_gains[i][...] = wide[i : i + 1, :each]
+    for i in range(4, 6):
+        o_gains[i][...] = narrow[i : i + 1, :few]
+
+
+def finish(nseq, qw, width, each, few, *arrays):
+    out, tokens, qkv, w_out, gate, up, down, gains = arrays
+    vm = pl.BlockSpec(memory_space=VMEM)
+    shape = lambda a: jax.ShapeDtypeStruct(a.shape, a.dtype)
+    f32 = jnp.float32
+    rows = qkv.shape[0]
+    wide, narrow = jax.ShapeDtypeStruct((1, each), f32), jax.ShapeDtypeStruct((1, few), f32)
+    return pl.pallas_call(
+        functools.partial(finish_kernel, nseq, qw, width, each, few),
+        out_shape=[shape(out), shape(tokens)]
+        + [jax.ShapeDtypeStruct((rows, n), f32) for n in (qw, width, width)]
+        + [shape(w_out), shape(gate), shape(up), shape(down)]
+        + [wide] * 4
+        + [narrow] * 2,
+        in_specs=[vm] * 8,
+        out_specs=[vm] * 15,
+        name="finish",
+        compiler_params=pltpu.CompilerParams(vmem_limit_bytes=LIMIT),
+    )(*arrays)
 
 
 def local(
@@ -1528,6 +1833,124 @@
     hidden_units = w_gate.shape[1]
     scale = 1.0 / math.sqrt(width)
     bf16 = jnp.bfloat16
+    if (nseq, heads) == (8, 4) and (model // nseq) % 16 == 0:
+        qw = qcount * width
+        each, few = model // (nseq * heads), width // (nseq * heads)
+        (
+            projected,
+            queries,
+            keys,
+            values,
+            starts,
+            index,
+            log_total,
+            attended_t,
+            q_linear,
+            k_linear,
+            cosines,
+            sines,
+            attn_t,
+        ) = front(
+            nseq,
+            heads,
+            qcount,
+            scale,
+            11,
+            tokens,
+            segment_ids,
+            w_key,
+            w_value,
+            gain_attn_in,
+            gain_query,
+            gain_key,
+            w_query,
+            w_out,
+        )
+        output, d_hidden, d_projected, gains, half_down, half_gate, all_up = feed_forward(
+            nseq,
+            heads,
+            10,
+            projected,
+            tokens,
+            cotangent,
+            gain_attn_out,
+            gain_ffn_in,
+            gain_ffn_out,
+            w_gate.T,
+            w_up.T,
+            w_down,
+        )
+        grad_tokens, sum_qkv, sum_out, sum_gate, sum_up, sum_down, sum_gains = tail(
+            nseq,
+            heads,
+            qcount,
+            scale,
+            9,
+            queries,
+            starts,
+            index,
+            log_total,
+            attended_t,
+            d_projected,
+            w_out,
+            q_linear,
+            k_linear,
+            cosines,
+            sines,
+            gain_query,
+            gain_key,
+            gain_attn_in,
+            attn_t,
+            tokens,
+            d_hidden,
+            gains,
+            keys.reshape(nseq, group, width),
+            values.reshape(nseq, group, width),
+            w_query,
+            w_key,
+            w_value,
+            half_gate,
+            all_up,
+            half_down,
+        )
+        (
+            output,
+            grad_tokens,
+            sum_query,
+            sum_key,
+            sum_value,
+            sum_out,
+            sum_gate,
+            sum_up,
+            sum_down,
+            *sum_gains,
+        ) = finish(
+            nseq,
+            qw,
+            width,
+            each,
+            few,
+            output,
+            grad_tokens,
+            sum_qkv,
+            sum_out,
+            sum_gate,
+            sum_up,
+            sum_down,
+            sum_gains,
+        )
+        return (
+            output,
+            grad_tokens,
+            sum_query,
+            sum_key,
+            sum_value,
+            sum_out,
+            sum_gate,
+            sum_up,
+            sum_down.T,
+            *[g[0] for g in sum_gains],
+        )
     first_row = (seq_index * heads + head_index) * local_rows
     my_index = first_row + jnp.arange(local_rows, dtype=jnp.int32)
     my_ids = lax.dynamic_slice_in_dim(segment_ids, first_row, local_rows)
@@ -1575,74 +1998,6 @@
     attended = attended_t.T
     mixed_local = unstacked(attended.astype(bf16))
     projected = jnp.dot(mixed_local, w_out, preferred_element_type=jnp.float32)
-    if (nseq, heads) == (8, 4) and (model // nseq) % 16 == 0:
-        qw = qcount * width
-        each, few = model // (nseq * heads), width // (nseq * heads)
-        output, d_hidden, d_projected, gains, half_down, half_gate, all_up = feed_forward(
-            nseq,
-            heads,
-            10,
-            projected,
-            tokens,
-            cotangent,
-            (gain_attn_out, gain_ffn_in, gain_ffn_out),
-            w_gate.T,
-            w_up.T,
-            w_down,
-        )
-        w_qkv = jnp.concatenate([w_query, w_key, w_value], axis=1)
-        grad_tokens, sum_qkv, sum_out, sum_gate, sum_up, sum_down, sum_gains = tail(
-            nseq,
-            heads,
-            qcount,
-            scale,
-            9,
-            queries,
-            starts,
-            index,
-            log_total,
-            attended_t,
-            mixed_local.T.reshape(nseq, -1, local_rows),
-            d_projected,
-            w_out,
-            q_linear,
-            k_linear,
-            cosines,
-            sines,
-            gain_query[None],
-            gain_key[None],
-            attn_in.T.reshape(nseq, -1, local_rows),
-            tokens,
-            gain_attn_in[None],
-            d_hidden,
-            gains,
-            keys,
-            values,
-            w_qkv,
-            half_gate,
-            all_up,
-            half_down,
-        )
-        which = seq_index * heads + head_index
-        wide = lax.dynamic_slice_in_dim(sum_gains[:4], which * each, each, 1)
-        narrow = lax.dynamic_slice_in_dim(sum_gains[4:6], which * few, few, 1)
-        return (
-            output,
-            grad_tokens,
-            sum_qkv[:, :qw],
-            sum_qkv[:, qw : qw + width],
-            sum_qkv[:, qw + width :],
-            sum_out,
-            sum_gate,
-            sum_up,
-            sum_down.T,
-            wide[0],
-            wide[1],
-            wide[2],
-            wide[3],
-            narrow[0],
-            narrow[1],
-        )
     hidden = inputs + norm_rows(projected, gain_attn_out)
     ffn_in = norm_rows(hidden, gain_ffn_in).astype(bf16)
     ffn_rows = line_gather(ffn_in, heads, 2).reshape(group, model)

time: 278 us -> 237 us (0.85)
  local copies, waits for them, and re-layouts: 18.6 us -> 0 us
  Pallas kernels: 245 us -> 236 us
  other arithmetic: 7.89 us -> 0 us
  matrix products: 5.07 us -> 0 us
    unnamed x50 -> x0, local copies, waits for them, and re-layouts: 7.07 us -> none
    pallas_call x2, Pallas kernels: 43.8 us -> 38.3 us  [the longest x1 34 us: front(): pl.pallas_call(kernel, out_shape=[shape((rows, model), f32), shape((stack...]
    dot_general x4 -> x0, matrix products: 5.07 us -> none  [the longest x1 2.4 us: local(): q_linear = jnp.dot(attn_in, w_query, preferred_element_type=jnp.float32)]
    slice x4 -> x0, local copies, waits for them, and re-layouts: 4.71 us -> none  [the longest x1 1.74 us: local(): sum_qkv[:, :qw]]
    concatenate x2 -> x0, other arithmetic: 3.89 us -> none  [the longest x1 3.25 us: local(): w_qkv = jnp.concatenate([w_query, w_key, w_value], axis=1)]
    pallas_call x1, Pallas kernels: 94.2 us -> 91.4 us  [feed_forward(): pl.pallas_call(functools.partial(ffn_kernel, nseq, heads, CHUNKS, SPANS),...]
where the time goes in v5:
time: 237 us
  Pallas kernels  236 us (100%)
    pallas_call x1, Pallas kernels, tail(): pl.pallas_call(kernel, out_shape=[jax.ShapeDtypeStruct((rows, model), bf1...  106 us
    pallas_call x1, Pallas kernels, feed_forward(): pl.pallas_call(functools.partial(ffn_kernel, nseq, heads, CHUNKS, SPANS),...  91.4 us
    pallas_call x1, Pallas kernels, front(): pl.pallas_call(kernel, out_shape=[shape((rows, model), f32), shape((stack...  34 us

profile of v5, /device:TPU:0, one launch (start us, length us, event | category | flops | bytes accessed | tf_op | source)
XLA Modules:
  0.0 236.9 jit_solution(739340836142788056)
XLA Ops:
  0.6 34.0 %front.1 = (f32[128,1152]{1,0:T(8,128)}, bf16[512,256]{1,0:T(8,128)(2,1)}, bf16[8,4,128,256]{3,2,1,0:T(8,128)(2,1)}, bf16[8,4,128,256]{3,2,1,0:T(8,128)(2,1)}, s...) custom-call(bf16[128,1152]{1,0:T(8,128)(2,1)} %refs_15_.1, ...), custom_call_target="tpu_custom_call" | custom-call | tf_op jit(solution)/shard_map/front/pallas_call | solution.py:733
  34.7 91.4 %feed_forward.1 = (bf16[128,1152]{1,0:T(8,128)(2,1)}, f32[128,1152]{1,0:T(8,128)}, bf16[128,1152]{1,0:T(8,128)(2,1)}, f32[8,1152]{1,0:T(8,128)}, bf16[4,144,1728...) custom-call(f32[128,1152]{1,0:T(8,128)} %get-tuple-element.57.proj_ref, ...), custom_call_target="tpu_custom_call" | custom-call | tf_op jit(solution)/shard_map/feed_forward/pallas_call | solution.py:1711
  126.1 106.4 %tail.1 = (bf16[128,1152]{1,0:T(8,128)(2,1)}, f32[36,1536]{1,0:T(8,128)}, f32[32,1152]{1,0:T(8,128)}, f32[144,1728]{1,0:T(8,128)}, f32[144,1728]{1,0:T(8,128)}, /*index=5*/f32[144,1728]{1,0:T(8,128)}, f32[8,1152]{1,0:T(8,128)}) custom-call(bf16[512,256]{1,0:T(8,128)(2,1)} %get-tuple-element.59.refs_0_, s32[1,512]{1,0:T(1,128)} %get-tuple-element.60.refs_1_, ...), custom_call_target="tpu_custom_call" | custom-call | tf_op jit(solution)/shard_map/tail/pallas_call | solution.py:1256
  232.5 4.2 %finish.1 = (bf16[128,1152]{1,0:T(8,128)(2,1)}, bf16[128,1152]{1,0:T(8,128)(2,1)}, f32[36,1024]{1,0:T(8,128)}, f32[36,256]{1,0:T(8,128)}, f32[36,256]{1,0:T(8,12...) custom-call(bf16[128,1152]{1,0:T(8,128)(2,1)} %get-tuple-element.58., ...), custom_call_target="tpu_custom_call" | custom-call | tf_op jit(solution)/shard_map/finish/pallas_call | solution.py:1791

commit v6 on v5

--- a/solution.py
+++ b/solution.py
@@ -833,6 +833,10 @@
                 step()
 
 
+def split_rows(rows):
+    return (rows // 2 + 15) // 16 * 16
+
+
 class Links:
     def __init__(self, nseq, heads, send, recv):
         self.s, self.h = place()
@@ -842,9 +846,10 @@
         self.started = []
         self.others = [lax.rem(self.h + d, heads) for d in range(1, heads)]
 
-    def greet(self):
+    def greet(self, more=()):
         bits = self.nseq.bit_length() - 1
-        greet([self.across(b) for b in range(bits)] + [(self.s, o) for o in self.others])
+        near = [self.across(b) for b in range(bits)]
+        greet(near + [(self.s, o) for o in self.others] + list(more))
 
     def across(self, bit):
         return (related(self.s, 1 << bit), self.h)
@@ -911,7 +916,8 @@
     w_value_far,
     d_gate_ref,
     d_up_ref,
-    d_down_ref,
+    d_down_first,
+    d_down_second,
     o_tokens,
     o_qkv,
     o_out,
@@ -941,14 +947,18 @@
     zsrc_qkv,
     zbox_qkv,
     d_qkv,
-    keep_gate,
-    keep_up,
-    keep_first,
-    keep_second,
-    box_gate,
-    box_up,
-    box_first,
-    box_second,
+    keep_gate_first,
+    keep_gate_second,
+    keep_up_first,
+    keep_up_second,
+    keep_down_first,
+    keep_down_second,
+    box_gate_first,
+    box_gate_second,
+    box_up_first,
+    box_up_second,
+    box_down_first,
+    box_down_second,
     gsum,
     gbox,
     gzbox,
@@ -975,32 +985,52 @@
 
     load_k = load(k_far, k_ref)
     load_v = load(v_far, v_ref)
-    links.greet()
+    plane = subsets(ups)[1:]
+    links.greet([(related(s, m), links.h) for m in plane if m & (m - 1)])
 
     held = subsets(ups)
     ffn = []
-    split = keep_first.shape[1]
-    for src, keep, box, order, low in (
-        (d_gate_ref, keep_gate, box_gate, ups, 0),
-        (d_up_ref, keep_up, box_up, [0] + downs, 0),
-        (d_down_ref, keep_first, box_first, ups, 0),
-        (d_down_ref, keep_second, box_second, downs, split),
+    split = keep_gate_first.shape[1]
+    for src, keep, box, order, low, past in (
+        (d_gate_ref, keep_gate_first, box_gate_first, ups, 0, 1),
+        (d_gate_ref, keep_gate_second, box_gate_second, downs, split, 1),
+        (d_up_ref, keep_up_first, box_up_first, [0] + ups, 0, 0),
+        (d_up_ref, keep_up_second, box_up_second, [0] + downs, split, 0),
+        (d_down_first, keep_down_first, box_down_first, ups[1:], 0, 2),
+        (d_down_second, keep_down_second, box_down_second, downs[1:], 0, 2),
     ):
         here = pl.ds(low, keep.shape[1])
 
-        def part(m, src=src, here=here):
-            if src is d_up_ref:
-                return src.at[related(s, m)]
-            return src.at[held.index(m), here]
+        def part(m, src=src, here=here, past=past, order=order):
+            if past == 0:
+                return src.at[related(s, m), here]
+            if past == 1:
+                return src.at[held.index(m), here]
+            return src.at[0 if m else 1, here]
 
         total = Sum(links, part, box, order)
         kept = subsets(order[1:])
         total.loads = [load(part(m), keep.at[i]) for i, m in enumerate(kept)]
         total.kept = lambda m, keep=keep, kept=kept: keep.at[kept.index(m)]
         ffn.append(total)
-    gate, up, first, second = ffn
-    up.start()
-    gate.start()
+    gate, up, down = ffn[0:2], ffn[2:4], ffn[4:6]
+    for total in up + gate + down:
+        total.start()
+
+    def settle(pair, stage, first=False):
+        if first:
+            for total in pair:
+                for copy in total.loads:
+                    copy.wait()
+        in_turn(*[total.steps(stage, total.kept if first else None) for total in pair])
+
+    def put(pair, out, first=False):
+        at = 0
+        for total in pair:
+            value = total.last(total.kept if first else None)
+            out[pl.ds(at, value.shape[0]), :] = value
+            at += value.shape[0]
+
     load_w = []
     at = 0
     for far in (w_query_far, w_key_far, w_value_far):
@@ -1027,9 +1057,10 @@
         part = w_out_ref[pl.ds(j * width, width), :]
         grads[pl.ds(j * rows, rows), :] = contract_last(d_proj, part).astype(bf16)
         grads_t[:, pl.ds(j * rows, rows)] = contract_last(part, d_proj).astype(bf16)
-    for copy in up.loads:
-        copy.wait()
-    in_turn(up.steps(0, up.kept))
+    in_turn(sum_out.steps(0))
+    z_out = [
+        links.go(box_out.at[:, o], zbox_out.at[d], (s, o)) for d, o in enumerate(links.others)
+    ]
     dots = jnp.sum(grads_t[...].astype(f32) * att_ref[...], axis=0, keepdims=True)
     start = start_ref[...]
     index = index_ref[...]
@@ -1084,11 +1115,6 @@
         for total in kv:
             total.send(0, total.masks(0)[mask_index])
 
-    for m in sum_out.steps(0):
-        m()
-    z_out = [
-        links.go(box_out.at[:, o], zbox_out.at[d], (s, o)) for d, o in enumerate(links.others)
-    ]
     in_turn(*[total.steps(0) for total in kv])
 
     cosines, sines = cos_ref[...], sin_ref[...]
@@ -1105,12 +1131,7 @@
 
     for stage in range(1, bits - 1):
         in_turn(*[total.steps(stage) for total in kv])
-    for total in (gate, first, second):
-        for copy in total.loads:
-            copy.wait()
-    in_turn(gate.steps(0, gate.kept), up.steps(1))
-    first.start()
-    second.start()
+    settle(gate, 0, True)
 
     arriving = {}
     for i, total in enumerate(kv):
@@ -1131,6 +1152,9 @@
     sum_end = Sum(links, lambda m: mid_out.at[held.index(m)], end_out, downs)
     sum_end.start()
 
+
+    settle(up, 0, True)
+
     def whole(i, zbox):
         total = kv[len(kv) - 2 + i].current(0)[...].astype(f32)
         for j in range(1, heads):
@@ -1182,30 +1206,38 @@
     gain_copy = links.go(gsum.at[0], gbox.at[0], links.across(0))
     for stage in range(1, bits - 1):
         in_turn(*[total.steps(stage) for total in qkv])
-    for bit in range(bits):
-        gain_copy.wait_recv()
-        gsum[bit + 1] = gsum[bit] + gbox[bit]
-        if bit + 1 < bits:
-            gain_copy = links.go(gsum.at[bit + 1], gbox.at[bit + 1], links.across(bit + 1))
-    gain_z = [
-        links.go(gsum.at[bits], gzbox.at[d], (s, o)) for d, o in enumerate(links.others)
-    ]
-    in_turn(sum_end.steps(0))
-    in_turn(first.steps(0, first.kept), second.steps(0, second.kept))
-
+    settle(up, 1)
     each = block_rows // heads
     z_qkv = []
+
+    gain_copy.wait_recv()
+    gsum[1] = gsum[0] + gbox[0]
+    gain_plane = [
+        links.go(gsum.at[1], gbox.at[1 + i], (related(s, m), h)) for i, m in enumerate(plane)
+    ]
     for j, total in enumerate(qkv):
+        if j == 2:
+            total_gains = gsum[1]
+            for i, copy in enumerate(gain_plane):
+                copy.wait_recv()
+                total_gains = total_gains + gbox[1 + i]
+            gsum[2] = total_gains
+            gain_z = [
+                links.go(gsum.at[2], gzbox.at[d], (s, o)) for d, o in enumerate(links.others)
+            ]
         value = total.last()
         for p in range(heads):
             zsrc_qkv[j, p] = value[p * each : (p + 1) * each].astype(bf16)
         z_qkv.append(links.over_heads(zsrc_qkv.at[j], zbox_qkv.at[j]))
-    o_gate[...] = gate.last()
-    o_up[...] = up.last()
-    o_down[pl.ds(0, split), :] = first.last()
-    o_down[pl.ds(split, o_down.shape[0] - split), :] = second.last()
+    for total in down:
+        for copy in total.loads:
+            copy.wait()
+    put(down, o_down, True)
+    put(gate, o_gate)
+    put(up, o_up)
+    in_turn(sum_end.steps(0))
     o_out[...] = sum_end.last()
-    total = gsum[bits]
+    total = gsum[2]
     for d, copy in enumerate(gain_z):
         copy.wait_recv()
         total = total + gzbox[d]
@@ -1221,7 +1253,7 @@
 
 def tail(nseq, heads, qcount, scale, cid, *arrays):
     (q, _, _, _, att, d_proj, w_out, q_lin, k_lin, _, _, _, _, _) = arrays[:14]
-    (attn_t, x, d_hid, gains, k, v, w_query, w_key, w_value, d_gate, _, _) = arrays[14:]
+    (attn_t, x, d_hid, gains, k, v, w_query, w_key, w_value, d_gate, _, _, _) = arrays[14:]
     f32, bf16 = jnp.float32, jnp.bfloat16
     rows, model = d_proj.shape
     width = k_lin.shape[1]
@@ -1231,20 +1263,19 @@
     out_rows, qkv_rows = w_out.shape[0] // nseq, attn_t.shape[1]
     ffn_block = d_gate.shape[1:]
     some, all_but = nseq // 2, nseq - 1
-    bits = nseq.bit_length() - 1
     out_block = (heads, out_rows // heads, model)
-    split = (ffn_block[0] // 2 + 15) // 16 * 16
-    parts = [ffn_block, ffn_block, (split, ffn_block[1]), (ffn_block[0] - split, ffn_block[1])]
+    split = split_rows(ffn_block[0])
+    low, high = (split, ffn_block[1]), (ffn_block[0] - split, ffn_block[1])
+    parts = [(part, *n) for n in ((2, 3), (4, 7), (1, 1)) for part in (low, high)]
     copies = (
-        3 * (some - 1)
-        + all_but
+        sum(n for _, _, n in parts)
         + some
         + (heads - 1)
         + (some - 1)
         + 2 * heads * all_but
         + 2 * (heads - 1)
         + pieces * (all_but + heads - 1)
-        + bits
+        + some
         + (heads - 1)
     )
     vm = pl.BlockSpec(memory_space=VMEM)
@@ -1264,7 +1295,7 @@
             jax.ShapeDtypeStruct(ffn_block, f32),
             jax.ShapeDtypeStruct(gains.shape, f32),
         ],
-        in_specs=[vm] * (len(arrays) - 8) + [anywhere] * 8,
+        in_specs=[vm] * (len(arrays) - 9) + [anywhere] * 9,
         out_specs=[vm] * 7,
         scratch_shapes=[
             VMEM(k.shape, bf16),
@@ -1290,15 +1321,15 @@
             VMEM((pieces, heads - 1, qkv_rows // heads, cut), bf16),
             VMEM((rows, cols), bf16),
         ]
-        + [VMEM((some if i == 1 else some // 2,) + part, bf16) for i, part in enumerate(parts)]
-        + [VMEM((all_but if i == 1 else some - 1,) + part, bf16) for i, part in enumerate(parts)]
+        + [VMEM((n,) + part, bf16) for part, n, _ in parts]
+        + [VMEM((n,) + part, bf16) for part, _, n in parts]
         + [
-            VMEM((bits + 1,) + gains.shape, f32),
-            VMEM((bits,) + gains.shape, f32),
+            VMEM((3,) + gains.shape, f32),
+            VMEM((some,) + gains.shape, f32),
             VMEM((heads - 1,) + gains.shape, f32),
             pltpu.SemaphoreType.DMA((copies,)),
             pltpu.SemaphoreType.DMA((copies,)),
-            pltpu.SemaphoreType.DMA((5 + 3 * some,)),
+            pltpu.SemaphoreType.DMA((5 + sum(n for _, n, _ in parts),)),
         ],
         name="tail",
         compiler_params=pltpu.CompilerParams(
@@ -1309,30 +1340,30 @@
 
 CHUNKS, SPANS = 4, 2
 ORDER = (
-    ("ags", 0, 0, 0), ("ags", 0, 1, 0), ("agw", 0, 0, 0), ("ags", 0, 0, 1), ("agw", 0, 1, 0),
-    ("ags", 0, 1, 1), ("ags", 0, 2, 0), ("agw", 0, 0, 1), ("ags", 0, 0, 2), ("agw", 0, 1, 1),
-    ("ags", 0, 1, 2), ("ags", 0, 3, 0), ("agw", 0, 0, 2), ("agw", 0, 1, 2), ("fa", 0), ("fb", 0),
-    ("agw", 0, 3, 0), ("agw", 0, 2, 0), ("ags", 0, 3, 1), ("ags", 0, 2, 1), ("fc", 0),
-    ("agw", 0, 3, 1), ("rss", 0, 0, 0), ("ags", 0, 3, 2), ("agw", 0, 3, 2), ("agw", 0, 2, 1),
-    ("rss", 0, 1, 0), ("ags", 0, 2, 2), ("rsw", 0, 0, 0), ("rss", 0, 0, 1), ("rsw", 0, 1, 0),
-    ("rss", 0, 1, 1), ("agw", 0, 2, 2), ("fa", 1), ("rsw", 0, 0, 1), ("fb", 1), ("rss", 0, 0, 2),
-    ("fc", 1), ("rss", 0, 2, 0), ("rsw", 0, 1, 1), ("rss", 0, 3, 0), ("rss", 0, 1, 2),
-    ("rsw", 0, 2, 0), ("rss", 0, 2, 1), ("rsw", 0, 0, 2), ("rsw", 0, 3, 0), ("n", 0),
-    ("ags", 1, 0, 0), ("rsw", 0, 1, 2), ("rss", 0, 3, 1), ("rsw", 0, 2, 1), ("rss", 0, 2, 2),
-    ("n", 1), ("agw", 1, 0, 0), ("ags", 1, 1, 0), ("ags", 1, 0, 1), ("rsw", 0, 3, 1),
-    ("rss", 0, 3, 2), ("agw", 1, 1, 0), ("ags", 1, 1, 1), ("rsw", 0, 2, 2), ("n", 2),
-    ("agw", 1, 0, 1), ("ags", 1, 0, 2), ("ags", 1, 2, 0), ("rsw", 0, 3, 2), ("n", 3),
-    ("agw", 1, 1, 1), ("ags", 1, 1, 2), ("ags", 1, 3, 0), ("agw", 1, 0, 2), ("agw", 1, 2, 0),
-    ("agw", 1, 1, 2), ("ga", 0), ("ags", 1, 2, 1), ("gb", 0), ("agw", 1, 3, 0), ("ags", 1, 3, 1),
-    ("gc", 0), ("agw", 1, 2, 1), ("ags", 1, 2, 2), ("rss", 1, 1, 0), ("rss", 1, 0, 0),
-    ("agw", 1, 3, 1), ("ags", 1, 3, 2), ("rsw", 1, 1, 0), ("rss", 1, 1, 1), ("agw", 1, 2, 2),
-    ("agw", 1, 3, 2), ("ga", 1), ("rsw", 1, 0, 0), ("gb", 1), ("rss", 1, 0, 1), ("gc", 1),
-    ("rss", 1, 3, 0), ("wd", 0), ("rsw", 1, 1, 1), ("rss", 1, 2, 0), ("wd", 1), ("rss", 1, 1, 2),
-    ("dd", 0), ("rsw", 1, 3, 0), ("rss", 1, 3, 1), ("wg", 0), ("rsw", 1, 2, 0), ("rsw", 1, 0, 1),
-    ("rss", 1, 2, 1), ("wg", 1), ("dg", 0), ("rss", 1, 0, 2), ("rsw", 1, 1, 2), ("wu", 0),
-    ("rsw", 1, 3, 1), ("e", 1), ("rss", 1, 3, 2), ("rsw", 1, 2, 1), ("rss", 1, 2, 2), ("wu", 1),
-    ("rsw", 1, 0, 2), ("Dd", 0), ("Dg", 0), ("e", 0), ("rsw", 1, 3, 2), ("e", 3), ("rsw", 1, 2, 2),
-    ("e", 2),
+    ("ags", 0, 0, 0), ("ags", 0, 1, 0), ("ags", 0, 3, 0), ("agw", 0, 0, 0), ("ags", 0, 0, 1),
+    ("agw", 0, 1, 0), ("ags", 0, 1, 1), ("agw", 0, 0, 1), ("ags", 0, 0, 2), ("agw", 0, 3, 0),
+    ("agw", 0, 1, 1), ("ags", 0, 1, 2), ("ags", 0, 2, 0), ("agw", 0, 0, 2), ("agw", 0, 1, 2),
+    ("fa", 0), ("fb", 0), ("ags", 0, 3, 1), ("agw", 0, 2, 0), ("ags", 0, 2, 1), ("fc", 0),
+    ("rss", 0, 0, 0), ("agw", 0, 3, 1), ("ags", 0, 3, 2), ("agw", 0, 2, 1), ("rss", 0, 1, 0),
+    ("ags", 0, 2, 2), ("rsw", 0, 0, 0), ("rss", 0, 0, 1), ("agw", 0, 2, 2), ("agw", 0, 3, 2),
+    ("rsw", 0, 1, 0), ("rss", 0, 1, 1), ("fa", 1), ("rsw", 0, 0, 1), ("rss", 0, 0, 2), ("fb", 1),
+    ("rsw", 0, 1, 1), ("rss", 0, 1, 2), ("fc", 1), ("rss", 0, 3, 0), ("rsw", 0, 0, 2),
+    ("rss", 0, 2, 0), ("n", 0), ("ags", 1, 0, 0), ("rsw", 0, 3, 0), ("rss", 0, 3, 1),
+    ("rsw", 0, 2, 0), ("rss", 0, 2, 1), ("rsw", 0, 1, 2), ("n", 1), ("ags", 1, 1, 0),
+    ("agw", 1, 0, 0), ("ags", 1, 0, 1), ("rsw", 0, 3, 1), ("rss", 0, 3, 2), ("rsw", 0, 2, 1),
+    ("rss", 0, 2, 2), ("agw", 1, 1, 0), ("ags", 1, 1, 1), ("agw", 1, 0, 1), ("ags", 1, 0, 2),
+    ("rsw", 0, 3, 2), ("rsw", 0, 2, 2), ("n", 2), ("ags", 1, 2, 0), ("agw", 1, 1, 1), ("n", 3),
+    ("ags", 1, 1, 2), ("ags", 1, 3, 0), ("agw", 1, 0, 2), ("agw", 1, 1, 2), ("ga", 0),
+    ("agw", 1, 2, 0), ("ags", 1, 2, 1), ("gb", 0), ("agw", 1, 3, 0), ("ags", 1, 3, 1), ("gc", 0),
+    ("agw", 1, 2, 1), ("rss", 1, 0, 0), ("ags", 1, 2, 2), ("agw", 1, 2, 2), ("agw", 1, 3, 1),
+    ("rss", 1, 1, 0), ("ags", 1, 3, 2), ("rsw", 1, 0, 0), ("rss", 1, 0, 1), ("agw", 1, 3, 2),
+    ("wd", 0), ("wd", 1), ("dd", 0), ("rsw", 1, 1, 0), ("ga", 1), ("gb", 1), ("rss", 1, 1, 1),
+    ("gc", 1), ("rss", 1, 2, 0), ("Dd", 0), ("rsw", 1, 0, 1), ("rsw", 1, 1, 1), ("rss", 1, 3, 0),
+    ("rss", 1, 1, 2), ("wg", 0), ("rsw", 1, 2, 0), ("rss", 1, 2, 1), ("wg", 1), ("rsw", 1, 3, 0),
+    ("rss", 1, 3, 1), ("wu", 0), ("rss", 1, 0, 2), ("dg", 0), ("wu", 1), ("rsw", 1, 2, 1),
+    ("rss", 1, 2, 2), ("rsw", 1, 3, 1), ("rsw", 1, 1, 2), ("rss", 1, 3, 2), ("Dg", 0),
+    ("rsw", 1, 0, 2), ("rsw", 1, 2, 2), ("e", 0), ("e", 2), ("e", 1), ("rsw", 1, 3, 2), ("e", 3),
+    ("D2", 0),
 )
 
 
@@ -1354,7 +1385,8 @@
     o_hid,
     o_proj,
     o_gains,
-    o_down,
+    o_first,
+    o_second,
     o_gate,
     o_up,
     hidden,
@@ -1377,6 +1409,8 @@
     dw_down,
     box_gate,
     box_down,
+    box_first,
+    box_second,
     sum_send,
     sum_recv,
     ag_send,
@@ -1615,12 +1649,18 @@
     sum_down = Sum(links, lambda m: dw_down.at[related(s, m)], box_down, [0])
     for total in (sum_gate, sum_down):
         total.masks = lambda stage: held
-    def keep(total, out, n):
-        for i, step in enumerate(total.steps(0)):
-            step()
-            copy = pltpu.make_async_copy(total.boxes.at[i], out.at[i], local_sem.at[n + i])
-            copy.start()
-            stores.append(copy)
+    def store(src, dst):
+        copy = pltpu.make_async_copy(src, dst, local_sem.at[3 + len(stores)])
+        copy.start()
+        stores.append(copy)
+
+    split = box_first.shape[1]
+    pieces = []
+    for box, order, low in ((box_first, ups, 0), (box_second, downs, split)):
+        here = pl.ds(low, box.shape[1])
+        pieces.append(
+            Sum(links, lambda m, here=here: box_down.at[held.index(m), here], box, order)
+        )
 
     for event in ORDER:
         kind, args = event[0], event[1:]
@@ -1659,17 +1699,26 @@
         elif kind == "wu":
             weight_grad(d_up, dw_up, args[0])
             if args[0] == 1:
-                copy = pltpu.make_async_copy(dw_up, o_up, local_sem.at[3 + 2 * len(held)])
-                copy.start()
-                stores.append(copy)
+                store(dw_up, o_up)
         elif kind == "dd":
             sum_down.start()
         elif kind == "dg":
             sum_gate.start()
+        elif kind == "Dg":
+            in_turn(sum_gate.steps(0))
+            store(box_gate, o_gate)
         elif kind == "Dd":
-            keep(sum_down, o_down, 3)
+            in_turn(sum_down.steps(0))
+            for total in pieces:
+                for m in total.masks(0):
+                    total.send(0, m)
         else:
-            keep(sum_gate, o_gate, 3 + len(held))
+            for total, out in zip(pieces, (o_first, o_second)):
+                for m in total.masks(0):
+                    copy, where = total.waiting.pop((0, m))
+                    copy.wait_recv()
+                    total.boxes[where] = total.boxes[where] + total.current(m)[...]
+                store(total.boxes, out)
 
     for event in ORDER:
         if event[0] == "ags":
@@ -1706,7 +1755,9 @@
     block = (model // nseq, units)
     some = nseq // 2
     half = jax.ShapeDtypeStruct((some,) + block, bf16)
-    messages = 2 * some
+    split = split_rows(block[0])
+    parts = [(split, units), (block[0] - split, units)]
+    messages = 3 * some
     hops = (2, chunks, 2, heads - 1)
     return pl.pallas_call(
         functools.partial(ffn_kernel, nseq, heads, CHUNKS, SPANS),
@@ -1715,12 +1766,12 @@
             jax.ShapeDtypeStruct((rows, model), f32),
             jax.ShapeDtypeStruct((rows, model), bf16),
             jax.ShapeDtypeStruct((8, model), f32),
-            half,
+            *[jax.ShapeDtypeStruct((some // 2,) + part, bf16) for part in parts],
             half,
             jax.ShapeDtypeStruct((nseq,) + block, bf16),
         ],
         in_specs=[vm] * 6 + [anywhere] * 3,
-        out_specs=[vm] * 4 + [anywhere] * 3,
+        out_specs=[vm] * 4 + [anywhere] * 4,
         scratch_shapes=[
             VMEM((rows, model), f32),
             VMEM(w_gate.shape, bf16),
@@ -1742,13 +1793,14 @@
             VMEM((nseq,) + block, bf16),
             VMEM((some,) + block, bf16),
             VMEM((some,) + block, bf16),
+            *[VMEM((some // 2,) + part, bf16) for part in parts],
             pltpu.SemaphoreType.DMA((messages,)),
             pltpu.SemaphoreType.DMA((messages,)),
             pltpu.SemaphoreType.DMA(hops),
             pltpu.SemaphoreType.DMA(hops),
             pltpu.SemaphoreType.DMA(hops),
             pltpu.SemaphoreType.DMA(hops),
-            pltpu.SemaphoreType.DMA((4 + 2 * some,)),
+            pltpu.SemaphoreType.DMA((7,)),
         ],
         name="feed_forward",
         compiler_params=pltpu.CompilerParams(
@@ -1866,7 +1918,7 @@
             w_query,
             w_out,
         )
-        output, d_hidden, d_projected, gains, half_down, half_gate, all_up = feed_forward(
+        output, d_hidden, d_projected, gains, down_first, down_second, half_gate, all_up = feed_forward(
             nseq,
             heads,
             10,
@@ -1911,7 +1963,8 @@
             w_value,
             half_gate,
             all_up,
-            half_down,
+            down_first,
+            down_second,
         )
         (
             output,

time: 237 us -> 223 us (0.941)
  Pallas kernels: 236 us -> 222 us
    pallas_call x1, Pallas kernels: 106 us -> 91.8 us  [tail(): pl.pallas_call(kernel, out_shape=[jax.ShapeDtypeStruct((rows, model), bf1...]
where the time goes in v6:
time: 223 us
  Pallas kernels  222 us (100%)
    pallas_call x1, Pallas kernels, feed_forward(): pl.pallas_call(functools.partial(ffn_kernel, nseq, heads, CHUNKS, SPANS),...  92.3 us
    pallas_call x1, Pallas kernels, tail(): pl.pallas_call(kernel, out_shape=[jax.ShapeDtypeStruct((rows, model), bf1...  91.8 us
    pallas_call x1, Pallas kernels, front(): pl.pallas_call(kernel, out_shape=[shape((rows, model), f32), shape((stack...  34 us

profile of v6, /device:TPU:0, one launch (start us, length us, event | category | flops | bytes accessed | tf_op | source)
XLA Modules:
  0.0 223.2 jit_solution(5799156694292931324)
XLA Ops:
  0.6 34.0 %front.1 = (f32[128,1152]{1,0:T(8,128)}, bf16[512,256]{1,0:T(8,128)(2,1)}, bf16[8,4,128,256]{3,2,1,0:T(8,128)(2,1)}, bf16[8,4,128,256]{3,2,1,0:T(8,128)(2,1)}, s...) custom-call(bf16[128,1152]{1,0:T(8,128)(2,1)} %refs_15_.1, ...), custom_call_target="tpu_custom_call" | custom-call | tf_op jit(solution)/shard_map/front/pallas_call | solution.py:733
  34.7 92.3 %feed_forward.1 = (bf16[128,1152]{1,0:T(8,128)(2,1)}, f32[128,1152]{1,0:T(8,128)}, bf16[128,1152]{1,0:T(8,128)(2,1)}, f32[8,1152]{1,0:T(8,128)}, bf16[2,80,1728]...) custom-call(f32[128,1152]{1,0:T(8,128)} %get-tuple-element.58.proj_r, ...), custom_call_target="tpu_custom_call" | custom-call | tf_op jit(solution)/shard_map/feed_forward/pallas_call | solution.py:1762
  127.0 91.8 %tail.1 = (bf16[128,1152]{1,0:T(8,128)(2,1)}, f32[36,1536]{1,0:T(8,128)}, f32[32,1152]{1,0:T(8,128)}, f32[144,1728]{1,0:T(8,128)}, f32[144,1728]{1,0:T(8,128)}, /*index=5*/f32[144,1728]{1,0:T(8,128)}, f32[8,1152]{1,0:T(8,128)}) custom-call(bf16[512,256]{1,0:T(8,128)(2,1)} %get-tuple-element.60.refs_0_, s32[1,512]{1,0:T(1,128)} %get-tuple-element.61.refs_1_, ...), custom_call_target="tpu_custom_call" | custom-call | tf_op jit(solution)/shard_map/tail/pallas_call | solution.py:1287
  218.8 4.2 %finish.1 = (bf16[128,1152]{1,0:T(8,128)(2,1)}, bf16[128,1152]{1,0:T(8,128)(2,1)}, f32[36,1024]{1,0:T(8,128)}, f32[36,256]{1,0:T(8,128)}, f32[36,256]{1,0:T(8,12...) custom-call(bf16[128,1152]{1,0:T(8,128)(2,1)} %get-tuple-element.59., ...), custom_call_target="tpu_custom_call" | custom-call | tf_op jit(solution)/shard_map/finish/pallas_call | solution.py:1843
